TPU v7x, 32 devices: a whole 2x2x4 slice. The times are simulated.
32 devices in a mesh: dp: 8 (over y, x, core), grp: 4 (over z).
Axes of the slice: x: 2, y: 2, z: 4, core: 2. Of those that a mesh axis runs over, the one named last changes fastest.
Arguments:
- tokens: bfloat16 [8, 12544, 384], P('dp', 'grp'), may hold values from -6 to 6
- cotangent: bfloat16 [8, 12544, 384], P('dp', 'grp'), may hold values from -6 to 6
- attn_master: float32 [598272], P(('dp', 'grp')), as said below
- attn_first: float32 [598272], P(('dp', 'grp')), as said below
- attn_second: float32 [598272], P(('dp', 'grp')), as said below
- mlp_master: float32 [1182464], P(('dp', 'grp')), as said below
- mlp_first: float32 [1182464], P(('dp', 'grp')), as said below
- mlp_second: float32 [1182464], P(('dp', 'grp')), as said below
Outputs:
- output: bfloat16 [8, 12544, 384], P('dp', 'grp')
- input_grad: float32 [8, 12544, 384], P('dp', 'grp')
- attn_first_new: float32 [598272], P(('dp', 'grp'))
- attn_second_new: float32 [598272], P(('dp', 'grp'))
- attn_master_new: float32 [598272], P(('dp', 'grp'))
- mlp_first_new: float32 [1182464], P(('dp', 'grp'))
- mlp_second_new: float32 [1182464], P(('dp', 'grp'))
- mlp_master_new: float32 [1182464], P(('dp', 'grp'))
Inputs may be any that keep to these rules, and one draw needn't show every extreme that they name: `attn_master`: entries past the parameters of the layout are zero. `attn_first`: entries past the parameters of the layout are zero. `attn_second`: positive on the parameters of the layout, zero past them. `mlp_master`: entries past the parameters of the layout are zero. `mlp_first`: entries past the parameters of the layout are zero. `mlp_second`: positive on the parameters of the layout, zero past them.
All inputs are finite; a program needn't handle non-finite values.
Results may differ from a plain program's by a relative error of at most 0.012.
Values may be sent and summed in bfloat16 or wider, within the bound.
A program may use at most 320 MiB of HBM per device.

v0:
```python
import jax
import jax.numpy as jnp
import numpy as np
from jax import lax
from jax.sharding import PartitionSpec as P

D = 384
HEADS = 12
HDIM = 32
FF = 1536
WIN = 7
STEP = 10


beta_one = 0.9
beta_two = 0.999
learn_rate = 0.04
decay_rate = 0.05
adam_eps = 1e-08
norm_eps = 1e-05
masked_score = -1e30
highest = lax.Precision.HIGHEST


def swapped(value, axis, stride):
    mask = 2**stride
    pairs = [(source, source ^ mask) for source in range(lax.axis_size(axis))]
    return lax.ppermute(value, axis, pairs)


def attn_layout():
    return [
        ("w_qkv", (D, 3 * D)),
        ("w_proj", (D, D)),
        ("table_fine", (HEADS, (3 * WIN - 2) ** 2)),
        ("table_coarse", (HEADS, (2 * WIN - 1) ** 2)),
        ("ln1_gain", (D,)),
        ("ln1_shift", (D,)),
        ("q_bias", (D,)),
        ("v_bias", (D,)),
        ("proj_bias", (D,)),
    ]


def mlp_layout():
    return [
        ("w_fc1", (D, FF)),
        ("w_fc2", (FF, D)),
        ("fc1_bias", (FF,)),
        ("ln2_gain", (D,)),
        ("ln2_shift", (D,)),
        ("fc2_bias", (D,)),
    ]


def unpack(flat, layout):
    pieces = {}
    offset = 0
    for seg_name, seg_shape in layout:
        length = int(np.prod(seg_shape))
        pieces[seg_name] = flat[offset : offset + length].reshape(seg_shape)
        offset += length
    return pieces


def pack(pieces, layout, total_len):
    flat_parts = [pieces[seg_name].reshape(-1) for seg_name, seg_shape in layout]
    joined = jnp.concatenate(flat_parts)
    return jnp.pad(joined, (0, total_len - joined.shape[0]))


def layer_norm(values, gain_vec, bias_vec):
    centered = values - jnp.mean(values, axis=-1, keepdims=True)
    variance = jnp.mean(centered * centered, axis=-1, keepdims=True)
    return centered * lax.rsqrt(variance + norm_eps) * gain_vec + bias_vec


def gelu_tanh(values):
    return jax.nn.gelu(values, approximate=True)


def adamw(master, first, second, grads):
    first_new = beta_one * first + (1.0 - beta_one) * grads
    second_new = beta_two * second + (1.0 - beta_two) * grads * grads
    first_hat = first_new / (1.0 - beta_one**STEP)
    second_hat = second_new / (1.0 - beta_two**STEP)
    master_new = master - learn_rate * (
        first_hat / (jnp.sqrt(second_hat) + adam_eps) + decay_rate * master
    )
    return (first_new, second_new, master_new)


def contract_rows(left, right):
    return lax.dot_general(
        left, right, (((0,), (0,)), ((), ())), preferred_element_type=jnp.float32
    )


def times_transposed(left, right):
    return lax.dot_general(
        left, right, (((1,), (1,)), ((), ())), preferred_element_type=jnp.float32
    )


def offset_hot(query_pos, key_pos, base_off, table_len):
    shifted = key_pos[None, :] - query_pos[:, None] + base_off
    return (shifted[:, :, None] == jnp.arange(table_len, dtype=jnp.int32)[None, None, :]).astype(
        jnp.float32
    )


def table_bias(table_vals, row_hot, col_hot):
    grid_data = table_vals.reshape(HEADS, row_hot.shape[2], col_hot.shape[2])
    half_done = jnp.einsum("hab,xia->hxib", grid_data, row_hot, precision=highest)
    full_bias = jnp.einsum("hxib,yjb->hxyij", half_done, col_hot, precision=highest)
    return full_bias.reshape(
        HEADS, row_hot.shape[0] * col_hot.shape[0], row_hot.shape[1] * col_hot.shape[1]
    )


def table_grad(d_bias, row_hot, col_hot):
    grid_data = d_bias.reshape(
        HEADS, row_hot.shape[0], col_hot.shape[0], row_hot.shape[1], col_hot.shape[1]
    )
    half_done = jnp.einsum("hxyij,yjb->hxib", grid_data, col_hot, precision=highest)
    return jnp.einsum("hxib,xia->hab", half_done, row_hot, precision=highest).reshape(HEADS, -1)


def grow_edge(grid_data, which_bit, own_flag, cat_dim):
    halo_width = WIN // 2
    first_cell = (WIN - halo_width) * (1 - own_flag)
    edge_strip = lax.dynamic_slice_in_dim(grid_data, first_cell, halo_width, cat_dim)
    arrived = swapped(edge_strip, "dp", which_bit)
    empty_side = jnp.zeros_like(arrived)
    before = jnp.where(own_flag == 1, arrived, empty_side)
    behind = jnp.where(own_flag == 0, arrived, empty_side)
    return jnp.concatenate([before, grid_data, behind], axis=cat_dim)


def shrink_edge(grid_data, which_bit, own_flag, cat_dim):
    halo_width = WIN // 2
    send_at = (WIN + halo_width) * (1 - own_flag)
    edge_strip = lax.dynamic_slice_in_dim(grid_data, send_at, halo_width, cat_dim)
    arrived = swapped(edge_strip.astype(jnp.bfloat16), "dp", which_bit).astype(edge_strip.dtype)
    middle = lax.slice_in_dim(grid_data, halo_width, halo_width + WIN, axis=cat_dim)
    place_at = (WIN - halo_width) * (1 - own_flag)
    current = lax.dynamic_slice_in_dim(middle, place_at, halo_width, cat_dim)
    return lax.dynamic_update_slice_in_dim(middle, current + arrived, place_at, cat_dim)


def gather_pooled(pooled, row_bit, col_bit):
    combined = pooled
    for which_bit, own_flag, cat_dim in ((0, col_bit, 2), (1, row_bit, 1)):
        other_part = swapped(combined, "dp", which_bit)
        first_part = jnp.where(own_flag == 0, combined, other_part)
        second_part = jnp.where(own_flag == 0, other_part, combined)
        combined = jnp.concatenate([first_part, second_part], axis=cat_dim)
    return combined


def reduce_pooled(grad_grid, row_bit, col_bit):
    current = grad_grid
    for which_bit, own_flag, cat_dim in ((1, row_bit, 1), (0, col_bit, 2)):
        half_len = current.shape[cat_dim] // 2
        first_half = lax.slice_in_dim(current, 0, half_len, axis=cat_dim)
        second_half = lax.slice_in_dim(current, half_len, 2 * half_len, axis=cat_dim)
        kept_half = jnp.where(own_flag == 0, first_half, second_half)
        sent_half = jnp.where(own_flag == 0, second_half, first_half)
        current = kept_half + swapped(sent_half.astype(jnp.bfloat16), "dp", which_bit).astype(
            sent_half.dtype
        )
    return current


def fetch_params(master):
    return lax.all_gather(master.astype(jnp.bfloat16), ("dp", "grp"), axis=0, tiled=True)


def sum_to_owner(flat):
    cube = flat.reshape(lax.axis_size("dp"), lax.axis_size("grp"), -1)
    partly = lax.psum_scatter(
        cube.astype(jnp.bfloat16), "grp", scatter_dimension=1, tiled=True
    ).astype(jnp.float32)
    return lax.psum_scatter(partly, "dp", scatter_dimension=0, tiled=True).reshape(-1)


def score_block(query_blk, kv_blk, bias_all, key_mask):
    window_count = query_blk.shape[0]
    query_heads = query_blk.reshape(window_count, -1, HEADS, HDIM)
    key_heads = kv_blk[..., :D].reshape(window_count, -1, HEADS, HDIM)
    value_heads = kv_blk[..., D:].reshape(window_count, -1, HEADS, HDIM)
    scores = (
        jnp.einsum("wqhe,wkhe->whqk", query_heads, key_heads, preferred_element_type=jnp.float32)
        + bias_all
    )
    return (jnp.where(key_mask, scores, masked_score), query_heads, key_heads, value_heads)


def body(
    tokens, cotangent, attn_master, attn_first, attn_second, mlp_master, mlp_first, mlp_second
):
    window_slot = lax.axis_index("dp") % 4
    row_bit = window_slot // 2
    col_bit = window_slot % 2
    device_count = lax.axis_size("dp") * lax.axis_size("grp")
    halo_width = WIN // 2
    region = WIN + 2 * halo_width
    cell_count = (WIN + 1) // 2
    query_scale = HDIM ** (-0.5)
    image_count = tokens.shape[1] // (WIN * WIN)
    block_size = min(image_count, 16)
    block_count = image_count // block_size
    key_count = region * region + 4 * cell_count * cell_count
    attn_params = unpack(fetch_params(attn_master), attn_layout())
    mlp_params = unpack(fetch_params(mlp_master), mlp_layout())
    inputs = tokens[0].astype(jnp.float32)
    grad_out = cotangent[0]
    gain_one = attn_params["ln1_gain"].astype(jnp.float32)
    shift_one = attn_params["ln1_shift"].astype(jnp.float32)
    normed_one = layer_norm(inputs, gain_one, shift_one).astype(jnp.bfloat16)
    projected = jnp.dot(normed_one, attn_params["w_qkv"], preferred_element_type=jnp.float32)
    queries = ((projected[:, :D] + attn_params["q_bias"].astype(jnp.float32)) * query_scale).astype(
        jnp.bfloat16
    )
    key_vals = jnp.concatenate(
        [
            projected[:, D : 2 * D],
            projected[:, 2 * D :] + attn_params["v_bias"].astype(jnp.float32),
        ],
        axis=1,
    ).astype(jnp.bfloat16)
    key_grid = key_vals.reshape(image_count, WIN, WIN, 2 * D)
    extended = grow_edge(grow_edge(key_grid, 0, col_bit, 2), 1, row_bit, 1)
    pool_rows = lax.dynamic_slice_in_dim(extended, halo_width - row_bit, 2 * cell_count, 1)
    pool_source = lax.dynamic_slice_in_dim(pool_rows, halo_width - col_bit, 2 * cell_count, 2)
    pooled = jnp.mean(
        pool_source.astype(jnp.float32).reshape(image_count, cell_count, 2, cell_count, 2, 2 * D),
        axis=(2, 4),
    ).astype(jnp.bfloat16)
    pooled_grid = gather_pooled(pooled, row_bit, col_bit)
    keys_all = jnp.concatenate(
        [
            extended.reshape(image_count, region * region, 2 * D),
            pooled_grid.reshape(image_count, 4 * cell_count * cell_count, 2 * D),
        ],
        axis=1,
    )
    query_pos = jnp.arange(WIN, dtype=jnp.int32)
    fine_keys = jnp.arange(region, dtype=jnp.int32) - halo_width
    fine_hot = offset_hot(query_pos, fine_keys, WIN - 1 + halo_width, 3 * WIN - 2)
    grid_pos = jnp.arange(2 * cell_count, dtype=jnp.int32)
    coarse_keys = grid_pos - (grid_pos >= cell_count).astype(jnp.int32)
    row_hot = offset_hot((WIN * row_bit + query_pos) // 2, coarse_keys, WIN - 1, 2 * WIN - 1)
    col_hot = offset_hot((WIN * col_bit + query_pos) // 2, coarse_keys, WIN - 1, 2 * WIN - 1)
    table_fine = attn_params["table_fine"].astype(jnp.float32)
    table_coarse = attn_params["table_coarse"].astype(jnp.float32)
    bias_all = jnp.concatenate(
        [table_bias(table_fine, fine_hot, fine_hot), table_bias(table_coarse, row_hot, col_hot)],
        axis=2,
    )
    fine_pos = jnp.arange(region, dtype=jnp.int32)
    row_fine = (fine_pos >= halo_width * (1 - row_bit)) & (fine_pos < region - halo_width * row_bit)
    col_fine = (fine_pos >= halo_width * (1 - col_bit)) & (fine_pos < region - halo_width * col_bit)
    coarse_ok = grid_pos != cell_count
    key_mask = jnp.concatenate(
        [
            (row_fine[:, None] & col_fine[None, :]).reshape(-1),
            (coarse_ok[:, None] & coarse_ok[None, :]).reshape(-1),
        ]
    )
    query_blocks = queries.reshape(block_count, block_size, WIN * WIN, D)
    kv_blocks = keys_all.reshape(block_count, block_size, key_count, 2 * D)

    def forward_block(pair_in):
        query_blk, kv_blk = pair_in
        scores, query_heads, key_heads, value_heads = score_block(
            query_blk, kv_blk, bias_all, key_mask
        )
        row_peak = jnp.max(scores, axis=-1, keepdims=True)
        log_total = row_peak + jnp.log(jnp.sum(jnp.exp(scores - row_peak), axis=-1, keepdims=True))
        attn_probs = jnp.exp(scores - log_total).astype(jnp.bfloat16)
        mixed_blk = jnp.einsum(
            "whqk,wkhe->wqhe", attn_probs, value_heads, preferred_element_type=jnp.float32
        )
        return (mixed_blk.reshape(block_size, WIN * WIN, D).astype(jnp.bfloat16), log_total)

    mixed_blocks, log_totals = lax.map(forward_block, (query_blocks, kv_blocks))
    mixed_rows = mixed_blocks.reshape(-1, D)
    attn_out = jnp.dot(
        mixed_rows, attn_params["w_proj"], preferred_element_type=jnp.float32
    ) + attn_params["proj_bias"].astype(jnp.float32)
    residual = inputs + attn_out
    gain_two = mlp_params["ln2_gain"].astype(jnp.float32)
    shift_two = mlp_params["ln2_shift"].astype(jnp.float32)
    normed_two = layer_norm(residual, gain_two, shift_two).astype(jnp.bfloat16)
    hidden = jnp.dot(
        normed_two, mlp_params["w_fc1"], preferred_element_type=jnp.float32
    ) + mlp_params["fc1_bias"].astype(jnp.float32)
    activated = gelu_tanh(hidden).astype(jnp.bfloat16)
    output = (
        residual
        + jnp.dot(activated, mlp_params["w_fc2"], preferred_element_type=jnp.float32)
        + mlp_params["fc2_bias"].astype(jnp.float32)
    ).astype(jnp.bfloat16)
    grad_float = grad_out.astype(jnp.float32)
    d_activated = times_transposed(grad_out, mlp_params["w_fc2"])
    unused_gelu, gelu_pull = jax.vjp(gelu_tanh, hidden)
    d_hidden = gelu_pull(d_activated)[0].astype(jnp.bfloat16)
    d_normed_two = times_transposed(d_hidden, mlp_params["w_fc1"])
    unused_norm, norm_pull = jax.vjp(layer_norm, residual, gain_two, shift_two)
    d_resid_norm, d_gain_two, d_shift_two = norm_pull(d_normed_two)
    mlp_grads = {
        "w_fc1": contract_rows(normed_two, d_hidden),
        "w_fc2": contract_rows(activated, grad_out),
        "fc1_bias": jnp.sum(d_hidden.astype(jnp.float32), axis=0),
        "ln2_gain": d_gain_two,
        "ln2_shift": d_shift_two,
        "fc2_bias": jnp.sum(grad_float, axis=0),
    }
    mlp_shard = sum_to_owner(pack(mlp_grads, mlp_layout(), mlp_master.shape[0] * device_count))
    d_residual = grad_float + d_resid_norm
    d_attn = d_residual.astype(jnp.bfloat16)
    grad_w_proj = contract_rows(mixed_rows, d_attn)
    grad_proj_bias = jnp.sum(d_attn.astype(jnp.float32), axis=0)
    d_mixed = times_transposed(d_attn, attn_params["w_proj"]).astype(jnp.bfloat16)
    dmix_blocks = d_mixed.reshape(block_count, block_size, WIN * WIN, D)

    def backward_block(table_sum, quad_in):
        query_blk, kv_blk, log_blk, dmix_blk = quad_in
        scores, query_heads, key_heads, value_heads = score_block(
            query_blk, kv_blk, bias_all, key_mask
        )
        exact_probs = jnp.exp(scores - log_blk)
        dmix_heads = dmix_blk.reshape(block_size, WIN * WIN, HEADS, HDIM)
        d_values = jnp.einsum(
            "whqk,wqhe->wkhe",
            exact_probs.astype(jnp.bfloat16),
            dmix_heads,
            preferred_element_type=jnp.float32,
        )
        d_probs = jnp.einsum(
            "wqhe,wkhe->whqk", dmix_heads, value_heads, preferred_element_type=jnp.float32
        )
        d_scores = (
            exact_probs * (d_probs - jnp.sum(d_probs * exact_probs, axis=-1, keepdims=True))
        ).astype(jnp.bfloat16)
        d_query = jnp.einsum(
            "whqk,wkhe->wqhe", d_scores, key_heads, preferred_element_type=jnp.float32
        )
        d_keys = jnp.einsum(
            "whqk,wqhe->wkhe", d_scores, query_heads, preferred_element_type=jnp.float32
        )
        d_kv = jnp.concatenate(
            [d_keys.reshape(block_size, key_count, D), d_values.reshape(block_size, key_count, D)],
            axis=2,
        )
        return (
            table_sum + jnp.sum(d_scores.astype(jnp.float32), axis=0),
            (d_query.reshape(block_size, WIN * WIN, D), d_kv),
        )

    table_start = jnp.zeros((HEADS, WIN * WIN, key_count), jnp.float32)
    table_sum, block_grads = lax.scan(
        backward_block, table_start, (query_blocks, kv_blocks, log_totals, dmix_blocks)
    )
    d_query_blocks, d_kv_blocks = block_grads
    d_kv_all = d_kv_blocks.reshape(image_count, key_count, 2 * D)
    d_fine = d_kv_all[:, : region * region].reshape(image_count, region, region, 2 * D)
    d_pool = d_kv_all[:, region * region :].reshape(
        image_count, 2 * cell_count, 2 * cell_count, 2 * D
    )
    d_cells = reduce_pooled(d_pool, row_bit, col_bit)
    spread_cells = jnp.broadcast_to(
        0.25 * d_cells[:, :, None, :, None, :], (image_count, cell_count, 2, cell_count, 2, 2 * D)
    ).reshape(image_count, 2 * cell_count, 2 * cell_count, 2 * D)
    zero_index = jnp.zeros((), jnp.int32)
    placed = lax.dynamic_update_slice(
        jnp.zeros_like(d_fine),
        spread_cells,
        (zero_index, halo_width - row_bit, halo_width - col_bit, zero_index),
    )
    d_own = shrink_edge(shrink_edge(d_fine + placed, 1, row_bit, 1), 0, col_bit, 2)
    d_query_rows = d_query_blocks.reshape(-1, D)
    d_qkv = jnp.concatenate(
        [
            (d_query_rows * query_scale).astype(jnp.bfloat16),
            d_own.reshape(-1, 2 * D).astype(jnp.bfloat16),
        ],
        axis=1,
    )
    d_normed_one = times_transposed(d_qkv, attn_params["w_qkv"])
    unused_first, first_pull = jax.vjp(layer_norm, inputs, gain_one, shift_one)
    d_input_norm, d_gain_one, d_shift_one = first_pull(d_normed_one)
    input_grad = d_residual + d_input_norm
    attn_grads = {
        "w_qkv": contract_rows(normed_one, d_qkv),
        "w_proj": grad_w_proj,
        "table_fine": table_grad(table_sum[:, :, : region * region], fine_hot, fine_hot),
        "table_coarse": table_grad(table_sum[:, :, region * region :], row_hot, col_hot),
        "ln1_gain": d_gain_one,
        "ln1_shift": d_shift_one,
        "q_bias": jnp.sum(d_qkv[:, :D].astype(jnp.float32), axis=0),
        "v_bias": jnp.sum(d_qkv[:, 2 * D :].astype(jnp.float32), axis=0),
        "proj_bias": grad_proj_bias,
    }
    attn_shard = sum_to_owner(pack(attn_grads, attn_layout(), attn_master.shape[0] * device_count))
    attn_new = adamw(attn_master, attn_first, attn_second, attn_shard)
    mlp_new = adamw(mlp_master, mlp_first, mlp_second, mlp_shard)
    return (
        output[None],
        input_grad[None],
        attn_new[0],
        attn_new[1],
        attn_new[2],
        mlp_new[0],
        mlp_new[1],
        mlp_new[2],
    )


def solution(mesh):
    placed = (
        P("dp", "grp", None),
        P("dp", "grp", None),
        P(("dp", "grp")),
        P(("dp", "grp")),
        P(("dp", "grp")),
        P(("dp", "grp")),
        P(("dp", "grp")),
        P(("dp", "grp")),
    )
    return jax.shard_map(
        body,
        mesh=mesh,
        in_specs=placed,
        out_specs=(
            P("dp", "grp", None),
            P("dp", "grp", None),
            P(("dp", "grp")),
            P(("dp", "grp")),
            P(("dp", "grp")),
            P(("dp", "grp")),
            P(("dp", "grp")),
            P(("dp", "grp")),
        ),
        check_vma=False,
    )
```

profile of v0, /device:TPU:0, one launch (start us, length us, event | category | flops | bytes accessed | tf_op | source)
XLA Modules:
  0.0 1457.9 jit_solution(8216672630588152380)
XLA Ops:
  17.5 140.4 %all-reduce.15.cloned.1.call-done = (bf16[598272]{0:T(1024)(128)(2,1)}, bf16[1182464]{0:T(1024)(128)(2,1)}) async-done(((bf16[598272]{0:T(1024)(128)(2,1)}, bf16[1182464]{0:T(1024)(128)(2,1)}), (bf16[598272]{0:T(1024)(128)(2,1)}, bf16[1182464]{0:T(1024)(128)(2,1)})) %all-reduce.15.cloned.1.call-update) | async-done | bytes 3561488
  180.9 6.9 fusion.47
  215.2 83.7 %collective-permute-done.1 = bf16[64,3,13,768]{3,0,2,1:T(8,128)(2,1)} collective-permute-done((bf16[64,3,13,768]{3,0,2,1:T(8,128)(2,1)}, bf16[64,3,13,768]{3,0,2,1:T(8,128)(2,1)}, u32[]{:S(2)}, u32[]{:S(2)}) %collective-permute-start.1) | collective-permute-done | bytes 3833888 | tf_op jit(solution)/shard_map/ppermute | solution.py:28
  298.9 8.8 broadcast_select_fusion.1
  307.8 14.7 %pad_maximum_fusion.1 = bf16[64,13,13,768]{3,2,1,0:T(8,128)(2,1)} fusion(bf16[64,3,13,768]{3,2,1,0:T(8,128)(2,1)} %get-tuple-element.280, bf16[64,7,3,768]{3,2,1,0:T(4,128)(2,1)S(1)} %copy-done.16, bf16[64,7,7,768]{3,2,1,0:T(8,128)(2,1)S(1)} %bitcast.291, bf16[64,7,3,768]{3,2,1,0:T(4,128)(2,1)S(1)} %copy-done.18, ...), kind=kLoop, calls=%fused_computation.38 | loop fusion | flops 83066880 | bytes 33226752 | tf_op jit(solution)/shard_map/concatenate | solution.py:137
  322.5 11.5 dynamic-slice_convert_fusion.1
  334.0 15.2 %reshape.482 = f32[64,4,2,4,2,768]{5,4,3,2,1,0:T(2,128)} reshape(f32[64,8,8,768]{3,2,1,0:T(8,128)} %dynamic-slice_convert_fusion.1) | data formatting | bytes 25165824 | tf_op jit(solution)/shard_map/reshape | solution.py:237
  349.2 14.5 reduce_sum.191
  399.9 7.5 copy.67
  421.6 18.4 %copy.65 = bf16[64,13,13,768]{3,0,2,1:T(8,128)(2,1)} copy(bf16[64,13,13,768]{3,2,1,0:T(8,128)(2,1)} %pad_maximum_fusion.1) | data formatting | bytes 33226752 | tf_op jit(solution)/shard_map/concatenate | solution.py:137
  439.9 6.0 collective-permute-done.3
  456.8 17.3 %pad_maximum_fusion = bf16[4,16,233,768]{3,1,0,2:T(8,128)(2,1)} fusion(bf16[4,16,64,768]{3,1,0,2:T(8,128)(2,1)S(1)} %copy.66, bf16[4,16,169,768]{3,1,0,2:T(8,128)(2,1)} %bitcast.286), kind=kLoop, calls=%fused_computation.37 | loop fusion | flops 11452416 | bytes 45809664 | tf_op jit(solution)/shard_map/concatenate | solution.py:241
  474.2 34.0 %copy.70 = bf16[4,16,233,768]{2,3,1,0:T(8,128)(2,1)} copy(bf16[4,16,233,768]{3,1,0,2:T(8,128)(2,1)} %pad_maximum_fusion) | data formatting | bytes 45809664 | tf_op jit(solution)/shard_map/while | solution.py:287
  508.1 74.4 %while.27 = (s32[]{:T(128)}, bf16[4,16,49,384]{3,2,1,0:T(8,128)(2,1)}, f32[4,16,12,49,1]{3,2,1,4,0:T(8,128)}, bf16[4,16,233,768]{2,3,1,0:T(8,128)(2,1)}, pred[23...) while((s32[]{:T(128)}, ...), condition=%wide.region_6.7_spmd, body=%wide.region_3.6_spmd.sunk | while | flops 304988544 | bytes 61878068 | solution.py:287
  593.0 13.4 multiply_convert_fusion.1
  606.4 21.0 %fusion.114 = (bf16[1536]{0:T(1024)(128)(2,1)}, bf16[3136,1536]{1,0:T(8,128)(2,1)}) fusion(f32[3136,1536]{1,0:T(8,128)} %get-tuple-element.300, f32[1536]{0:T(1024)S(1)} %copy-done.60, bf16[1536,384]{1,0:T(8,128)(2,1)S(1)} %copy-done.31, bf16[1,3136,384]{2,1,0:T(8,128)(2,1)S(1)} %copy-done.19), kind=kOutput, calls=%fused_computation.238 | convolution fusion | flops 3805346304 | bytes 32498688 | tf_op jit(solution)/shard_map/dot_general | solution.py:100
  627.4 11.2 multiply_reduce_fusion.1
  652.4 314.8 %while.28 = (s32[]{:T(128)}, f32[12,49,233]{2,1,0:T(8,128)S(1)}, f32[4,16,49,384]{2,3,1,0:T(8,128)}, f32[4,16,233,768]{3,1,0,2:T(8,128)}, pred[233]{0:T(512)(128...) while((s32[]{:T(128)}, f32[12,49,233]{2,1,0:T(8,128)S(1)}, ...), condition=%wide.region_14.15_spmd.clone, body=%wide.region_11.14_spmd.clone.sunk | while | flops 741716288 | bytes 213909424 | solution.py:363
  665.8 6.1 fusion.194
  671.9 9.1 multiply_reduce_fusion.5
  680.9 8.3 convert_reduce_fusion.3
  696.6 10.3 maximum_bitcast_fusion.2
  706.9 12.8 copy.135
  721.7 9.8 constant_dynamic-update-slice_fusion.14
  744.4 6.1 fusion.194
  750.6 9.1 multiply_reduce_fusion.5
  759.6 8.3 convert_reduce_fusion.3
  775.3 10.3 maximum_bitcast_fusion.2
  785.6 12.8 copy.135
  800.3 9.7 constant_dynamic-update-slice_fusion.14
  823.0 6.1 fusion.194
  829.1 9.1 multiply_reduce_fusion.5
  838.1 8.3 convert_reduce_fusion.3
  853.8 10.3 maximum_bitcast_fusion.2
  864.1 12.8 copy.135
  878.8 9.7 constant_dynamic-update-slice_fusion.14
  901.5 6.1 fusion.194
  907.6 9.1 multiply_reduce_fusion.5
  916.7 8.3 convert_reduce_fusion.3
  932.3 10.3 maximum_bitcast_fusion.2
  942.6 12.8 copy.135
  957.3 9.7 constant_dynamic-update-slice_fusion.14
  967.2 10.6 slice.165
  977.8 16.4 %copy.129 = f32[64,64,768]{2,1,0:T(8,128)} copy(f32[64,64,768]{2,0,1:T(8,128)} %slice.165) | data formatting | bytes 25165824 | tf_op jit(solution)/shard_map/slice | solution.py:369
  994.1 6.9 select_convert_fusion
  1004.7 10.8 convolution_convert_fusion.3
  1018.2 52.4 %collective-permute-done.4 = bf16[64,4,8,768]{3,2,1,0:T(8,128)(2,1)} collective-permute-done((bf16[64,4,8,768]{3,2,1,0:T(8,128)(2,1)}, bf16[64,4,8,768]{3,2,1,0:T(8,128)(2,1)}, u32[]{:S(2)}, u32[]{:S(2)}) %collective-permute-start.4) | collective-permute-done | bytes 3145760 | tf_op jit(solution)/shard_map/ppermute | solution.py:28
  1070.6 7.8 convert_add_fusion
  1082.3 25.0 %slice.164 = f32[64,169,768]{2,0,1:T(8,128)} slice(f32[64,233,768]{2,0,1:T(8,128)} %bitcast.293), slice={[0:64], [0:169], [0:768]} | slice | bytes 66453504 | tf_op jit(solution)/shard_map/slice | solution.py:368
  1107.4 6.5 convolution_convert_fusion.2
  1116.5 7.1 add_multiply_fusion
  1127.1 11.1 add_dynamic-update-slice_fusion
  1170.5 12.2 slice.170
  1182.8 46.6 %collective-permute-done.6 = bf16[64,3,13,768]{3,0,2,1:T(8,128)(2,1)} collective-permute-done((bf16[64,3,13,768]{3,0,2,1:T(8,128)(2,1)}, bf16[64,3,13,768]{3,0,2,1:T(8,128)(2,1)}, u32[]{:S(2)}, u32[]{:S(2)}) %collective-permute-start.6) | collective-permute-done | bytes 3833888 | tf_op jit(solution)/shard_map/ppermute | solution.py:28
  1229.4 8.9 add_dynamic-update-slice_fusion.1
  1252.7 10.5 fusion.108
  1288.0 8.4 convert_element_type.224
  1301.5 7.8 convolution_convert_fusion.1
  1311.3 8.7 fusion.103
  1327.0 18.5 %concatenate.62 = bf16[598104]{0:T(1024)(128)(2,1)} concatenate(bf16[442368]{0:T(1024)(128)(2,1)S(1)} %reshape.473, bf16[147456]{0:T(1024)(128)(2,1)} %reshape.474, bf16[4332]{0:T(1024)(128)(2,1)S(1)} %reshape_reshape.8, bf16[2028]{0:T(1024)(128)(2,1)S(1)} %reshape_reshape.9, bf16[384]{0:T(512)(128)(2,1)S(1)} %get-tuple-element.208, bf16[384]{0:T(512)(128)(2,1)S(1)} %get-tuple-element.211, ...), dimensions={0} | concatenate | bytes 2392416 | tf_op jit(solution)/shard_map/concatenate | solution.py:68
  1354.7 9.9 fusion.36
  1367.7 15.6 %reduce-scatter.7.cloned.1.call-done = bf16[8,1,18696]{2,0,1:T(8,128)(2,1)} async-done(((bf16[8,4,18696]{2,0,1:T(8,128)(2,1)}), bf16[8,1,18696]{2,0,1:T(8,128)(2,1)}) %reduce-scatter.7.cloned.1.call-update) | async-done | bytes 299152
  1385.6 9.2 add_bitcast_fusion
  1394.8 50.8 %all-reduce.13.cloned.1.call-done = (f32[8,1,18696]{2,1,0:T(1,128)}, f32[8,1,36952]{2,1,0:T(1,128)}) async-done(((f32[8,1,18696]{2,1,0:T(1,128)}, f32[8,1,36952]{2,1,0:T(1,128)}), (f32[8,1,18696]{2,1,0:T(1,128)}, f32[8,1,36952]{2,1,0:T(1,128)})) %all-reduce.13.cloned.1.call-update) | async-done | bytes 1780752
  (441 shorter events, 430.2 us)
Async XLA Ops:
  7.2 150.7 %all-reduce.15.cloned.1.call-start = ((), (), s32[]{:S(2)}) async-start(), calls=%async_computation.5 | async-start | bytes 7127040
  15.7 1349.0 %reduce-scatter.9.cloned.1.call-start = ((), (), s32[]{:S(2)}) async-start(), calls=%async_computation.3 | async-start | bytes 2959360
  16.3 151.8 %copy-start.35 = (f32[3136]{0:T(1024)}, f32[3136]{0:T(1024)S(1)}, u32[]{:S(2)}) copy-start(f32[3136]{0:T(1024)S(1)} %broadcast_multiply_fusion.1) | copy-start | bytes 37636
  17.4 140.4 %copy-start.39 = (f32[3136]{0:T(1024)}, f32[3136]{0:T(1024)S(1)}, u32[]{:S(2)}) copy-start(f32[3136]{0:T(1024)S(1)} %fusion.40) | copy-start | bytes 37636
  17.5 150.7 %copy-start.41 = (f32[3136]{0:T(1024)}, f32[3136]{0:T(1024)S(1)}, u32[]{:S(2)}) copy-start(f32[3136]{0:T(1024)S(1)} %fusion.94) | copy-start | bytes 37636
  197.3 9.8 slice-start
  197.7 4.3 collective-permute-start
  197.8 9.4 slice-start.1
  213.7 85.2 %collective-permute-start.1 = (bf16[64,3,13,768]{3,0,2,1:T(8,128)(2,1)}, bf16[64,3,13,768]{3,0,2,1:T(8,128)(2,1)}, u32[]{:S(2)}, u32[]{:S(2)}) collective-permute-start(bf16[64,3,13,768]{3,0,2,1:T(8,128)(2,1)} %copy.62), channel_id=1, source_target_pairs={{0,8},{4,12},{8,0},{12,4},{16,24},{20,28},{24,16},{28,20},{1,9},{5... | collective-permute-start | bytes 11501576 | tf_op jit(solution)/shard_map/ppermute | solution.py:28
  215.2 92.5 %slice-start.2 = ((s8[5505024]{0:T(1024)(128)(4,1)}), s8[1310720]{0:T(1024)(128)(4,1)S(1)}, s32[]{:S(2)}) async-start(s8[5505024]{0:T(1024)(128)(4,1)} %bitcast.290), calls=%async_computation.8 | async-start | bytes 2621440
  215.2 92.5 %slice-start.3 = ((s8[5505024]{0:T(1024)(128)(4,1)}), s8[4194304]{0:T(1024)(128)(4,1)S(1)}, s32[]{:S(2)}) async-start(s8[5505024]{0:T(1024)(128)(4,1)} %bitcast.290), calls=%async_computation.9 | async-start | bytes 8388608
  215.2 92.5 %copy-start.16 = (bf16[64,7,3,768]{3,2,1,0:T(4,128)(2,1)S(1)}, bf16[64,7,3,768]{3,2,1,0:T(4,128)(2,1)}, u32[]{:S(2)}) copy-start(bf16[64,7,3,768]{3,2,1,0:T(4,128)(2,1)} %copy-done.15) | copy-start | bytes 6193156
  215.2 92.5 %copy-start.18 = (bf16[64,7,3,768]{3,2,1,0:T(4,128)(2,1)S(1)}, bf16[64,7,3,768]{3,2,1,0:T(4,128)(2,1)}, u32[]{:S(2)}) copy-start(bf16[64,7,3,768]{3,2,1,0:T(4,128)(2,1)} %copy-done.17) | copy-start | bytes 6193156
  365.7 3.8 collective-permute-start.2
  366.2 28.4 %copy-start.47 = (s32[7,13]{1,0:T(8,128)}, s32[7,13]{1,0:T(8,128)S(1)}, u32[]{:S(2)}) copy-start(s32[7,13]{1,0:T(8,128)S(1)} %subtract_add_fusion.2) | copy-start | bytes 1096
  366.3 18.2 %copy-start.53 = (s32[7,8]{1,0:T(8,128)}, s32[7,8]{1,0:T(8,128)S(1)}, u32[]{:S(2)}) copy-start(s32[7,8]{1,0:T(8,128)S(1)} %get-tuple-element.296) | copy-start | bytes 676
  366.3 18.5 %copy-start.55 = (s32[7,8]{1,0:T(8,128)}, s32[7,8]{1,0:T(8,128)S(1)}, u32[]{:S(2)}) copy-start(s32[7,8]{1,0:T(8,128)S(1)} %get-tuple-element.295) | copy-start | bytes 676
  375.5 70.5 %collective-permute-start.3 = (bf16[64,4,8,768]{3,2,1,0:T(8,128)(2,1)}, bf16[64,4,8,768]{3,2,1,0:T(8,128)(2,1)}, u32[]{:S(2)}, u32[]{:S(2)}) collective-permute-start(bf16[64,4,8,768]{3,2,1,0:T(8,128)(2,1)} %pad_maximum_fusion.3), channel_id=1, source_target_pairs={{0,8},{4,12},{8,0},{12,4},{16,24},{20,28},{24,16},{28,20},{1,9},{5... | collective-permute-start | bytes 9437192 | tf_op jit(solution)/shard_map/ppermute | solution.py:28
  421.6 24.4 %copy-start.24 = (bf16[64,4,4,768]{3,2,1,0:T(4,128)(2,1)S(1)}, bf16[64,4,4,768]{3,2,1,0:T(4,128)(2,1)}, u32[]{:S(2)}) copy-start(bf16[64,4,4,768]{3,2,1,0:T(4,128)(2,1)} %copy-done.23) | copy-start | bytes 4718596
  421.6 24.4 %copy-start.26 = (bf16[64,4,4,768]{3,2,1,0:T(4,128)(2,1)S(1)}, bf16[64,4,4,768]{3,2,1,0:T(4,128)(2,1)}, u32[]{:S(2)}) copy-start(bf16[64,4,4,768]{3,2,1,0:T(4,128)(2,1)} %copy-done.25) | copy-start | bytes 4718596
  590.8 47.7 %copy-start.9 = (f32[3136,384]{1,0:T(8,128)}, f32[3136,384]{1,0:T(8,128)S(1)}, u32[]{:S(2)}) copy-start(f32[3136,384]{1,0:T(8,128)S(1)} %get-tuple-element.298) | copy-start | bytes 14450692
  590.9 47.7 %copy-start.45 = (f32[3136]{0:T(1024)}, f32[3136]{0:T(1024)S(1)}, u32[]{:S(2)}) copy-start(f32[3136]{0:T(1024)S(1)} %broadcast_multiply_fusion) | copy-start | bytes 37636
  592.0 46.6 %copy-start.51 = (f32[3136]{0:T(1024)}, f32[3136]{0:T(1024)S(1)}, u32[]{:S(2)}) copy-start(f32[3136]{0:T(1024)S(1)} %fusion.95) | copy-start | bytes 37636
  593.0 13.4 copy-start.19
  593.0 13.4 copy-start.31
  706.9 12.8 copy-start.5
  721.7 9.8 copy-start.3
  721.7 9.8 copy-start.14
  785.6 12.8 copy-start.5
  800.3 9.7 copy-start.3
  800.3 9.7 copy-start.14
  864.1 12.8 copy-start.5
  878.8 9.7 copy-start.3
  878.8 9.7 copy-start.14
  942.6 12.8 copy-start.5
  957.3 9.7 copy-start.3
  957.3 9.7 copy-start.14
  994.1 10.5 copy-start.46
  994.1 10.5 copy-start.52
  994.1 10.5 copy-start.62
  994.1 10.5 copy-start.69
  1001.0 69.6 %collective-permute-start.4 = (bf16[64,4,8,768]{3,2,1,0:T(8,128)(2,1)}, bf16[64,4,8,768]{3,2,1,0:T(8,128)(2,1)}, u32[]{:S(2)}, u32[]{:S(2)}) collective-permute-start(bf16[64,4,8,768]{3,2,1,0:T(8,128)(2,1)} %select_convert_fusion), channel_id=1, source_target_pairs={{0,8},{4,12},{8,0},{12,4},{16,24},{20,28},{24,16},{28,20},{1,9},{5... | collective-permute-start | bytes 9437192 | tf_op jit(solution)/shard_map/ppermute | solution.py:28
  1078.5 28.9 %copy-start.11 = (f32[64,4,8,768]{3,2,1,0:T(8,128)}, f32[64,4,8,768]{3,2,1,0:T(8,128)S(1)}, u32[]{:S(2)}) copy-start(f32[64,4,8,768]{3,2,1,0:T(8,128)S(1)} %convert_add_fusion) | copy-start | bytes 18874372
  1081.2 35.3 %collective-permute-start.5 = (bf16[64,4,4,768]{3,2,1,0:T(4,128)(2,1)}, bf16[64,4,4,768]{3,2,1,0:T(4,128)(2,1)}, u32[]{:S(2)}, u32[]{:S(2)}) collective-permute-start(bf16[64,4,4,768]{3,2,1,0:T(4,128)(2,1)} %select_convert_fusion.1), channel_id=1, source_target_pairs={{0,4},{4,0},{8,12},{12,8},{16,20},{20,16},{24,28},{28,24},{1,5},{5... | collective-permute-start | bytes 4718600 | tf_op jit(solution)/shard_map/ppermute | solution.py:28
  1081.2 26.1 %slice-start.4 = ((s8[9633792]{0:T(1024)(128)(4,1)}), s8[4194304]{0:T(1024)(128)(4,1)S(1)}, s32[]{:S(2)}) async-start(s8[9633792]{0:T(1024)(128)(4,1)} %bitcast.297), calls=%async_computation.10 | async-start | bytes 8388608
  1082.3 25.0 %copy-start.20 = (bf16[1,3136,384]{2,1,0:T(8,128)(2,1)S(1)}, bf16[1,3136,384]{2,1,0:T(8,128)(2,1)}, u32[]{:S(2)}) copy-start(bf16[1,3136,384]{2,1,0:T(8,128)(2,1)} %param.13) | copy-start | bytes 7225348
  1082.3 25.0 %slice-start.5 = ((s8[9633792]{0:T(1024)(128)(4,1)}), s8[4194304]{0:T(1024)(128)(4,1)S(1)}, s32[]{:S(2)}) async-start(s8[9633792]{0:T(1024)(128)(4,1)} %bitcast.297), calls=%async_computation.11 | async-start | bytes 8388608
  1082.3 25.0 %slice-start.6 = ((s8[9633792]{0:T(1024)(128)(4,1)}), s8[1245184]{0:T(1024)(128)(4,1)S(1)}, s32[]{:S(2)}) async-start(s8[9633792]{0:T(1024)(128)(4,1)} %bitcast.297), calls=%async_computation.12 | async-start | bytes 2490368
  1138.2 9.7 copy-start.71
  1138.2 11.1 copy-start.70
  1143.8 85.6 %collective-permute-start.6 = (bf16[64,3,13,768]{3,0,2,1:T(8,128)(2,1)}, bf16[64,3,13,768]{3,0,2,1:T(8,128)(2,1)}, u32[]{:S(2)}, u32[]{:S(2)}) collective-permute-start(bf16[64,3,13,768]{3,0,2,1:T(8,128)(2,1)} %dynamic-slice_convert_fusion), channel_id=1, source_target_pairs={{0,8},{4,12},{8,0},{12,4},{16,24},{20,28},{24,16},{28,20},{1,9},{5... | collective-permute-start | bytes 11501576 | tf_op jit(solution)/shard_map/ppermute | solution.py:28
  1164.2 219.0 %reduce-scatter.7.cloned.1.call-start = ((), (), s32[]{:S(2)}) async-start(), calls=%async_computation.2 | async-start | bytes 1505280
  1182.8 59.4 %copy-start.56 = (s32[7,8]{1,0:T(8,128)S(1)}, s32[7,8]{1,0:T(8,128)}, u32[]{:S(2)}) copy-start(s32[7,8]{1,0:T(8,128)} %copy-done.55) | copy-start | bytes 676
  1242.2 37.5 %collective-permute-start.7 = (bf16[64,7,3,768]{3,0,2,1:T(8,128)(2,1)}, bf16[64,7,3,768]{3,0,2,1:T(8,128)(2,1)}, u32[]{:S(2)}, u32[]{:S(2)}) collective-permute-start(bf16[64,7,3,768]{3,0,2,1:T(8,128)(2,1)} %dynamic-slice_convert_fusion.2), channel_id=1, source_target_pairs={{0,4},{4,0},{8,12},{12,8},{16,20},{20,16},{24,28},{28,24},{1,5},{5... | collective-permute-start | bytes 6193160 | tf_op jit(solution)/shard_map/ppermute | solution.py:28
  1311.3 8.7 copy-start.40
  1345.5 9.3 copy-start.65
  1354.1 91.6 %all-reduce.13.cloned.1.call-start = ((), (), s32[]{:S(2)}) async-start(), calls=%async_computation.4 | async-start | bytes 3571712
  1354.7 30.8 %copy-start.44 = (f32[3136]{0:T(1024)S(1)}, f32[3136]{0:T(1024)}, u32[]{:S(2)}) copy-start(f32[3136]{0:T(1024)} %copy-done.43) | copy-start | bytes 37636
  1385.6 63.8 %copy-start.34 = (f32[18696]{0:T(1024)S(1)}, f32[18696]{0:T(1024)}, u32[]{:S(2)}) copy-start(f32[18696]{0:T(1024)} %param.14) | copy-start | bytes 224356
  1385.6 63.8 %copy-start.49 = (f32[18696]{0:T(1024)S(1)}, f32[18696]{0:T(1024)}, u32[]{:S(2)}) copy-start(f32[18696]{0:T(1024)} %param.16) | copy-start | bytes 224356
  1385.6 63.8 %copy-start.50 = (f32[18696]{0:T(1024)S(1)}, f32[18696]{0:T(1024)}, u32[]{:S(2)}) copy-start(f32[18696]{0:T(1024)} %param.15) | copy-start | bytes 224356
  1385.6 64.5 %copy-start.33 = (f32[36952]{0:T(1024)S(1)}, f32[36952]{0:T(1024)}, u32[]{:S(2)}) copy-start(f32[36952]{0:T(1024)} %param.17) | copy-start | bytes 443428
  1385.6 64.5 %copy-start.37 = (f32[36952]{0:T(1024)S(1)}, f32[36952]{0:T(1024)}, u32[]{:S(2)}) copy-start(f32[36952]{0:T(1024)} %param.19) | copy-start | bytes 443428
  1385.6 64.5 %copy-start.38 = (f32[36952]{0:T(1024)S(1)}, f32[36952]{0:T(1024)}, u32[]{:S(2)}) copy-start(f32[36952]{0:T(1024)} %param.18) | copy-start | bytes 443428
  (52 other events, 235.8 us)
Sparse Core Ops, SparseCore 0:
  15.8 141.9 all-reduce.14
  1164.3 46.2 reduce-scatter.8
  1354.2 28.9 reduce-scatter.6
  1386.5 59.1 all-reduce.12
where the time goes:
time: 1470 us; the launch traced here: 1460 us
  local copies, waits for them, and re-layouts  506 us (34%)
  waiting for transfers between devices  403 us (27%)
  other arithmetic  283 us (19%)
  matrix products  243 us (17%)
  between operations  15.4 us (1%)
    unnamed x8, waiting for transfers between devices  207 us
    ppermute x8, waiting for transfers between devices, swapped(): return lax.ppermute(value, axis, pairs)  196 us
    dynamic_update_slice x12, local copies, waits for them, and re-layouts, body(): lax.scan(backward_block, table_start, (query_blocks, kv_blocks, log_total...  97.7 us
    dot_general x4, matrix products, times_transposed(): lax.dot_general(left, right, (((1,), (1,)), ((), ())), preferred_element_...  43.8 us
    broadcast_in_dim x6, other arithmetic, body(): lax.scan(backward_block, table_start, (query_blocks, kv_blocks, log_total...  41.2 us
    while x2, local copies, waits for them, and re-layouts, body(): mixed_blocks, log_totals = lax.map(forward_block, (query_blocks, kv_blocks))  39.1 us
    dot_general x4, matrix products, backward_block(): jnp.einsum('wqhe,wkhe->whqk', dmix_heads, value_heads, preferred_element_...  36.2 us
    reduce_sum x4, other arithmetic, backward_block(): jnp.sum(d_scores.astype(jnp.float32), axis=0)  33 us
  transfers between devices with their start and end apart: 12, of which 9 were waited for; matrix products, arithmetic and copies ran while one was open for 21% of the time, Pallas kernels for 0%

commit v1 on v0

v1 whole, which is shorter than its diff:
```python
import functools

import jax
import jax.numpy as jnp
import ml_dtypes
import numpy as np
from jax import lax
from jax.experimental import pallas as pl
from jax.experimental.pallas import tpu as pltpu
from jax.sharding import PartitionSpec as P

D = 384
HEADS = 12
HDIM = 32
FF = 1536
WIN = 7
STEP = 10
SEQ = WIN * WIN
HALF = 64
FINE = (3 * WIN - 2) ** 2
COARSE = (2 * WIN - 1) ** 2
KEYS = 192

beta_one = 0.9
beta_two = 0.999
learn_rate = 0.04
decay_rate = 0.05
adam_eps = 1e-08
norm_eps = 1e-05
masked_score = -1e30

F32 = jnp.float32
BF16 = jnp.bfloat16
MESH = pl.DeviceIdType.MESH
VMEM_LIMIT = 56 * 2**20


def token_place(gy, gx):
    window = 2 * (gy // WIN) + gx // WIN
    return window * HALF + (gy % WIN) * WIN + gx % WIN


@functools.cache
def gather_tables(images):
    keys = np.zeros((images, 256, 256), np.float32)
    queries = np.zeros((images, 256, 256), np.float32)
    for i in range(images):
        for gy in range(2 * WIN):
            for gx in range(2 * WIN):
                at = token_place(gy, gx) + i
                key = gy * 14 + gx if gy < 10 else 192 + (gy - 10) * 14 + gx
                keys[i, key, at] = 1.0
                keys[i, 140 + (gy // 2) * WIN + gx // 2, at] = 0.25
                queries[i, (gy // WIN) * 128 + (gy % WIN) * 14 + gx, at] = 1.0
    return (
        keys.astype(ml_dtypes.bfloat16),
        queries.astype(ml_dtypes.bfloat16),
        np.ascontiguousarray(keys.transpose(0, 2, 1)).astype(ml_dtypes.bfloat16),
        np.ascontiguousarray(queries.transpose(0, 2, 1)).astype(ml_dtypes.bfloat16),
    )


@functools.cache
def bias_tables():
    fine = np.zeros((14, 384, 384), np.float32)
    coarse = np.zeros((14, 256, 128), np.float32)
    for qx in range(14):
        for a in range(27):
            for kx in range(14):
                col = kx - qx + 9
                if 4 <= a <= 22 and 0 <= col <= 18:
                    fine[qx, 19 * (a - 4) + col, a * 14 + kx] = 1.0
        for p in range(13):
            for s in range(WIN):
                coarse[qx, 13 * p + s - qx // 2 + 6, p * WIN + s] = 1.0
    mask = np.zeros((2, KEYS, 128), np.float32)
    for half in range(2):
        for q in range(98):
            qx = q % 14
            for e in range(KEYS):
                at = e + 56 * half
                if at < 140:
                    ok = abs_ok(qx, at % 14)
                elif at < 189:
                    ok = True
                elif at < 192:
                    ok = False
                else:
                    ok = at < 248 and abs_ok(qx, (at - 192) % 14)
                mask[half, e, q] = 0.0 if ok else masked_score
    return fine.astype(ml_dtypes.bfloat16), coarse.astype(ml_dtypes.bfloat16), mask


def abs_ok(qx, kx):
    return kx < 10 if qx < WIN else kx >= 4


def bias_runs(half, qy):
    fine = (13 - qy) * 14
    pool = 384 + (6 - qy // 2) * WIN
    if half == 0:
        return [(0, 140, fine), (140, 49, pool)]
    return [(0, 84, fine + 56), (84, 49, pool), (136, 56, fine + 140)]


class Flat:
    def __init__(self, devices, part_a, part_b):
        self.devices = devices
        self.part = (part_a, part_b)
        self.rows = tuple(-(-((p + 126) // 128 + 1) // 8) * 8 for p in self.part)
        self.total = sum(self.rows)
        extra = -self.total % 16
        self.rows = (self.rows[0], self.rows[1] + extra)
        self.total += extra
        self.buffer = tuple(
            -(-(self.start(w, devices - 1) + self.rows[w]) // 8) * 8 for w in range(2)
        )

    def start(self, which, device):
        return device * self.part[which] // 128


def bit_order(n_dp, n_grp):
    dp_bits = [("dp", 2**b) for b in range(n_dp.bit_length() - 1)]
    grp_bits = [("grp", 2**b) for b in reversed(range(n_grp.bit_length() - 1))]
    return dp_bits[1:2] + grp_bits + dp_bits[2:] + dp_bits[:1]


def place_of(order, dp, grp):
    place = 0
    for k, (axis, stride) in enumerate(order):
        place = place + ((dp if axis == "dp" else grp) // stride) % 2 * 2**k
    return place


def partner_of(axis, stride, dp, grp):
    if axis == "dp":
        return (dp + (1 - 2 * ((dp // stride) % 2)) * stride, grp)
    return (dp, grp + (1 - 2 * ((grp // stride) % 2)) * stride)


def greet(order, dp, grp):
    barrier = pltpu.get_barrier_semaphore()
    for axis, stride in order:
        pl.semaphore_signal(
            barrier, inc=1, device_id=partner_of(axis, stride, dp, grp), device_id_type=MESH
        )
    pl.semaphore_wait(barrier, len(order))


def shift_lanes(values, amount, up):
    lane = lax.broadcasted_iota(jnp.int32, values.shape, 1)
    if up:
        turned = pltpu.roll(values, amount, 1)
        return jnp.where(lane >= amount, turned, pltpu.roll(turned, 1, 0))
    turned = pltpu.roll(values, lax.rem(128 - amount, 128), 1)
    return jnp.where(lane < 128 - amount, turned, pltpu.roll(turned, values.shape[0] - 1, 0))


def gather_kernel(flat, order, a_ref, b_ref, out_ref, own, own_sem, send_sems, recv_sems):
    dp, grp = lax.axis_index("dp"), lax.axis_index("grp")
    device = dp * lax.axis_size("grp") + grp
    place = place_of(order, dp, grp)
    parts = [
        shift_lanes(ref[...], lax.rem(device * flat.part[w], 128), True)
        for w, ref in enumerate((a_ref, b_ref))
    ]
    own[...] = jnp.concatenate(parts, axis=0).astype(BF16)
    copy = pltpu.make_async_copy(own, out_ref.at[place], own_sem)
    copy.start()
    greet(order, dp, grp)
    copy.wait()
    for k, (axis, stride) in enumerate(order):
        held = out_ref.at[pl.ds(place // 2**k * 2**k, 2**k)]
        send = pltpu.make_async_remote_copy(
            src_ref=held,
            dst_ref=held,
            send_sem=send_sems.at[k],
            recv_sem=recv_sems.at[k],
            device_id=partner_of(axis, stride, dp, grp),
            device_id_type=MESH,
        )
        send.start()
        send.wait()


def gather_params(flat, order, master_a, master_b):
    padded = [
        jnp.pad(m, (0, flat.rows[w] * 128 - m.shape[0])).reshape(flat.rows[w], 128)
        for w, m in enumerate((master_a, master_b))
    ]
    stages = len(order)
    return pl.pallas_call(
        functools.partial(gather_kernel, flat, order),
        out_shape=jax.ShapeDtypeStruct((flat.devices, flat.total, 128), BF16),
        in_specs=[pl.BlockSpec(memory_space=pltpu.VMEM)] * 2,
        out_specs=pl.BlockSpec(memory_space=pl.ANY),
        scratch_shapes=[
            pltpu.VMEM((flat.total, 128), BF16),
            pltpu.SemaphoreType.DMA,
            pltpu.SemaphoreType.DMA((stages,)),
            pltpu.SemaphoreType.DMA((stages,)),
        ],
        compiler_params=pltpu.CompilerParams(
            collective_id=0, has_side_effects=True, vmem_limit_bytes=VMEM_LIMIT
        ),
        name="gather_params",
    )(*padded)


def sum_kernel(
    flat, order, x_ref, a_ref, b_ref, total, outgoing, arrived, send_sems, recv_sems
):
    dp, grp = lax.axis_index("dp"), lax.axis_index("grp")
    device = dp * lax.axis_size("grp") + grp
    place = place_of(order, dp, grp)
    greet(order, dp, grp)
    stages = len(order)
    for k in reversed(range(stages)):
        axis, stride = order[k]
        size = 2**k
        mine = place // size % 2 * size
        other = size - mine
        if k == stages - 1:
            source = x_ref.at[pl.ds(other, size)]
        else:

            def fill(j, carry):
                outgoing[size + j] = total[other + j].astype(BF16)
                return carry

            lax.fori_loop(0, size, fill, 0)
            source = outgoing.at[pl.ds(size, size)]
        send = pltpu.make_async_remote_copy(
            src_ref=source,
            dst_ref=arrived.at[pl.ds(size, size)],
            send_sem=send_sems.at[k],
            recv_sem=recv_sems.at[k],
            device_id=partner_of(axis, stride, dp, grp),
            device_id_type=MESH,
        )
        send.start()
        send.wait()

        def add(j, carry):
            if k == stages - 1:
                held = x_ref[mine + j].astype(F32)
            else:
                held = total[mine + j]
            total[j] = held + arrived[size + j].astype(F32)
            return carry

        lax.fori_loop(0, size, add, 0)
    result = total[0]
    rows = flat.rows[0]
    for w, (ref, part) in enumerate(((a_ref, result[:rows]), (b_ref, result[rows:]))):
        ref[...] = shift_lanes(part, lax.rem(device * flat.part[w], 128), False)


def sum_grads(flat, order, blocks):
    stages = len(order)
    n = flat.devices
    outs = pl.pallas_call(
        functools.partial(sum_kernel, flat, order),
        out_shape=[jax.ShapeDtypeStruct((r, 128), F32) for r in flat.rows],
        in_specs=[pl.BlockSpec(memory_space=pltpu.VMEM)],
        out_specs=[pl.BlockSpec(memory_space=pltpu.VMEM)] * 2,
        scratch_shapes=[
            pltpu.VMEM((n // 2, flat.total, 128), F32),
            pltpu.VMEM((n // 2, flat.total, 128), BF16),
            pltpu.VMEM((n, flat.total, 128), BF16),
            pltpu.SemaphoreType.DMA((stages,)),
            pltpu.SemaphoreType.DMA((stages,)),
        ],
        compiler_params=pltpu.CompilerParams(
            collective_id=1, has_side_effects=True, vmem_limit_bytes=VMEM_LIMIT
        ),
        name="sum_grads",
    )(blocks)
    return [o.reshape(-1)[: flat.part[w]] for w, o in enumerate(outs)]


def place_list(order, n_dp, n_grp):
    return [place_of(order, d // n_grp, d % n_grp) for d in range(n_dp * n_grp)]


ATTN_VECTORS = (D * 3 * D + D * D + HEADS * FINE + HEADS * COARSE, 5)
TABLE_AT = D * 3 * D + D * D


def prep_kernel(
    flat,
    places,
    parts_ref,
    one_fine,
    one_coarse,
    mask_ref,
    wqkv,
    wproj,
    w1,
    w2,
    vecs,
    bias,
    flat_a,
    flat_b,
    tab_fine,
    tab_coarse,
    shifted,
    turned,
):
    flat_a[...] = jnp.zeros_like(flat_a)
    flat_b[...] = jnp.zeros_like(flat_b)
    for device, place in enumerate(places):
        block = parts_ref[place].astype(F32)
        a_at, b_at = flat.start(0, device), flat.start(1, device)
        a_rows, b_rows = flat.rows
        flat_a[a_at : a_at + a_rows, :] += block[:a_rows]
        flat_b[b_at : b_at + b_rows, :] += block[a_rows:]
    for j in range(9):
        wqkv[:, j * 128 : (j + 1) * 128] = flat_a[pl.ds(j, D, stride=9), :].astype(BF16)
    for j in range(3):
        wproj[:, j * 128 : (j + 1) * 128] = flat_a[pl.ds(3456 + j, D, stride=3), :].astype(BF16)
        w2[:, j * 128 : (j + 1) * 128] = flat_b[pl.ds(4608 + j, FF, stride=3), :].astype(BF16)
    for j in range(12):
        w1[:, j * 128 : (j + 1) * 128] = flat_b[pl.ds(j, D, stride=12), :].astype(BF16)
    vecs[...] = jnp.zeros_like(vecs)
    row, lane = divmod(ATTN_VECTORS[0], 128)
    rows = shift_lanes(flat_a[row : row + 16, :], lane, False)
    for v in range(5):
        for j in range(3):
            vecs[v : v + 1, j * 128 : (j + 1) * 128] = rows[3 * v + j : 3 * v + j + 1]
    for j in range(12):
        vecs[8:9, j * 128 : (j + 1) * 128] = flat_b[9216 + j : 9217 + j, :]
    for v in range(3):
        for j in range(3):
            at = 9228 + 3 * v + j
            vecs[5 + v : 6 + v, j * 128 : (j + 1) * 128] = flat_b[at : at + 1, :]
    tab_fine[...] = jnp.zeros_like(tab_fine)
    tab_coarse[...] = jnp.zeros_like(tab_coarse)
    for ref, first, length in (
        (tab_fine, TABLE_AT, FINE),
        (tab_coarse, TABLE_AT + HEADS * FINE, COARSE),
    ):
        for h in range(HEADS):
            row, lane = divmod(first + h * length, 128)
            count = -(-(lane + length) // 128)
            line = jnp.concatenate(
                [flat_a[row + c : row + c + 1, :] for c in range(count)], axis=1
            )
            ref[h : h + 1, 0:length] = line[:, lane : lane + length]
    for qx in range(14):
        at = slice(qx * 16, qx * 16 + 16)
        moved = dot(tab_fine[...].astype(BF16), one_fine[qx])
        for c in range(3):
            shifted[c, at, :] = moved[:, c * 128 : (c + 1) * 128]
        shifted[3, at, :] = dot(tab_coarse[...].astype(BF16), one_coarse[qx])
    turned[...] = jnp.zeros_like(turned)
    for h in range(HEADS):
        table = jnp.concatenate(
            [shifted[c, pl.ds(h, 14, stride=16), :] for c in range(4)], axis=1
        )
        for half in range(2):
            for y in range(WIN):
                for at, length, source in bias_runs(half, WIN * half + y):
                    turned[half, y * 14 : y * 14 + 14, at : at + length] = table[
                        :, source : source + length
                    ]
            bias[h, half] = turned[half].T[0:KEYS] + mask_ref[half]


def prepare(flat, places, gathered):
    fine, coarse, mask = bias_tables()
    vm = pl.BlockSpec(memory_space=pltpu.VMEM)
    return pl.pallas_call(
        functools.partial(prep_kernel, flat, places),
        out_shape=[
            jax.ShapeDtypeStruct((D, 3 * D), BF16),
            jax.ShapeDtypeStruct((D, D), BF16),
            jax.ShapeDtypeStruct((D, FF), BF16),
            jax.ShapeDtypeStruct((FF, D), BF16),
            jax.ShapeDtypeStruct((16, FF), F32),
            jax.ShapeDtypeStruct((HEADS, 2, KEYS, 128), F32),
        ],
        in_specs=[vm] * 4,
        out_specs=[vm] * 6,
        scratch_shapes=[
            pltpu.VMEM((flat.buffer[0], 128), F32),
            pltpu.VMEM((flat.buffer[1], 128), F32),
            pltpu.VMEM((16, 384), F32),
            pltpu.VMEM((16, 256), F32),
            pltpu.VMEM((4, 14 * 16, 128), F32),
            pltpu.VMEM((2, 128, 256), F32),
        ],
        compiler_params=pltpu.CompilerParams(vmem_limit_bytes=VMEM_LIMIT),
        name="prepare",
    )(gathered, jnp.asarray(fine), jnp.asarray(coarse), jnp.asarray(mask))


def dot(a, b):
    return jnp.dot(a, b, preferred_element_type=F32)


def dot_t(a, b):
    return lax.dot_general(a, b, (((1,), (1,)), ((), ())), preferred_element_type=F32)


def norm_parts(values):
    centered = values - jnp.mean(values, axis=-1, keepdims=True)
    scale = lax.rsqrt(jnp.mean(centered * centered, axis=-1, keepdims=True) + norm_eps)
    return centered * scale, scale


def norm_back(d_normed, xhat, scale, gain):
    dh = d_normed * gain
    return scale * (
        dh
        - jnp.mean(dh, axis=-1, keepdims=True)
        - xhat * jnp.mean(dh * xhat, axis=-1, keepdims=True)
    )


def xor_slot(slot, k):
    low, high = lax.rem(slot, 2), slot // 2
    if k % 2:
        low = 1 - low
    if k // 2:
        high = 1 - high
    return 2 * high + low


def split_copies(slot, refs, whole, sems, rows, outward):
    copies = []
    for k, ref in enumerate(refs):
        part = whole.at[pl.ds(pl.multiple_of(xor_slot(slot, k) * rows, 16), rows)]
        ends = (part, ref) if outward else (ref, part)
        copies.append(pltpu.make_async_copy(*ends, sems.at[k]))
    return copies


def lane_heads(j):
    lane = lax.broadcasted_iota(jnp.int32, (256, 128), 1)
    return (lane // HDIM) == j


def image_rows(ref, i, rows, columns):
    at = pl.multiple_of(48 * i, 16)
    parts = [
        ref[pl.ds(pl.multiple_of(w * rows + at, 16), HALF), columns] for w in range(4)
    ]
    return jnp.concatenate(parts, axis=0)


def put_image_rows(ref, i, rows, columns, values):
    at = 48 * i
    for w in range(4):
        part = values[w * HALF : (w + 1) * HALF]
        first = pl.ds(pl.multiple_of(w * rows + at, 16), 16)
        rest = pl.ds(pl.multiple_of(w * rows + at + 16, 16), HALF - 16)
        held = jnp.where(i > 0, ref[first, columns].astype(F32), 0.0)
        ref[first, columns] = (held + part[:16]).astype(ref.dtype)
        ref[rest, columns] = part[16:].astype(ref.dtype)


def attend_kernel(
    rows,
    slot_ref,
    tok_ref,
    in1,
    in2,
    in3,
    wqkv,
    vecs,
    bias,
    keys_tab,
    query_tab,
    query_back,
    mixed,
    probs,
    qkv,
    x_out,
    x_buf,
    normed,
    mixed_t,
    sems,
    out_sem,
):
    i = pl.program_id(0)
    slot = slot_ref[0]

    @pl.when(i == 0)
    def _():
        own = tok_ref.at[pl.ds(pl.multiple_of(slot * rows, 16), rows)]
        copies = split_copies(slot, (own, in1, in2, in3), x_buf, sems, rows, False)
        for c in copies:
            c.start()
        for c in copies:
            c.wait()
        pltpu.make_async_copy(x_buf, x_out, out_sem).start()

        def project(w, carry):
            base = pl.multiple_of(w * rows, 16)
            step = rows // 7

            def norm(c, inner):
                at = pl.multiple_of(c * step, 16)
                xhat, _ = norm_parts(x_buf[pl.ds(base + at, step), :].astype(F32))
                normed[pl.ds(at, step), :] = (xhat * vecs[0:1, :D] + vecs[1:2, :D]).astype(BF16)
                return inner

            lax.fori_loop(0, 7, norm, 0)
            here = pl.ds(base, rows)
            q = dot(normed[...], wqkv[:, :D]) + vecs[2:3, :D]
            qkv[here, :D] = (q * HDIM ** (-0.5)).astype(BF16)
            qkv[here, D : 2 * D] = dot(normed[...], wqkv[:, D : 2 * D]).astype(BF16)
            v = dot(normed[...], wqkv[:, 2 * D :]) + vecs[3:4, :D]
            qkv[here, 2 * D :] = v.astype(BF16)
            return carry

        lax.fori_loop(0, 4, project, 0)

    q_ext = dot(query_tab[0], image_rows(qkv, i, rows, slice(0, D))).astype(BF16)
    kv_ext = dot(keys_tab[0], image_rows(qkv, i, rows, slice(D, 3 * D)))
    k_ext = kv_ext[:, :D].astype(BF16)
    v_t = kv_ext[:, D:].T.astype(BF16)
    for h in range(HEADS):
        tile = slice(h // 4 * 128, h // 4 * 128 + 128)
        q_head = jnp.where(lane_heads(h % 4), q_ext[:, tile], 0)
        scores = dot_t(k_ext[:, tile], q_head)
        halves = []
        for half in range(2):
            s = scores[56 * half : 56 * half + KEYS, 128 * half : 128 * half + 128] + bias[h, half]
            e = jnp.exp(s - jnp.max(s, axis=0, keepdims=True))
            p = e * (1.0 / jnp.sum(e, axis=0, keepdims=True))
            above, below = 56 * half, 64 - 56 * half
            pieces = [p, jnp.zeros((below, 128), F32)]
            if above:
                pieces = [jnp.zeros((above, 128), F32)] + pieces
            halves.append(jnp.concatenate(pieces, axis=0))
        p = jnp.concatenate(halves, axis=1).astype(BF16)
        probs[0, h] = p
        mixed_t[h * HDIM : (h + 1) * HDIM, :] = dot(
            v_t[h * HDIM : (h + 1) * HDIM, :], p
        ).astype(BF16)
    put_image_rows(mixed, i, rows, slice(None), dot_t(query_back[0], mixed_t[...]))

    @pl.when(i == pl.num_programs(0) - 1)
    def _():
        pltpu.make_async_copy(x_buf, x_out, out_sem).wait()


def attend(slot, tok, arrived, wqkv, vecs, bias, images):
    tokens = tok.shape[0]
    rows = tokens // 4
    keys_tab, query_tab, _, query_back = gather_tables(images)
    vm = pl.BlockSpec(memory_space=pltpu.VMEM)
    hbm = pl.BlockSpec(memory_space=pl.ANY)
    table = pl.BlockSpec((1, 256, 256), lambda i: (i, 0, 0))
    whole = lambda width: pl.BlockSpec((tokens, width), lambda i: (0, 0))
    return pl.pallas_call(
        functools.partial(attend_kernel, rows),
        grid=(images,),
        out_shape=[
            jax.ShapeDtypeStruct((tokens, D), BF16),
            jax.ShapeDtypeStruct((images, HEADS, 256, 256), BF16),
            jax.ShapeDtypeStruct((tokens, 3 * D), BF16),
            jax.ShapeDtypeStruct((tokens, D), BF16),
        ],
        in_specs=[pl.BlockSpec(memory_space=pltpu.SMEM)] + [hbm] * 4 + [vm] * 3 + [table] * 3,
        out_specs=[
            whole(D),
            pl.BlockSpec((1, HEADS, 256, 256), lambda i: (i, 0, 0, 0)),
            whole(3 * D),
            hbm,
        ],
        scratch_shapes=[
            pltpu.VMEM((tokens, D), BF16),
            pltpu.VMEM((rows, D), BF16),
            pltpu.VMEM((D, 256), BF16),
            pltpu.SemaphoreType.DMA((4,)),
            pltpu.SemaphoreType.DMA,
        ],
        compiler_params=pltpu.CompilerParams(vmem_limit_bytes=VMEM_LIMIT),
        name="attend",
    )(slot, tok, *arrived, wqkv, vecs, bias, keys_tab, query_tab, query_back)


GELU_A = float(np.sqrt(2.0 / np.pi))
GELU_B = 0.044715


def mlp_kernel(
    rows,
    slot_ref,
    cot_ref,
    in1,
    in2,
    in3,
    mixed_ref,
    x_ref,
    wproj,
    w1,
    w2,
    vecs,
    out0,
    out1,
    out2,
    out3,
    d_res_ref,
    d_mixed_ref,
    g_w1,
    g_w2t,
    g_proj,
    g_vec,
    g_buf,
    o_buf,
    sems,
):
    i = pl.program_id(0)
    slot = slot_ref[0]
    chunk = mixed_ref.shape[0]

    @pl.when(i == 0)
    def _():
        own = cot_ref.at[pl.ds(pl.multiple_of(slot * rows, 16), rows)]
        copies = split_copies(slot, (own, in1, in2, in3), g_buf, sems, rows, False)
        for c in copies:
            c.start()
        for c in copies:
            c.wait()
        g_w1[...] = jnp.zeros_like(g_w1)
        g_w2t[...] = jnp.zeros_like(g_w2t)
        g_proj[...] = jnp.zeros_like(g_proj)
        g_vec[...] = jnp.zeros_like(g_vec)

    here = pl.ds(pl.multiple_of(i * chunk, 16), chunk)
    mix = mixed_ref[...]
    res = x_ref[...].astype(F32) + dot(mix, wproj[...]) + vecs[4:5, :D]
    xhat, scale = norm_parts(res)
    gain = vecs[5:6, :D]
    normed = (xhat * gain + vecs[6:7, :D]).astype(BF16)
    grad = g_buf[here, :]
    grad_t = grad.T
    normed_t = normed.T
    out = res + vecs[7:8, :D]
    d_normed = jnp.zeros((chunk, D), F32)
    for f in range(3):
        cols = slice(f * 512, f * 512 + 512)
        hidden = dot(normed, w1[:, cols]) + vecs[8:9, cols]
        square = hidden * hidden
        t = jnp.tanh(hidden * (GELU_A + (GELU_A * GELU_B) * square))
        half = 0.5 + 0.5 * t
        act = (hidden * half).astype(BF16)
        slope = half + (0.5 * hidden) * (1.0 - t * t) * (GELU_A + (3 * GELU_A * GELU_B) * square)
        out += dot(act, w2[cols, :])
        d_hidden32 = dot_t(grad, w2[cols, :]) * slope
        d_hidden = d_hidden32.astype(BF16)
        g_vec[0:1, cols] += jnp.sum(d_hidden32, axis=0, keepdims=True)
        d_normed += dot_t(d_hidden, w1[:, cols])
        g_w1[:, cols] += dot(normed_t, d_hidden)
        g_w2t[:, cols] += dot(grad_t, act)
    o_buf[here, :] = out.astype(BF16)
    grad32 = grad.astype(F32)
    d_res = grad32 + norm_back(d_normed, xhat, scale, gain)
    d_res_ref[...] = d_res
    d_attn = d_res.astype(BF16)
    d_mixed_ref[...] = dot_t(d_attn, wproj[...]).astype(BF16)
    g_proj[...] += dot(mix.T, d_attn)
    g_vec[1:2, :D] += jnp.sum(d_normed * xhat, axis=0, keepdims=True)
    g_vec[2:3, :D] += jnp.sum(d_normed, axis=0, keepdims=True)
    g_vec[3:4, :D] += jnp.sum(grad32, axis=0, keepdims=True)
    g_vec[4:5, :D] += jnp.sum(d_res, axis=0, keepdims=True)

    @pl.when(i == pl.num_programs(0) - 1)
    def _():
        copies = split_copies(slot, (out0, out1, out2, out3), o_buf, sems, rows, True)
        for c in copies:
            c.start()
        for c in copies:
            c.wait()


def mlp(slot, cot, arrived, mixed, x, wproj, w1, w2, vecs):
    tokens = x.shape[0]
    rows = tokens // 4
    chunk = tokens // 7
    vm = pl.BlockSpec(memory_space=pltpu.VMEM)
    hbm = pl.BlockSpec(memory_space=pl.ANY)
    tile = pl.BlockSpec((chunk, D), lambda i: (i, 0))
    fixed = lambda *shape: pl.BlockSpec(shape, lambda i: (0, 0))
    return pl.pallas_call(
        functools.partial(mlp_kernel, rows),
        grid=(7,),
        out_shape=[jax.ShapeDtypeStruct((rows, D), BF16)] * 4
        + [
            jax.ShapeDtypeStruct((tokens, D), F32),
            jax.ShapeDtypeStruct((tokens, D), BF16),
            jax.ShapeDtypeStruct((D, FF), F32),
            jax.ShapeDtypeStruct((D, FF), F32),
            jax.ShapeDtypeStruct((D, D), F32),
            jax.ShapeDtypeStruct((8, FF), F32),
        ],
        in_specs=[pl.BlockSpec(memory_space=pltpu.SMEM)] + [hbm] * 4 + [tile] * 2 + [vm] * 4,
        out_specs=[hbm] * 4
        + [tile, tile, fixed(D, FF), fixed(D, FF), fixed(D, D), fixed(8, FF)],
        scratch_shapes=[
            pltpu.VMEM((tokens, D), BF16),
            pltpu.VMEM((tokens, D), BF16),
            pltpu.SemaphoreType.DMA((4,)),
        ],
        compiler_params=pltpu.CompilerParams(vmem_limit_bytes=VMEM_LIMIT),
        name="mlp",
    )(slot, cot, *arrived, mixed, x, wproj, w1, w2, vecs)


def attend_back_kernel(
    rows,
    qkv,
    d_mixed,
    probs,
    keys_tab,
    query_tab,
    keys_back,
    query_back,
    d_qkv,
    g_bias,
    d_query_t,
    d_key_value,
):
    i = pl.program_id(0)

    @pl.when(i == 0)
    def _():
        g_bias[...] = jnp.zeros_like(g_bias)

    q_ext = dot(query_tab[0], image_rows(qkv, i, rows, slice(0, D))).astype(BF16)
    dm_ext = dot(query_tab[0], image_rows(d_mixed, i, rows, slice(None))).astype(BF16)
    kv_ext = dot(keys_tab[0], image_rows(qkv, i, rows, slice(D, 3 * D)))
    k_t = kv_ext[:, :D].T.astype(BF16)
    v_ext = kv_ext[:, D:].astype(BF16)
    for tile_at in range(3):
        tile = slice(tile_at * 128, tile_at * 128 + 128)
        d_key = jnp.zeros((256, 128), F32)
        d_value = jnp.zeros((256, 128), F32)
        for j in range(4):
            h = tile_at * 4 + j
            mine = lane_heads(j)
            q_head = jnp.where(mine, q_ext[:, tile], 0)
            dm_head = jnp.where(mine, dm_ext[:, tile], 0)
            p = probs[0, h]
            d_value += dot(p, dm_head)
            d_probs = dot_t(v_ext[:, tile], dm_head)
            halves = []
            for half in range(2):
                at = (slice(56 * half, 56 * half + KEYS), slice(128 * half, 128 * half + 128))
                p32 = p[:, at[1]].astype(F32)[at[0]]
                dp = d_probs[at]
                ds = p32 * (dp - jnp.sum(p32 * dp, axis=0, keepdims=True))
                g_bias[h, half] += ds
                above, below = 56 * half, 64 - 56 * half
                pieces = [ds, jnp.zeros((below, 128), F32)]
                if above:
                    pieces = [jnp.zeros((above, 128), F32)] + pieces
                halves.append(jnp.concatenate(pieces, axis=0))
            ds = jnp.concatenate(halves, axis=1).astype(BF16)
            d_key += dot(ds, q_head)
            d_query_t[h * HDIM : (h + 1) * HDIM, :] = (
                dot(k_t[h * HDIM : (h + 1) * HDIM, :], ds) * HDIM ** (-0.5)
            ).astype(BF16)
        d_key_value[:, tile] = d_key.astype(BF16)
        d_key_value[:, D + tile_at * 128 : D + tile_at * 128 + 128] = d_value.astype(BF16)
    put_image_rows(d_qkv, i, rows, slice(0, D), dot_t(query_back[0], d_query_t[...]))
    put_image_rows(d_qkv, i, rows, slice(D, 3 * D), dot(keys_back[0], d_key_value[...]))


def attend_back(qkv, d_mixed, probs, images):
    tokens = qkv.shape[0]
    tables = gather_tables(images)
    vm = pl.BlockSpec(memory_space=pltpu.VMEM)
    table = pl.BlockSpec((1, 256, 256), lambda i: (i, 0, 0))
    return pl.pallas_call(
        functools.partial(attend_back_kernel, tokens // 4),
        grid=(images,),
        out_shape=[
            jax.ShapeDtypeStruct((tokens, 3 * D), BF16),
            jax.ShapeDtypeStruct((HEADS, 2, KEYS, 128), F32),
        ],
        in_specs=[vm, vm, pl.BlockSpec((1, HEADS, 256, 256), lambda i: (i, 0, 0, 0))]
        + [table] * 4,
        out_specs=[
            pl.BlockSpec((tokens, 3 * D), lambda i: (0, 0)),
            pl.BlockSpec((HEADS, 2, KEYS, 128), lambda i: (0, 0, 0, 0)),
        ],
        scratch_shapes=[pltpu.VMEM((D, 256), BF16), pltpu.VMEM((256, 2 * D), BF16)],
        compiler_params=pltpu.CompilerParams(vmem_limit_bytes=VMEM_LIMIT),
        name="attend_back",
    )(qkv, d_mixed, probs, *tables)


def input_kernel(
    rows,
    slot_ref,
    d_qkv_ref,
    x_ref,
    d_res_ref,
    wqkv,
    vecs,
    out0,
    out1,
    out2,
    out3,
    g_qkv,
    g_vec,
    o_buf,
    sems,
):
    i = pl.program_id(0)
    slot = slot_ref[0]
    chunk = x_ref.shape[0]

    @pl.when(i == 0)
    def _():
        g_qkv[...] = jnp.zeros_like(g_qkv)
        g_vec[...] = jnp.zeros_like(g_vec)

    xhat, scale = norm_parts(x_ref[...].astype(F32))
    gain = vecs[0:1, :D]
    normed = (xhat * gain + vecs[1:2, :D]).astype(BF16)
    d_qkv = d_qkv_ref[...]
    d_normed = dot_t(d_qkv, wqkv[...])
    d_in = d_res_ref[...] + norm_back(d_normed, xhat, scale, gain)
    o_buf[pl.ds(pl.multiple_of(i * chunk, 16), chunk), :] = d_in.astype(BF16)
    g_qkv[...] += dot(normed.T, d_qkv)
    g_vec[0:1, :] += jnp.sum(d_qkv.astype(F32), axis=0, keepdims=True)
    g_vec[1:2, :D] += jnp.sum(d_normed * xhat, axis=0, keepdims=True)
    g_vec[2:3, :D] += jnp.sum(d_normed, axis=0, keepdims=True)

    @pl.when(i == pl.num_programs(0) - 1)
    def _():
        copies = split_copies(slot, (out0, out1, out2, out3), o_buf, sems, rows, True)
        for c in copies:
            c.start()
        for c in copies:
            c.wait()


def input_back(slot, d_qkv, x, d_res, wqkv, vecs):
    tokens = x.shape[0]
    rows = tokens // 4
    chunk = tokens // 7
    vm = pl.BlockSpec(memory_space=pltpu.VMEM)
    hbm = pl.BlockSpec(memory_space=pl.ANY)
    tile = lambda width: pl.BlockSpec((chunk, width), lambda i: (i, 0))
    return pl.pallas_call(
        functools.partial(input_kernel, rows),
        grid=(7,),
        out_shape=[jax.ShapeDtypeStruct((rows, D), BF16)] * 4
        + [jax.ShapeDtypeStruct((D, 3 * D), F32), jax.ShapeDtypeStruct((8, 3 * D), F32)],
        in_specs=[pl.BlockSpec(memory_space=pltpu.SMEM), tile(3 * D), tile(D), tile(D), vm, vm],
        out_specs=[hbm] * 4
        + [
            pl.BlockSpec((D, 3 * D), lambda i: (0, 0)),
            pl.BlockSpec((8, 3 * D), lambda i: (0, 0)),
        ],
        scratch_shapes=[pltpu.VMEM((tokens, D), BF16), pltpu.SemaphoreType.DMA((4,))],
        compiler_params=pltpu.CompilerParams(vmem_limit_bytes=VMEM_LIMIT),
        name="input_back",
    )(slot, d_qkv, x, d_res, wqkv, vecs)


def pack_kernel(
    flat,
    places,
    one_fine,
    one_coarse,
    g_bias,
    g_qkv,
    g_vec1,
    g_proj,
    g_w1,
    g_w2t,
    g_vec2,
    out,
    flat_a,
    flat_b,
    table,
    shifted,
    line,
):
    flat_a[...] = jnp.zeros_like(flat_a)
    flat_b[...] = jnp.zeros_like(flat_b)
    for j in range(9):
        flat_a[pl.ds(j, D, stride=9), :] = g_qkv[:, j * 128 : (j + 1) * 128]
    for j in range(3):
        flat_a[pl.ds(3456 + j, D, stride=3), :] = g_proj[:, j * 128 : (j + 1) * 128]
        flat_b[pl.ds(4608 + j, FF, stride=3), :] = g_w2t[j * 128 : (j + 1) * 128, :].T
    for j in range(12):
        flat_b[pl.ds(j, D, stride=12), :] = g_w1[:, j * 128 : (j + 1) * 128]
        flat_b[9216 + j : 9217 + j, :] = g_vec2[0:1, j * 128 : (j + 1) * 128]
    for v in range(3):
        for j in range(3):
            at = 9228 + 3 * v + j
            flat_b[at : at + 1, :] = g_vec2[1 + v : 2 + v, j * 128 : (j + 1) * 128]
    vectors = [
        g_vec1[1:2, :D],
        g_vec1[2:3, :D],
        g_vec1[0:1, :D],
        g_vec1[0:1, 2 * D :],
        g_vec2[4:5, :D],
    ]
    pieces = [v[:, j * 128 : (j + 1) * 128] for v in vectors for j in range(3)]
    pieces += [jnp.zeros((1, 128), F32)]
    row, lane = divmod(ATTN_VECTORS[0], 128)
    flat_a[row : row + 16, :] += shift_lanes(jnp.concatenate(pieces, axis=0), lane, True)
    for h in range(HEADS):
        table[...] = jnp.zeros_like(table)
        for half in range(2):
            turned = g_bias[h, half].T
            for y in range(WIN):
                for at, length, source in bias_runs(half, WIN * half + y):
                    table[0:14, source : source + length] += turned[
                        y * 14 : y * 14 + 14, at : at + length
                    ]
        for c in range(4):
            shifted[c, pl.ds(h, 14, stride=16), :] = table[0:14, c * 128 : (c + 1) * 128]
    g_fine = jnp.zeros((16, 384), F32)
    g_coarse = jnp.zeros((16, 256), F32)
    for qx in range(14):
        at = slice(qx * 16, qx * 16 + 16)
        part = jnp.concatenate([shifted[c, at, :] for c in range(4)], axis=1)
        high = part.astype(BF16)
        low = (part - high.astype(F32)).astype(BF16)
        g_fine += dot_t(high[:, :384], one_fine[qx]) + dot_t(low[:, :384], one_fine[qx])
        g_coarse += dot_t(high[:, 384:], one_coarse[qx]) + dot_t(low[:, 384:], one_coarse[qx])
    for value, first, length in (
        (g_fine, TABLE_AT, FINE),
        (g_coarse, TABLE_AT + HEADS * FINE, COARSE),
    ):
        for h in range(HEADS):
            row, lane = divmod(first + h * length, 128)
            count = -(-(lane + length) // 128)
            line[...] = jnp.zeros_like(line)
            line[0:1, lane : lane + length] = value[h : h + 1, :length]
            for c in range(count):
                flat_a[row + c : row + c + 1, :] += line[0:1, c * 128 : (c + 1) * 128]
    for device, place in enumerate(places):
        a_at, b_at = flat.start(0, device), flat.start(1, device)
        out[place] = jnp.concatenate(
            [
                flat_a[a_at : a_at + flat.rows[0], :],
                flat_b[b_at : b_at + flat.rows[1], :],
            ],
            axis=0,
        ).astype(BF16)


def pack(flat, places, g_bias, g_qkv, g_vec1, g_proj, g_w1, g_w2t, g_vec2):
    fine, coarse, _ = bias_tables()
    vm = pl.BlockSpec(memory_space=pltpu.VMEM)
    return pl.pallas_call(
        functools.partial(pack_kernel, flat, places),
        out_shape=jax.ShapeDtypeStruct((flat.devices, flat.total, 128), BF16),
        in_specs=[vm] * 9,
        out_specs=vm,
        scratch_shapes=[
            pltpu.VMEM((flat.buffer[0], 128), F32),
            pltpu.VMEM((flat.buffer[1], 128), F32),
            pltpu.VMEM((16, 512), F32),
            pltpu.VMEM((4, 14 * 16, 128), F32),
            pltpu.VMEM((8, 512), F32),
        ],
        compiler_params=pltpu.CompilerParams(vmem_limit_bytes=VMEM_LIMIT),
        name="pack",
    )(
        jnp.asarray(fine),
        jnp.asarray(coarse),
        g_bias,
        g_qkv,
        g_vec1,
        g_proj,
        g_w1,
        g_w2t,
        g_vec2,
    )


def join_kernel(rows, slot_ref, in0, in1, in2, in3, out):
    for k, ref in enumerate((in0, in1, in2, in3)):
        at = pl.multiple_of(xor_slot(slot_ref[0], k) * rows, 16)
        out[pl.ds(at, rows), :] = ref[...].astype(out.dtype)


def join(slot, parts, dtype):
    rows = parts[0].shape[0]
    vm = pl.BlockSpec(memory_space=pltpu.VMEM)
    return pl.pallas_call(
        functools.partial(join_kernel, rows),
        out_shape=jax.ShapeDtypeStruct((4 * rows, D), dtype),
        in_specs=[pl.BlockSpec(memory_space=pltpu.SMEM)] + [vm] * 4,
        out_specs=vm,
        compiler_params=pltpu.CompilerParams(vmem_limit_bytes=VMEM_LIMIT),
        name="join",
    )(slot, *parts)


def adamw(master, first, second, grads):
    first_new = beta_one * first + (1.0 - beta_one) * grads
    second_new = beta_two * second + (1.0 - beta_two) * grads * grads
    first_hat = first_new / (1.0 - beta_one**STEP)
    second_hat = second_new / (1.0 - beta_two**STEP)
    master_new = master - learn_rate * (
        first_hat / (jnp.sqrt(second_hat) + adam_eps) + decay_rate * master
    )
    return (first_new, second_new, master_new)


def swap(value, k):
    pairs = [(s, s ^ k) for s in range(lax.axis_size("dp"))]
    return lax.ppermute(value, "dp", pairs)


def body(
    tokens, cotangent, attn_master, attn_first, attn_second, mlp_master, mlp_first, mlp_second
):
    n_dp, n_grp = lax.axis_size("dp"), lax.axis_size("grp")
    order = bit_order(n_dp, n_grp)
    places = place_list(order, n_dp, n_grp)
    flat = Flat(n_dp * n_grp, attn_master.shape[0], mlp_master.shape[0])
    slot = lax.rem(lax.axis_index("dp"), 4).astype(jnp.int32)
    slot_arr = slot.reshape(1)
    token_count = tokens.shape[1]
    rows = token_count // 4
    images = rows // SEQ

    def exchanged(array):
        return [
            swap(lax.dynamic_slice_in_dim(array, xor_slot(slot, k) * rows, rows, 0), k)
            for k in (1, 2, 3)
        ]

    tok, cot = tokens[0], cotangent[0]
    tok_in = exchanged(tok)
    cot_in = exchanged(cot)
    gathered = gather_params(flat, order, attn_master, mlp_master)
    wqkv, wproj, w1, w2, vecs, bias = prepare(flat, places, gathered)
    mixed, probs, qkv, x = attend(slot_arr, tok, tok_in, wqkv, vecs, bias, images)
    mlp_out = mlp(slot_arr, cot, cot_in, mixed, x, wproj, w1, w2, vecs)
    out_parts, (d_res, d_mixed, g_w1, g_w2t, g_proj, g_vec2) = mlp_out[:4], mlp_out[4:]
    out_parts = [out_parts[0]] + [swap(out_parts[k], k) for k in (1, 2, 3)]
    d_qkv, g_bias = attend_back(qkv, d_mixed, probs, images)
    back = input_back(slot_arr, d_qkv, x, d_res, wqkv, vecs)
    in_parts, (g_qkv, g_vec1) = back[:4], back[4:]
    in_parts = [in_parts[0]] + [swap(in_parts[k], k) for k in (1, 2, 3)]
    blocks = pack(flat, places, g_bias, g_qkv, g_vec1, g_proj, g_w1, g_w2t, g_vec2)
    grad_a, grad_b = sum_grads(flat, order, blocks)
    attn_new = adamw(attn_master, attn_first, attn_second, grad_a)
    mlp_new = adamw(mlp_master, mlp_first, mlp_second, grad_b)
    output = join(slot_arr, out_parts, BF16)
    input_grad = join(slot_arr, in_parts, F32)
    return (output[None], input_grad[None], *attn_new, *mlp_new)


def solution(mesh):
    flat_spec = P(("dp", "grp"))
    token_spec = P("dp", "grp", None)
    placed = (token_spec, token_spec) + (flat_spec,) * 6
    return jax.shard_map(
        body, mesh=mesh, in_specs=placed, out_specs=placed, check_vma=False
    )
```

time: 1470 us -> 434 us (0.30)
  local copies, waits for them, and re-layouts: 506 us -> 7.3 us
  Pallas kernels: 0 us -> 389 us
  waiting for transfers between devices: 403 us -> 20.6 us
  other arithmetic: 283 us -> 3.43 us
  matrix products: 243 us -> 0 us
    pallas_call x0 -> x10, Pallas kernels: none -> 389 us  [the longest x1 88 us: gather_params(): pl.pallas_call(functools.partial(gather_kernel, flat, order), out_shape=j...]
    dot_general x48 -> x0, matrix products: 243 us -> none  [the longest x4 43.8 us: times_transposed(): lax.dot_general(left, right, (((1,), (1,)), ((), ())), preferred_element_...]
    unnamed x8 -> x0, waiting for transfers between devices: 207 us -> none
    ppermute x8 -> x12, waiting for transfers between devices: 196 us -> 20.6 us  [swap(): return lax.ppermute(value, 'dp', pairs)]
    dynamic_update_slice x20 -> x0, local copies, waits for them, and re-layouts: 105 us -> none  [the longest x12 97.7 us: body(): lax.scan(backward_block, table_start, (query_blocks, kv_blocks, log_total...]
    reduce_sum x18 -> x0, other arithmetic: 91.1 us -> none  [the longest x4 33 us: backward_block(): jnp.sum(d_scores.astype(jnp.float32), axis=0)]
    slice x21 -> x0, local copies, waits for them, and re-layouts: 86.1 us -> none  [the longest x2 26.9 us: body(): d_kv_all[:, region * region:]]
    concatenate x8 -> x0, local copies, waits for them, and re-layouts: 56.2 us -> none  [the longest x2 19.8 us: pack(): joined = jnp.concatenate(flat_parts)]
  transfers between devices with their start and end apart: 12 -> 12, of which waited for: 9 -> 2; matrix products, arithmetic and copies ran while one was open for 21% -> 1% of each run, Pallas kernels for 0% -> 77%
where the time goes in v1:
time: 434 us; the launch traced here: 433 us
  Pallas kernels  389 us (90%)
  waiting for transfers between devices  20.6 us (5%)
  starting transfers between devices  11.8 us (3%)
  local copies, waits for them, and re-layouts  7.3 us (2%)
    pallas_call x1, Pallas kernels, gather_params(): pl.pallas_call(functools.partial(gather_kernel, flat, order), out_shape=j...  88 us
    pallas_call x1, Pallas kernels, attend(): pl.pallas_call(functools.partial(attend_kernel, rows), grid=(images,), ou...  83 us
    pallas_call x1, Pallas kernels, attend_back(): pl.pallas_call(functools.partial(attend_back_kernel, tokens // 4), grid=(...  63 us
    pallas_call x1, Pallas kernels, sum_grads(): pl.pallas_call(functools.partial(sum_kernel, flat, order), out_shape=[jax...  57.3 us
    pallas_call x1, Pallas kernels, mlp(): pl.pallas_call(functools.partial(mlp_kernel, rows), grid=(7,), out_shape=...  50.8 us
    ppermute x12, waiting for transfers between devices, swap(): return lax.ppermute(value, 'dp', pairs)  20.6 us
    pallas_call x1, Pallas kernels, input_back(): pl.pallas_call(functools.partial(input_kernel, rows), grid=(7,), out_shap...  14.7 us
    pallas_call x1, Pallas kernels, pack(): pl.pallas_call(functools.partial(pack_kernel, flat, places), out_shape=ja...  13.8 us
  transfers between devices with their start and end apart: 12, of which 2 were waited for; matrix products, arithmetic and copies ran while one was open for 1% of the time, Pallas kernels for 77%

profile of v1, /device:TPU:0, one launch (start us, length us, event | category | flops | bytes accessed | tf_op | source)
XLA Modules:
  0.0 433.1 jit_solution(13387820713674633284)
XLA Ops:
  0.6 0.0 copy-start
  0.7 1.8 dynamic-slice_bitcast_fusion
  2.5 0.0 copy-start.14
  2.5 0.0 copy-start.1
  2.5 2.4 collective-permute-start.5
  4.9 0.7 collective-permute-start.3
  5.6 0.0 collective-permute-start.4
  5.7 0.0 copy-done
  5.7 0.2 dynamic-slice_bitcast_fusion.3
  5.8 1.4 collective-permute-start.2
  7.2 0.8 collective-permute-start
  8.0 10.9 %collective-permute-done.5.in3 = bf16[784,384]{1,0:T(8,128)(2,1)S(1)} collective-permute-done((bf16[784,384]{1,0:T(8,128)(2,1)S(1)}, bf16[784,384]{1,0:T(8,128)(2,1)S(1)}, u32[]{:S(2)}, u32[]{:S(2)}) %collective-permute-start.5) | collective-permute-done | bytes 602144 | tf_op jit(solution)/shard_map/ppermute | solution.py:1018
  18.9 2.5 collective-permute-start.1
  21.4 0.0 copy-done.14
  21.4 0.6 pad_bitcast_fusion.1.a_ref
  22.0 0.0 copy-done.1
  22.0 0.7 pad_bitcast_fusion.b_ref
  22.7 88.0 %gather_params.1.parts_ref = bf16[32,448,128]{2,1,0:T(8,128)(2,1)} custom-call(f32[152,128]{1,0:T(8,128)} %pad_bitcast_fusion.1.a_ref, f32[296,128]{1,0:T(8,128)} %pad_bitcast_fusion.b_ref), custom_call_target="tpu_custom_call" | custom-call | tf_op jit(solution)/shard_map/gather_params/pallas_call | solution.py:193
  110.7 11.0 %prepare.1 = (bf16[384,1152]{1,0:T(8,128)(2,1)}, bf16[384,384]{1,0:T(8,128)(2,1)}, bf16[384,1536]{1,0:T(8,128)(2,1)}, bf16[1536,384]{1,0:T(8,128)(2,1)}, f32[16,...) custom-call(bf16[32,448,128]{2,1,0:T(8,128)(2,1)} %gather_params.1.parts_ref, bf16[14,384,384]{2,1,0:T(8,128)(2,1)} %constant.94.clone.one_fine, ...), custom_call_target="tpu_custom_call" | custom-call | tf_op jit(solution)/shard_map/prepare/pallas_call | solution.py:374
  121.7 0.0 copy-done.4
  121.7 0.0 collective-permute-done.3.in1
  121.7 0.0 copy-start.5
  121.7 0.0 collective-permute-done.4.in2
  121.7 0.0 copy-start.6
  121.7 0.8 copy-done.5
  122.5 0.2 copy-done.6
  122.7 83.0 %attend.1 = (bf16[3136,384]{1,0:T(8,128)(2,1)}, bf16[16,12,256,256]{3,2,1,0:T(8,128)(2,1)}, bf16[3136,1152]{1,0:T(8,128)(2,1)}, bf16[3136,384]{1,0:T(8,128)(2,1)}) custom-call(s32[1]{0:T(128)} %bitcast.slot_ref, bf16[3136,384]{1,0:T(8,128)(2,1)} %bitcast.23, bf16[784,384]{1,0:T(8,128)(2,1)} %copy-done.5, bf16[784,384]{1,0:T(8,128)(2,1)} %copy-done.6, ...), custom_call_target="tpu_custom_call" | custom-call | tf_op jit(solution)/shard_map/attend/pallas_call | solution.py:559
  205.7 0.0 collective-permute-done.2.in3
  205.7 0.0 copy-start.11
  205.8 0.0 collective-permute-done.in1
  205.8 0.0 copy-start.12
  205.8 0.0 collective-permute-done.1.in2
  205.8 0.0 copy-start.13
  205.8 0.8 copy-done.11
  206.6 0.2 copy-done.12
  206.7 0.2 copy-done.13
  207.0 50.8 %mlp.1 = (bf16[784,384]{1,0:T(8,128)(2,1)}, bf16[784,384]{1,0:T(8,128)(2,1)}, bf16[784,384]{1,0:T(8,128)(2,1)}, bf16[784,384]{1,0:T(8,128)(2,1)}, f32[3136,384]{...) custom-call(s32[1]{0:T(128)} %bitcast.slot_ref, ...), custom_call_target="tpu_custom_call" | custom-call | tf_op jit(solution)/shard_map/mlp/pallas_call | solution.py:690
  257.8 0.4 collective-permute-start.6
  258.2 1.5 collective-permute-start.7
  259.8 0.0 collective-permute-start.8
  259.8 63.0 %attend_back.1 = (bf16[3136,1152]{1,0:T(8,128)(2,1)}, f32[12,2,192,128]{3,2,1,0:T(8,128)}) custom-call(bf16[3136,1152]{1,0:T(8,128)(2,1)} %get-tuple-element.50.qkv, bf16[3136,384]{1,0:T(8,128)(2,1)} %get-tuple-element.51.d_mixed, bf16[16,12,256,256]{3,2,1,0:T(8,128)(2,1)} %get-tuple-element.52.probs, bf16[16,256,256]{2,1,0:T(8,128)(2,1)} %constant.97.clone.keys_tab, ...), custom_call_target="tpu_custom_call" | custom-call | tf_op jit(solution)/shard_map/attend_back/pallas_call | solution.py:780
  322.8 14.7 %input_back.1 = (bf16[784,384]{1,0:T(8,128)(2,1)}, bf16[784,384]{1,0:T(8,128)(2,1)}, bf16[784,384]{1,0:T(8,128)(2,1)}, bf16[784,384]{1,0:T(8,128)(2,1)}, f32[384,1152]{1,0:T(8,128)}, /*index=5*/f32[8,1152]{1,0:T(8,128)}) custom-call(s32[1]{0:T(128)} %bitcast.slot_ref, bf16[3136,1152]{1,0:T(8,128)(2,1)} %get-tuple-element.53.d_qkv_ref, ...), custom_call_target="tpu_custom_call" | custom-call | tf_op jit(solution)/shard_map/input_back/pallas_call | solution.py:853
  337.5 0.4 collective-permute-start.9
  338.0 1.5 collective-permute-start.10
  339.5 13.8 %pack.1.x_ref = bf16[32,448,128]{2,1,0:T(8,128)(2,1)} custom-call(bf16[14,384,384]{2,1,0:T(8,128)(2,1)} %constant.94.clone.one_fine, bf16[14,256,128]{2,1,0:T(8,128)(2,1)} %constant.95.clone.one_coarse, f32[12,2,192,128]{3,2,1,0:T(8,128)} %get-tuple-element.59.g_bias, f32[384,1152]{1,0:T(8,128)} %get-tuple-element.60.g_qkv, ...), custom_call_target="tpu_custom_call" | custom-call | tf_op jit(solution)/shard_map/pack/pallas_call | solution.py:959
  353.3 0.0 copy-start.17
  353.3 0.0 copy-start.18
  353.3 57.3 %sum_grads.1 = (f32[152,128]{1,0:T(8,128)}, f32[296,128]{1,0:T(8,128)}) custom-call(bf16[32,448,128]{2,1,0:T(8,128)(2,1)} %pack.1.x_ref), custom_call_target="tpu_custom_call" | custom-call | tf_op jit(solution)/shard_map/sum_grads/pallas_call | solution.py:263
  410.6 0.0 copy-done.15
  410.7 1.7 multiply_subtract_fusion
  412.4 0.0 collective-permute-done.6.in1
  412.4 0.0 copy-done.19
  412.4 0.1 collective-permute-start.11
  412.5 1.7 multiply_subtract_fusion.1
  414.2 0.0 collective-permute-done.7.in2
  414.2 0.0 collective-permute-done.8.in3
  414.2 0.8 copy-done.9
  415.0 0.2 copy-done.10
  415.2 3.3 join.2
  418.5 0.0 collective-permute-done.9.in1
  418.5 0.0 collective-permute-done.10.in2
  418.5 9.6 %collective-permute-done.11.in3 = bf16[784,384]{1,0:T(8,128)(2,1)S(1)} collective-permute-done((bf16[784,384]{1,0:T(8,128)(2,1)S(1)}, bf16[784,384]{1,0:T(8,128)(2,1)S(1)}, u32[]{:S(2)}, u32[]{:S(2)}) %collective-permute-start.11) | collective-permute-done | bytes 602144 | tf_op jit(solution)/shard_map/ppermute | solution.py:1018
  428.1 0.8 copy-done.7
  429.0 4.1 join.3
  (16 shorter events, 0.0 us)
Async XLA Ops:
  0.6 5.0 %copy-start = (bf16[1,3136,384]{2,1,0:T(8,128)(2,1)S(1)}, bf16[1,3136,384]{2,1,0:T(8,128)(2,1)}, u32[]{:S(2)}) copy-start(bf16[1,3136,384]{2,1,0:T(8,128)(2,1)} %param.16) | copy-start | bytes 7225348
  2.5 18.9 %copy-start.14 = (f32[18696]{0:T(1024)S(1)}, f32[18696]{0:T(1024)}, u32[]{:S(2)}) copy-start(f32[18696]{0:T(1024)} %param.17) | copy-start | bytes 224356
  2.5 19.5 %copy-start.1 = (f32[36952]{0:T(1024)S(1)}, f32[36952]{0:T(1024)}, u32[]{:S(2)}) copy-start(f32[36952]{0:T(1024)} %param.20) | copy-start | bytes 443428
  2.5 16.4 %collective-permute-start.5 = (bf16[784,384]{1,0:T(8,128)(2,1)S(1)}, bf16[784,384]{1,0:T(8,128)(2,1)S(1)}, u32[]{:S(2)}, u32[]{:S(2)}) collective-permute-start(bf16[784,384]{1,0:T(8,128)(2,1)S(1)} %get-tuple-element.74), channel_id=1, source_target_pairs={{0,12},{4,8},{8,4},{12,0},{16,28},{20,24},{24,20},{28,16},{1,13},{... | collective-permute-start | bytes 1806344 | tf_op jit(solution)/shard_map/ppermute | solution.py:1018
  4.9 116.7 %collective-permute-start.3 = (bf16[784,384]{1,0:T(8,128)(2,1)S(1)}, bf16[784,384]{1,0:T(8,128)(2,1)S(1)}, u32[]{:S(2)}, u32[]{:S(2)}) collective-permute-start(bf16[784,384]{1,0:T(8,128)(2,1)S(1)} %get-tuple-element.75), channel_id=1, source_target_pairs={{0,4},{4,0},{8,12},{12,8},{16,20},{20,16},{24,28},{28,24},{1,5},{5... | collective-permute-start | bytes 1806344 | tf_op jit(solution)/shard_map/ppermute | solution.py:1018
  5.6 116.1 %collective-permute-start.4 = (bf16[784,384]{1,0:T(8,128)(2,1)S(1)}, bf16[784,384]{1,0:T(8,128)(2,1)S(1)}, u32[]{:S(2)}, u32[]{:S(2)}) collective-permute-start(bf16[784,384]{1,0:T(8,128)(2,1)S(1)} %get-tuple-element.76), channel_id=1, source_target_pairs={{0,8},{4,12},{8,0},{12,4},{16,24},{20,28},{24,16},{28,20},{1,9},{5... | collective-permute-start | bytes 1806344 | tf_op jit(solution)/shard_map/ppermute | solution.py:1018
  5.8 199.9 %collective-permute-start.2 = (bf16[784,384]{1,0:T(8,128)(2,1)S(1)}, bf16[784,384]{1,0:T(8,128)(2,1)S(1)}, u32[]{:S(2)}, u32[]{:S(2)}) collective-permute-start(bf16[784,384]{1,0:T(8,128)(2,1)S(1)} %get-tuple-element.77), channel_id=1, source_target_pairs={{0,12},{4,8},{8,4},{12,0},{16,28},{20,24},{24,20},{28,16},{1,13},{... | collective-permute-start | bytes 1806344 | tf_op jit(solution)/shard_map/ppermute | solution.py:1018
  7.2 198.5 %collective-permute-start = (bf16[784,384]{1,0:T(8,128)(2,1)S(1)}, bf16[784,384]{1,0:T(8,128)(2,1)S(1)}, u32[]{:S(2)}, u32[]{:S(2)}) collective-permute-start(bf16[784,384]{1,0:T(8,128)(2,1)S(1)} %get-tuple-element.78), channel_id=1, source_target_pairs={{0,4},{4,0},{8,12},{12,8},{16,20},{20,16},{24,28},{28,24},{1,5},{5... | collective-permute-start | bytes 1806344 | tf_op jit(solution)/shard_map/ppermute | solution.py:1018
  18.9 102.7 %copy-start.4 = (bf16[784,384]{1,0:T(8,128)(2,1)}, bf16[784,384]{1,0:T(8,128)(2,1)S(1)}, u32[]{:S(2)}) copy-start(bf16[784,384]{1,0:T(8,128)(2,1)S(1)} %collective-permute-done.5.in3) | copy-start | bytes 1806340
  18.9 186.9 %collective-permute-start.1 = (bf16[784,384]{1,0:T(8,128)(2,1)S(1)}, bf16[784,384]{1,0:T(8,128)(2,1)S(1)}, u32[]{:S(2)}, u32[]{:S(2)}) collective-permute-start(bf16[784,384]{1,0:T(8,128)(2,1)S(1)} %get-tuple-element.79), channel_id=1, source_target_pairs={{0,8},{4,12},{8,0},{12,4},{16,24},{20,28},{24,16},{28,20},{1,9},{5... | collective-permute-start | bytes 1806344 | tf_op jit(solution)/shard_map/ppermute | solution.py:1018
  121.7 0.8 copy-start.5
  121.7 1.0 copy-start.6
  205.7 0.8 copy-start.11
  205.8 1.0 copy-start.12
  205.8 1.2 copy-start.13
  257.8 154.6 %collective-permute-start.6 = (bf16[784,384]{1,0:T(8,128)(2,1)}, bf16[784,384]{1,0:T(8,128)(2,1)S(1)}, u32[]{:S(2)}, u32[]{:S(2)}) collective-permute-start(bf16[784,384]{1,0:T(8,128)(2,1)} %get-tuple-element.47), channel_id=1, source_target_pairs={{0,4},{4,0},{8,12},{12,8},{16,20},{20,16},{24,28},{28,24},{1,5},{5... | collective-permute-start | bytes 1806344 | tf_op jit(solution)/shard_map/ppermute | solution.py:1018
  258.2 156.0 %collective-permute-start.7 = (bf16[784,384]{1,0:T(8,128)(2,1)}, bf16[784,384]{1,0:T(8,128)(2,1)S(1)}, u32[]{:S(2)}, u32[]{:S(2)}) collective-permute-start(bf16[784,384]{1,0:T(8,128)(2,1)} %get-tuple-element.48), channel_id=1, source_target_pairs={{0,8},{4,12},{8,0},{12,4},{16,24},{20,28},{24,16},{28,20},{1,9},{5... | collective-permute-start | bytes 1806344 | tf_op jit(solution)/shard_map/ppermute | solution.py:1018
  259.8 154.4 %collective-permute-start.8 = (bf16[784,384]{1,0:T(8,128)(2,1)}, bf16[784,384]{1,0:T(8,128)(2,1)S(1)}, u32[]{:S(2)}, u32[]{:S(2)}) collective-permute-start(bf16[784,384]{1,0:T(8,128)(2,1)} %get-tuple-element.49), channel_id=1, source_target_pairs={{0,12},{4,8},{8,4},{12,0},{16,28},{20,24},{24,20},{28,16},{1,13},{... | collective-permute-start | bytes 1806344 | tf_op jit(solution)/shard_map/ppermute | solution.py:1018
  337.5 81.0 %collective-permute-start.9 = (bf16[784,384]{1,0:T(8,128)(2,1)}, bf16[784,384]{1,0:T(8,128)(2,1)S(1)}, u32[]{:S(2)}, u32[]{:S(2)}) collective-permute-start(bf16[784,384]{1,0:T(8,128)(2,1)} %get-tuple-element.56), channel_id=1, source_target_pairs={{0,4},{4,0},{8,12},{12,8},{16,20},{20,16},{24,28},{28,24},{1,5},{5... | collective-permute-start | bytes 1806344 | tf_op jit(solution)/shard_map/ppermute | solution.py:1018
  338.0 80.5 %collective-permute-start.10 = (bf16[784,384]{1,0:T(8,128)(2,1)}, bf16[784,384]{1,0:T(8,128)(2,1)S(1)}, u32[]{:S(2)}, u32[]{:S(2)}) collective-permute-start(bf16[784,384]{1,0:T(8,128)(2,1)} %get-tuple-element.57), channel_id=1, source_target_pairs={{0,8},{4,12},{8,0},{12,4},{16,24},{20,28},{24,16},{28,20},{1,9},{5... | collective-permute-start | bytes 1806344 | tf_op jit(solution)/shard_map/ppermute | solution.py:1018
  353.3 57.4 %copy-start.15 = (f32[36952]{0:T(1024)S(1)}, f32[36952]{0:T(1024)}, u32[]{:S(2)}) copy-start(f32[36952]{0:T(1024)} %param.22) | copy-start | bytes 443428
  353.3 57.4 %copy-start.16 = (f32[36952]{0:T(1024)S(1)}, f32[36952]{0:T(1024)}, u32[]{:S(2)}) copy-start(f32[36952]{0:T(1024)} %param.21) | copy-start | bytes 443428
  353.3 59.1 %copy-start.19 = (bf16[784,384]{1,0:T(8,128)(2,1)S(1)}, bf16[784,384]{1,0:T(8,128)(2,1)}, u32[]{:S(2)}) copy-start(bf16[784,384]{1,0:T(8,128)(2,1)} %get-tuple-element.58) | copy-start | bytes 1806340
  353.3 59.2 %copy-start.17 = (f32[18696]{0:T(1024)S(1)}, f32[18696]{0:T(1024)}, u32[]{:S(2)}) copy-start(f32[18696]{0:T(1024)} %param.19) | copy-start | bytes 224356
  353.3 59.2 %copy-start.18 = (f32[18696]{0:T(1024)S(1)}, f32[18696]{0:T(1024)}, u32[]{:S(2)}) copy-start(f32[18696]{0:T(1024)} %param.18) | copy-start | bytes 224356
  412.4 1.8 copy-start.8
  412.4 15.7 %collective-permute-start.11 = (bf16[784,384]{1,0:T(8,128)(2,1)S(1)}, bf16[784,384]{1,0:T(8,128)(2,1)S(1)}, u32[]{:S(2)}, u32[]{:S(2)}) collective-permute-start(bf16[784,384]{1,0:T(8,128)(2,1)S(1)} %copy-done.19), channel_id=1, source_target_pairs={{0,12},{4,8},{8,4},{12,0},{16,28},{20,24},{24,20},{28,16},{1,13},{... | collective-permute-start | bytes 1806344 | tf_op jit(solution)/shard_map/ppermute | solution.py:1018
  414.2 0.8 copy-start.9
  414.2 1.0 copy-start.10
  418.5 9.7 %copy-start.2 = (bf16[784,384]{1,0:T(8,128)(2,1)}, bf16[784,384]{1,0:T(8,128)(2,1)S(1)}, u32[]{:S(2)}) copy-start(bf16[784,384]{1,0:T(8,128)(2,1)S(1)} %collective-permute-done.9.in1) | copy-start | bytes 1806340
  418.5 9.7 %copy-start.3 = (bf16[784,384]{1,0:T(8,128)(2,1)}, bf16[784,384]{1,0:T(8,128)(2,1)S(1)}, u32[]{:S(2)}) copy-start(bf16[784,384]{1,0:T(8,128)(2,1)S(1)} %collective-permute-done.10.in2) | copy-start | bytes 1806340
  428.1 0.8 copy-start.7

commit v2 on v1

--- a/solution.py
+++ b/solution.py
@@ -139,13 +139,15 @@
     return (dp, grp + (1 - 2 * ((grp // stride) % 2)) * stride)
 
 
-def greet(order, dp, grp):
+def greet(partners):
     barrier = pltpu.get_barrier_semaphore()
-    for axis, stride in order:
-        pl.semaphore_signal(
-            barrier, inc=1, device_id=partner_of(axis, stride, dp, grp), device_id_type=MESH
-        )
-    pl.semaphore_wait(barrier, len(order))
+    for partner in partners:
+        pl.semaphore_signal(barrier, inc=1, device_id=partner, device_id_type=MESH)
+    pl.semaphore_wait(barrier, len(partners))
+
+
+def cube_partners(order, dp, grp):
+    return [partner_of(axis, stride, dp, grp) for axis, stride in order]
 
 
 def shift_lanes(values, amount, up):
@@ -157,7 +159,54 @@
     return jnp.where(lane < 128 - amount, turned, pltpu.roll(turned, values.shape[0] - 1, 0))
 
 
-def gather_kernel(flat, order, a_ref, b_ref, out_ref, own, own_sem, send_sems, recv_sems):
+def window_partner(dp, grp, k):
+    low, high = dp % 2, dp // 2 % 2
+    to = dp
+    if k % 2:
+        to = to + 1 - 2 * low
+    if k // 2:
+        to = to + 2 * (1 - 2 * high)
+    return (to, grp)
+
+
+def exchange_copies(source, target, dp, grp, own_sem, send_sems, recv_sems):
+    rows = source.shape[0] // 4
+    slot = dp % 4
+    mine = pl.ds(pl.multiple_of(slot * rows, 16), rows)
+    own = pltpu.make_async_copy(source.at[mine], target.at[mine], own_sem)
+    sends = []
+    for k in (3, 2, 1):
+        to, _ = window_partner(dp, grp, k)
+        theirs = pl.ds(pl.multiple_of(to % 4 * rows, 16), rows)
+        sends.append(
+            pltpu.make_async_remote_copy(
+                src_ref=source.at[theirs],
+                dst_ref=target.at[mine],
+                send_sem=send_sems.at[k - 1],
+                recv_sem=recv_sems.at[k - 1],
+                device_id=(to, grp),
+                device_id_type=MESH,
+            )
+        )
+    return [own] + sends
+
+
+def gather_kernel(
+    flat,
+    order,
+    a_ref,
+    b_ref,
+    tok_ref,
+    out_ref,
+    x_ref,
+    own,
+    own_sem,
+    send_sems,
+    recv_sems,
+    x_sem,
+    x_send,
+    x_recv,
+):
     dp, grp = lax.axis_index("dp"), lax.axis_index("grp")
     device = dp * lax.axis_size("grp") + grp
     place = place_of(order, dp, grp)
@@ -168,8 +217,9 @@
     own[...] = jnp.concatenate(parts, axis=0).astype(BF16)
     copy = pltpu.make_async_copy(own, out_ref.at[place], own_sem)
     copy.start()
-    greet(order, dp, grp)
+    greet(cube_partners(order, dp, grp) + [window_partner(dp, grp, 3)])
     copy.wait()
+    exchange = exchange_copies(tok_ref, x_ref, dp, grp, x_sem, x_send, x_recv)
     for k, (axis, stride) in enumerate(order):
         held = out_ref.at[pl.ds(place // 2**k * 2**k, 2**k)]
         send = pltpu.make_async_remote_copy(
@@ -181,10 +231,15 @@
             device_id_type=MESH,
         )
         send.start()
+        if k == 0:
+            for c in exchange:
+                c.start()
         send.wait()
-
-
-def gather_params(flat, order, master_a, master_b):
+    for c in exchange:
+        c.wait()
+
+
+def gather_params(flat, order, master_a, master_b, tok):
     padded = [
         jnp.pad(m, (0, flat.rows[w] * 128 - m.shape[0])).reshape(flat.rows[w], 128)
         for w, m in enumerate((master_a, master_b))
@@ -192,20 +247,27 @@
     stages = len(order)
     return pl.pallas_call(
         functools.partial(gather_kernel, flat, order),
-        out_shape=jax.ShapeDtypeStruct((flat.devices, flat.total, 128), BF16),
-        in_specs=[pl.BlockSpec(memory_space=pltpu.VMEM)] * 2,
-        out_specs=pl.BlockSpec(memory_space=pl.ANY),
+        out_shape=[
+            jax.ShapeDtypeStruct((flat.devices, flat.total, 128), BF16),
+            jax.ShapeDtypeStruct(tok.shape, BF16),
+        ],
+        in_specs=[pl.BlockSpec(memory_space=pltpu.VMEM)] * 2
+        + [pl.BlockSpec(memory_space=pl.ANY)],
+        out_specs=[pl.BlockSpec(memory_space=pl.ANY)] * 2,
         scratch_shapes=[
             pltpu.VMEM((flat.total, 128), BF16),
             pltpu.SemaphoreType.DMA,
             pltpu.SemaphoreType.DMA((stages,)),
             pltpu.SemaphoreType.DMA((stages,)),
+            pltpu.SemaphoreType.DMA,
+            pltpu.SemaphoreType.DMA((3,)),
+            pltpu.SemaphoreType.DMA((3,)),
         ],
         compiler_params=pltpu.CompilerParams(
             collective_id=0, has_side_effects=True, vmem_limit_bytes=VMEM_LIMIT
         ),
         name="gather_params",
-    )(*padded)
+    )(*padded, tok)
 
 
 def sum_kernel(
@@ -214,7 +276,7 @@
     dp, grp = lax.axis_index("dp"), lax.axis_index("grp")
     device = dp * lax.axis_size("grp") + grp
     place = place_of(order, dp, grp)
-    greet(order, dp, grp)
+    greet(cube_partners(order, dp, grp))
     stages = len(order)
     for k in reversed(range(stages)):
         axis, stride = order[k]
@@ -463,11 +525,8 @@
 
 def attend_kernel(
     rows,
-    slot_ref,
-    tok_ref,
-    in1,
-    in2,
-    in3,
+    x_buf,
+    cot_ref,
     wqkv,
     vecs,
     bias,
@@ -477,25 +536,22 @@
     mixed,
     probs,
     qkv,
-    x_out,
-    x_buf,
+    cot_out,
     normed,
     mixed_t,
-    sems,
-    out_sem,
+    own_sem,
+    send_sems,
+    recv_sems,
 ):
     i = pl.program_id(0)
-    slot = slot_ref[0]
+    dp, grp = lax.axis_index("dp"), lax.axis_index("grp")
+    exchange = exchange_copies(cot_ref, cot_out, dp, grp, own_sem, send_sems, recv_sems)
 
     @pl.when(i == 0)
     def _():
-        own = tok_ref.at[pl.ds(pl.multiple_of(slot * rows, 16), rows)]
-        copies = split_copies(slot, (own, in1, in2, in3), x_buf, sems, rows, False)
-        for c in copies:
+        greet([window_partner(dp, grp, k) for k in (1, 2, 3)])
+        for c in exchange:
             c.start()
-        for c in copies:
-            c.wait()
-        pltpu.make_async_copy(x_buf, x_out, out_sem).start()
 
         def project(w, carry):
             base = pl.multiple_of(w * rows, 16)
@@ -545,11 +601,12 @@
 
     @pl.when(i == pl.num_programs(0) - 1)
     def _():
-        pltpu.make_async_copy(x_buf, x_out, out_sem).wait()
-
-
-def attend(slot, tok, arrived, wqkv, vecs, bias, images):
-    tokens = tok.shape[0]
+        for c in exchange:
+            c.wait()
+
+
+def attend(x, cot, wqkv, vecs, bias, images):
+    tokens = x.shape[0]
     rows = tokens // 4
     keys_tab, query_tab, _, query_back = gather_tables(images)
     vm = pl.BlockSpec(memory_space=pltpu.VMEM)
@@ -565,7 +622,7 @@
             jax.ShapeDtypeStruct((tokens, 3 * D), BF16),
             jax.ShapeDtypeStruct((tokens, D), BF16),
         ],
-        in_specs=[pl.BlockSpec(memory_space=pltpu.SMEM)] + [hbm] * 4 + [vm] * 3 + [table] * 3,
+        in_specs=[vm, hbm] + [vm] * 3 + [table] * 3,
         out_specs=[
             whole(D),
             pl.BlockSpec((1, HEADS, 256, 256), lambda i: (i, 0, 0, 0)),
@@ -573,15 +630,17 @@
             hbm,
         ],
         scratch_shapes=[
-            pltpu.VMEM((tokens, D), BF16),
             pltpu.VMEM((rows, D), BF16),
             pltpu.VMEM((D, 256), BF16),
-            pltpu.SemaphoreType.DMA((4,)),
             pltpu.SemaphoreType.DMA,
-        ],
-        compiler_params=pltpu.CompilerParams(vmem_limit_bytes=VMEM_LIMIT),
+            pltpu.SemaphoreType.DMA((3,)),
+            pltpu.SemaphoreType.DMA((3,)),
+        ],
+        compiler_params=pltpu.CompilerParams(
+            collective_id=2, has_side_effects=True, vmem_limit_bytes=VMEM_LIMIT
+        ),
         name="attend",
-    )(slot, tok, *arrived, wqkv, vecs, bias, keys_tab, query_tab, query_back)
+    )(x, cot, wqkv, vecs, bias, keys_tab, query_tab, query_back)
 
 
 GELU_A = float(np.sqrt(2.0 / np.pi))
@@ -592,9 +651,6 @@
     rows,
     slot_ref,
     cot_ref,
-    in1,
-    in2,
-    in3,
     mixed_ref,
     x_ref,
     wproj,
@@ -611,7 +667,6 @@
     g_w2t,
     g_proj,
     g_vec,
-    g_buf,
     o_buf,
     sems,
 ):
@@ -621,12 +676,6 @@
 
     @pl.when(i == 0)
     def _():
-        own = cot_ref.at[pl.ds(pl.multiple_of(slot * rows, 16), rows)]
-        copies = split_copies(slot, (own, in1, in2, in3), g_buf, sems, rows, False)
-        for c in copies:
-            c.start()
-        for c in copies:
-            c.wait()
         g_w1[...] = jnp.zeros_like(g_w1)
         g_w2t[...] = jnp.zeros_like(g_w2t)
         g_proj[...] = jnp.zeros_like(g_proj)
@@ -638,7 +687,7 @@
     xhat, scale = norm_parts(res)
     gain = vecs[5:6, :D]
     normed = (xhat * gain + vecs[6:7, :D]).astype(BF16)
-    grad = g_buf[here, :]
+    grad = cot_ref[...]
     grad_t = grad.T
     normed_t = normed.T
     out = res + vecs[7:8, :D]
@@ -679,7 +728,7 @@
             c.wait()
 
 
-def mlp(slot, cot, arrived, mixed, x, wproj, w1, w2, vecs):
+def mlp(slot, cot, mixed, x, wproj, w1, w2, vecs):
     tokens = x.shape[0]
     rows = tokens // 4
     chunk = tokens // 7
@@ -699,17 +748,16 @@
             jax.ShapeDtypeStruct((D, D), F32),
             jax.ShapeDtypeStruct((8, FF), F32),
         ],
-        in_specs=[pl.BlockSpec(memory_space=pltpu.SMEM)] + [hbm] * 4 + [tile] * 2 + [vm] * 4,
+        in_specs=[pl.BlockSpec(memory_space=pltpu.SMEM)] + [tile] * 3 + [vm] * 4,
         out_specs=[hbm] * 4
         + [tile, tile, fixed(D, FF), fixed(D, FF), fixed(D, D), fixed(8, FF)],
         scratch_shapes=[
             pltpu.VMEM((tokens, D), BF16),
-            pltpu.VMEM((tokens, D), BF16),
             pltpu.SemaphoreType.DMA((4,)),
         ],
         compiler_params=pltpu.CompilerParams(vmem_limit_bytes=VMEM_LIMIT),
         name="mlp",
-    )(slot, cot, *arrived, mixed, x, wproj, w1, w2, vecs)
+    )(slot, cot, mixed, x, wproj, w1, w2, vecs)
 
 
 def attend_back_kernel(
@@ -1031,19 +1079,10 @@
     rows = token_count // 4
     images = rows // SEQ
 
-    def exchanged(array):
-        return [
-            swap(lax.dynamic_slice_in_dim(array, xor_slot(slot, k) * rows, rows, 0), k)
-            for k in (1, 2, 3)
-        ]
-
-    tok, cot = tokens[0], cotangent[0]
-    tok_in = exchanged(tok)
-    cot_in = exchanged(cot)
-    gathered = gather_params(flat, order, attn_master, mlp_master)
+    gathered, x = gather_params(flat, order, attn_master, mlp_master, tokens[0])
     wqkv, wproj, w1, w2, vecs, bias = prepare(flat, places, gathered)
-    mixed, probs, qkv, x = attend(slot_arr, tok, tok_in, wqkv, vecs, bias, images)
-    mlp_out = mlp(slot_arr, cot, cot_in, mixed, x, wproj, w1, w2, vecs)
+    mixed, probs, qkv, cot = attend(x, cotangent[0], wqkv, vecs, bias, images)
+    mlp_out = mlp(slot_arr, cot, mixed, x, wproj, w1, w2, vecs)
     out_parts, (d_res, d_mixed, g_w1, g_w2t, g_proj, g_vec2) = mlp_out[:4], mlp_out[4:]
     out_parts = [out_parts[0]] + [swap(out_parts[k], k) for k in (1, 2, 3)]
     d_qkv, g_bias = attend_back(qkv, d_mixed, probs, images)

time: 434 us -> 381 us (0.88)
  Pallas kernels: 389 us -> 358 us
  waiting for transfers between devices: 20.6 us -> 9.79 us
  starting transfers between devices: 11.8 us -> 2.83 us
    pallas_call x1, Pallas kernels: 88 us -> 56.7 us  [gather_params(): pl.pallas_call(functools.partial(gather_kernel, flat, order), out_shape=[...]
    ppermute x12 -> x6, waiting for transfers between devices: 20.6 us -> 9.79 us  [swap(): return lax.ppermute(value, 'dp', pairs)]
    ppermute x12 -> x6, starting transfers between devices: 11.8 us -> 2.83 us  [swap(): return lax.ppermute(value, 'dp', pairs)]
  transfers between devices with their start and end apart: 12 -> 6, of which waited for: 2 -> 1; matrix products, arithmetic and copies ran while one was open for 1% -> 1% of each run, Pallas kernels for 77% -> 40%
where the time goes in v2:
time: 381 us; the launch traced here: 380 us
  Pallas kernels  358 us (94%)
  waiting for transfers between devices  9.79 us (3%)
  local copies, waits for them, and re-layouts  4.99 us (1%)
    pallas_call x1, Pallas kernels, attend(): pl.pallas_call(functools.partial(attend_kernel, rows), grid=(images,), ou...  85.2 us
    pallas_call x1, Pallas kernels, attend_back(): pl.pallas_call(functools.partial(attend_back_kernel, tokens // 4), grid=(...  62.7 us
    pallas_call x1, Pallas kernels, sum_grads(): pl.pallas_call(functools.partial(sum_kernel, flat, order), out_shape=[jax...  57.5 us
    pallas_call x1, Pallas kernels, gather_params(): pl.pallas_call(functools.partial(gather_kernel, flat, order), out_shape=[...  56.7 us
    pallas_call x1, Pallas kernels, mlp(): pl.pallas_call(functools.partial(mlp_kernel, rows), grid=(7,), out_shape=...  49.4 us
    pallas_call x1, Pallas kernels, input_back(): pl.pallas_call(functools.partial(input_kernel, rows), grid=(7,), out_shap...  14.7 us
    pallas_call x1, Pallas kernels, pack(): pl.pallas_call(functools.partial(pack_kernel, flat, places), out_shape=ja...  13.8 us
    pallas_call x1, Pallas kernels, prepare(): pl.pallas_call(functools.partial(prep_kernel, flat, places), out_shape=[j...  11 us
  transfers between devices with their start and end apart: 6, of which 1 were waited for; matrix products, arithmetic and copies ran while one was open for 1% of the time, Pallas kernels for 40%

profile of v2, /device:TPU:0, one launch (start us, length us, event | category | flops | bytes accessed | tf_op | source)
XLA Modules:
  0.0 380.2 jit_solution(14833308987385963487)
XLA Ops:
  0.6 1.5 pad_bitcast_fusion.1.a_ref
  2.2 1.6 pad_bitcast_fusion.b_ref
  3.7 56.7 %gather_params.1 = (bf16[32,448,128]{2,1,0:T(8,128)(2,1)}, bf16[3136,384]{1,0:T(8,128)(2,1)}) custom-call(f32[152,128]{1,0:T(8,128)} %pad_bitcast_fusion.1.a_ref, f32[296,128]{1,0:T(8,128)} %pad_bitcast_fusion.b_ref, bf16[3136,384]{1,0:T(8,128)(2,1)} %bitcast.14), custom_call_target="tpu_custom_call" | custom-call | tf_op jit(solution)/shard_map/gather_params/pallas_call | solution.py:248
  60.5 11.0 %prepare.1 = (bf16[384,1152]{1,0:T(8,128)(2,1)}, bf16[384,384]{1,0:T(8,128)(2,1)}, bf16[384,1536]{1,0:T(8,128)(2,1)}, bf16[1536,384]{1,0:T(8,128)(2,1)}, f32[16,...) custom-call(bf16[32,448,128]{2,1,0:T(8,128)(2,1)} %get-tuple-element.41.parts_ref, ...), custom_call_target="tpu_custom_call" | custom-call | tf_op jit(solution)/shard_map/prepare/pallas_call | solution.py:436
  71.4 85.2 %attend.1 = (bf16[3136,384]{1,0:T(8,128)(2,1)}, bf16[16,12,256,256]{3,2,1,0:T(8,128)(2,1)}, bf16[3136,1152]{1,0:T(8,128)(2,1)}, bf16[3136,384]{1,0:T(8,128)(2,1)}) custom-call(bf16[3136,384]{1,0:T(8,128)(2,1)} %get-tuple-element.40.x_buf.x_ref, bf16[3136,384]{1,0:T(8,128)(2,1)} %bitcast.12, bf16[384,1152]{1,0:T(8,128)(2,1)} %get-tuple-element.42.wqkv, ...), custom_call_target="tpu_custom_call" | custom-call | tf_op jit(solution)/shard_map/attend/pallas_call | solution.py:616
  156.6 49.4 %mlp.1 = (bf16[784,384]{1,0:T(8,128)(2,1)}, bf16[784,384]{1,0:T(8,128)(2,1)}, bf16[784,384]{1,0:T(8,128)(2,1)}, bf16[784,384]{1,0:T(8,128)(2,1)}, f32[3136,384]{...) custom-call(s32[1]{0:T(128)} %bitcast.slot_ref, ...), custom_call_target="tpu_custom_call" | custom-call | tf_op jit(solution)/shard_map/mlp/pallas_call | solution.py:739
  206.0 0.2 collective-permute-start
  206.2 0.4 collective-permute-start.1
  206.6 1.4 collective-permute-start.2
  207.9 62.7 %attend_back.1 = (bf16[3136,1152]{1,0:T(8,128)(2,1)}, f32[12,2,192,128]{3,2,1,0:T(8,128)}) custom-call(bf16[3136,1152]{1,0:T(8,128)(2,1)} %get-tuple-element.54.qkv, bf16[3136,384]{1,0:T(8,128)(2,1)} %get-tuple-element.55.d_mixed, bf16[16,12,256,256]{3,2,1,0:T(8,128)(2,1)} %get-tuple-element.56.probs, bf16[16,256,256]{2,1,0:T(8,128)(2,1)} %constant.62.clone.keys_tab, ...), custom_call_target="tpu_custom_call" | custom-call | tf_op jit(solution)/shard_map/attend_back/pallas_call | solution.py:828
  270.7 14.7 %input_back.1 = (bf16[784,384]{1,0:T(8,128)(2,1)}, bf16[784,384]{1,0:T(8,128)(2,1)}, bf16[784,384]{1,0:T(8,128)(2,1)}, bf16[784,384]{1,0:T(8,128)(2,1)}, f32[384,1152]{1,0:T(8,128)}, /*index=5*/f32[8,1152]{1,0:T(8,128)}) custom-call(s32[1]{0:T(128)} %bitcast.slot_ref, bf16[3136,1152]{1,0:T(8,128)(2,1)} %get-tuple-element.57.d_qkv_ref, ...), custom_call_target="tpu_custom_call" | custom-call | tf_op jit(solution)/shard_map/input_back/pallas_call | solution.py:901
  285.3 0.5 collective-permute-start.3
  285.8 0.3 collective-permute-start.4
  286.2 13.8 %pack.1.x_ref = bf16[32,448,128]{2,1,0:T(8,128)(2,1)} custom-call(bf16[14,384,384]{2,1,0:T(8,128)(2,1)} %constant.59.clone.one_fine, bf16[14,256,128]{2,1,0:T(8,128)(2,1)} %constant.60.clone.one_coarse, f32[12,2,192,128]{3,2,1,0:T(8,128)} %get-tuple-element.63.g_bias, f32[384,1152]{1,0:T(8,128)} %get-tuple-element.64.g_qkv, ...), custom_call_target="tpu_custom_call" | custom-call | tf_op jit(solution)/shard_map/pack/pallas_call | solution.py:1007
  300.0 0.0 copy-start
  300.0 0.0 copy-start.8
  300.0 0.0 copy-start.9
  300.0 0.0 copy-start.12
  300.0 0.0 copy-start.7
  300.0 0.0 copy-start.10
  300.0 0.0 copy-start.11
  300.0 57.5 %sum_grads.1 = (f32[152,128]{1,0:T(8,128)}, f32[296,128]{1,0:T(8,128)}) custom-call(bf16[32,448,128]{2,1,0:T(8,128)(2,1)} %pack.1.x_ref), custom_call_target="tpu_custom_call" | custom-call | tf_op jit(solution)/shard_map/sum_grads/pallas_call | solution.py:325
  357.6 0.0 copy-done
  357.6 0.0 copy-done.8
  357.6 0.0 copy-done.9
  357.6 1.7 multiply_subtract_fusion
  359.3 0.0 collective-permute-done.in1
  359.3 0.0 copy-start.4
  359.4 0.0 copy-done.12
  359.4 0.1 collective-permute-start.5
  359.4 0.0 copy-done.7
  359.4 0.0 copy-done.10
  359.5 0.0 copy-done.11
  359.5 1.7 multiply_subtract_fusion.1
  361.2 0.0 collective-permute-done.1.in2
  361.2 0.0 copy-start.5
  361.2 0.0 collective-permute-done.2.in3
  361.2 0.0 copy-start.6
  361.2 0.0 copy-done.4
  361.2 0.8 copy-done.5
  362.0 0.2 copy-done.6
  362.2 3.3 join.2
  365.4 0.0 collective-permute-done.3.in1
  365.4 0.0 copy-start.1
  365.4 0.0 collective-permute-done.4.in2
  365.4 0.0 copy-start.2
  365.5 9.8 %collective-permute-done.5.in3 = bf16[784,384]{1,0:T(8,128)(2,1)S(1)} collective-permute-done((bf16[784,384]{1,0:T(8,128)(2,1)S(1)}, bf16[784,384]{1,0:T(8,128)(2,1)S(1)}, u32[]{:S(2)}, u32[]{:S(2)}) %collective-permute-start.5) | collective-permute-done | bytes 602144 | tf_op jit(solution)/shard_map/ppermute | solution.py:1066
  375.2 0.0 copy-start.3
  375.2 0.0 copy-done.1
  375.2 0.0 copy-done.2
  375.2 0.8 copy-done.3
  376.1 4.1 %join.3 = f32[3136,384]{1,0:T(8,128)} custom-call(s32[1]{0:T(128)} %bitcast.slot_ref, bf16[784,384]{1,0:T(8,128)(2,1)} %get-tuple-element.59.in0, bf16[784,384]{1,0:T(8,128)(2,1)} %copy-done.1, bf16[784,384]{1,0:T(8,128)(2,1)} %copy-done.2, bf16[784,384]{1,0:T(8,128)(2,1)} %copy-done.3), custom_call_target="tpu_custom_call" | custom-call | tf_op jit(solution)/shard_map/join/pallas_call | solution.py:1043
Async XLA Ops:
  206.0 153.3 %collective-permute-start = (bf16[784,384]{1,0:T(8,128)(2,1)}, bf16[784,384]{1,0:T(8,128)(2,1)S(1)}, u32[]{:S(2)}, u32[]{:S(2)}) collective-permute-start(bf16[784,384]{1,0:T(8,128)(2,1)} %get-tuple-element.51), channel_id=1, source_target_pairs={{0,4},{4,0},{8,12},{12,8},{16,20},{20,16},{24,28},{28,24},{1,5},{5... | collective-permute-start | bytes 1806344 | tf_op jit(solution)/shard_map/ppermute | solution.py:1066
  206.2 154.9 %collective-permute-start.1 = (bf16[784,384]{1,0:T(8,128)(2,1)}, bf16[784,384]{1,0:T(8,128)(2,1)S(1)}, u32[]{:S(2)}, u32[]{:S(2)}) collective-permute-start(bf16[784,384]{1,0:T(8,128)(2,1)} %get-tuple-element.52), channel_id=1, source_target_pairs={{0,8},{4,12},{8,0},{12,4},{16,24},{20,28},{24,16},{28,20},{1,9},{5... | collective-permute-start | bytes 1806344 | tf_op jit(solution)/shard_map/ppermute | solution.py:1066
  206.6 154.6 %collective-permute-start.2 = (bf16[784,384]{1,0:T(8,128)(2,1)}, bf16[784,384]{1,0:T(8,128)(2,1)S(1)}, u32[]{:S(2)}, u32[]{:S(2)}) collective-permute-start(bf16[784,384]{1,0:T(8,128)(2,1)} %get-tuple-element.53), channel_id=1, source_target_pairs={{0,12},{4,8},{8,4},{12,0},{16,28},{20,24},{24,20},{28,16},{1,13},{... | collective-permute-start | bytes 1806344 | tf_op jit(solution)/shard_map/ppermute | solution.py:1066
  285.3 80.1 %collective-permute-start.3 = (bf16[784,384]{1,0:T(8,128)(2,1)}, bf16[784,384]{1,0:T(8,128)(2,1)S(1)}, u32[]{:S(2)}, u32[]{:S(2)}) collective-permute-start(bf16[784,384]{1,0:T(8,128)(2,1)} %get-tuple-element.60), channel_id=1, source_target_pairs={{0,4},{4,0},{8,12},{12,8},{16,20},{20,16},{24,28},{28,24},{1,5},{5... | collective-permute-start | bytes 1806344 | tf_op jit(solution)/shard_map/ppermute | solution.py:1066
  285.8 79.6 %collective-permute-start.4 = (bf16[784,384]{1,0:T(8,128)(2,1)}, bf16[784,384]{1,0:T(8,128)(2,1)S(1)}, u32[]{:S(2)}, u32[]{:S(2)}) collective-permute-start(bf16[784,384]{1,0:T(8,128)(2,1)} %get-tuple-element.61), channel_id=1, source_target_pairs={{0,8},{4,12},{8,0},{12,4},{16,24},{20,28},{24,16},{28,20},{1,9},{5... | collective-permute-start | bytes 1806344 | tf_op jit(solution)/shard_map/ppermute | solution.py:1066
  300.0 57.6 %copy-start = (f32[36952]{0:T(1024)S(1)}, f32[36952]{0:T(1024)}, u32[]{:S(2)}) copy-start(f32[36952]{0:T(1024)} %param.20) | copy-start | bytes 443428
  300.0 57.6 %copy-start.8 = (f32[36952]{0:T(1024)S(1)}, f32[36952]{0:T(1024)}, u32[]{:S(2)}) copy-start(f32[36952]{0:T(1024)} %param.22) | copy-start | bytes 443428
  300.0 57.6 %copy-start.9 = (f32[36952]{0:T(1024)S(1)}, f32[36952]{0:T(1024)}, u32[]{:S(2)}) copy-start(f32[36952]{0:T(1024)} %param.21) | copy-start | bytes 443428
  300.0 59.4 %copy-start.12 = (bf16[784,384]{1,0:T(8,128)(2,1)S(1)}, bf16[784,384]{1,0:T(8,128)(2,1)}, u32[]{:S(2)}) copy-start(bf16[784,384]{1,0:T(8,128)(2,1)} %get-tuple-element.62) | copy-start | bytes 1806340
  300.0 59.4 %copy-start.7 = (f32[18696]{0:T(1024)S(1)}, f32[18696]{0:T(1024)}, u32[]{:S(2)}) copy-start(f32[18696]{0:T(1024)} %param.17) | copy-start | bytes 224356
  300.0 59.4 %copy-start.10 = (f32[18696]{0:T(1024)S(1)}, f32[18696]{0:T(1024)}, u32[]{:S(2)}) copy-start(f32[18696]{0:T(1024)} %param.19) | copy-start | bytes 224356
  300.0 59.4 %copy-start.11 = (f32[18696]{0:T(1024)S(1)}, f32[18696]{0:T(1024)}, u32[]{:S(2)}) copy-start(f32[18696]{0:T(1024)} %param.18) | copy-start | bytes 224356
  359.3 1.8 copy-start.4
  359.4 15.9 %collective-permute-start.5 = (bf16[784,384]{1,0:T(8,128)(2,1)S(1)}, bf16[784,384]{1,0:T(8,128)(2,1)S(1)}, u32[]{:S(2)}, u32[]{:S(2)}) collective-permute-start(bf16[784,384]{1,0:T(8,128)(2,1)S(1)} %copy-done.12), channel_id=1, source_target_pairs={{0,12},{4,8},{8,4},{12,0},{16,28},{20,24},{24,20},{28,16},{1,13},{... | collective-permute-start | bytes 1806344 | tf_op jit(solution)/shard_map/ppermute | solution.py:1066
  361.2 0.8 copy-start.5
  361.2 1.0 copy-start.6
  365.4 9.8 %copy-start.1 = (bf16[784,384]{1,0:T(8,128)(2,1)}, bf16[784,384]{1,0:T(8,128)(2,1)S(1)}, u32[]{:S(2)}) copy-start(bf16[784,384]{1,0:T(8,128)(2,1)S(1)} %collective-permute-done.3.in1) | copy-start | bytes 1806340
  365.4 9.8 %copy-start.2 = (bf16[784,384]{1,0:T(8,128)(2,1)}, bf16[784,384]{1,0:T(8,128)(2,1)S(1)}, u32[]{:S(2)}) copy-start(bf16[784,384]{1,0:T(8,128)(2,1)S(1)} %collective-permute-done.4.in2) | copy-start | bytes 1806340
  375.2 0.8 copy-start.3

commit v3 on v2

v3 whole, which is shorter than its diff:
```python
import functools

import jax
import jax.numpy as jnp
import ml_dtypes
import numpy as np
from jax import lax
from jax.experimental import pallas as pl
from jax.experimental.pallas import tpu as pltpu
from jax.sharding import PartitionSpec as P

D = 384
HEADS = 12
HDIM = 32
FF = 1536
WIN = 7
STEP = 10
SEQ = WIN * WIN
HALF = 64
FINE = (3 * WIN - 2) ** 2
COARSE = (2 * WIN - 1) ** 2
KEYS = 192

beta_one = 0.9
beta_two = 0.999
learn_rate = 0.04
decay_rate = 0.05
adam_eps = 1e-08
norm_eps = 1e-05
masked_score = -1e30

F32 = jnp.float32
BF16 = jnp.bfloat16
MESH = pl.DeviceIdType.MESH
VMEM_LIMIT = 56 * 2**20


def token_place(gy, gx):
    window = 2 * (gy // WIN) + gx // WIN
    return window * HALF + (gy % WIN) * WIN + gx % WIN


@functools.cache
def gather_tables(images):
    keys = np.zeros((images, 256, 256), np.float32)
    queries = np.zeros((images, 256, 256), np.float32)
    for i in range(images):
        for gy in range(2 * WIN):
            for gx in range(2 * WIN):
                at = token_place(gy, gx) + i
                key = gy * 14 + gx if gy < 10 else 192 + (gy - 10) * 14 + gx
                keys[i, key, at] = 1.0
                keys[i, 140 + (gy // 2) * WIN + gx // 2, at] = 0.25
                queries[i, (gy // WIN) * 128 + (gy % WIN) * 14 + gx, at] = 1.0
    return (
        keys.astype(ml_dtypes.bfloat16),
        queries.astype(ml_dtypes.bfloat16),
        np.ascontiguousarray(keys.transpose(0, 2, 1)).astype(ml_dtypes.bfloat16),
        np.ascontiguousarray(queries.transpose(0, 2, 1)).astype(ml_dtypes.bfloat16),
    )


@functools.cache
def bias_tables():
    fine = np.zeros((14, 384, 384), np.float32)
    coarse = np.zeros((14, 256, 128), np.float32)
    for qx in range(14):
        for a in range(27):
            for kx in range(14):
                col = kx - qx + 9
                if 4 <= a <= 22 and 0 <= col <= 18:
                    fine[qx, 19 * (a - 4) + col, a * 14 + kx] = 1.0
        for p in range(13):
            for s in range(WIN):
                coarse[qx, 13 * p + s - qx // 2 + 6, p * WIN + s] = 1.0
    mask = np.zeros((2, KEYS, 128), np.float32)
    for half in range(2):
        for q in range(98):
            qx = q % 14
            for e in range(KEYS):
                at = e + 56 * half
                if at < 140:
                    ok = abs_ok(qx, at % 14)
                elif at < 189:
                    ok = True
                elif at < 192:
                    ok = False
                else:
                    ok = at < 248 and abs_ok(qx, (at - 192) % 14)
                mask[half, e, q] = 0.0 if ok else masked_score
    return fine.astype(ml_dtypes.bfloat16), coarse.astype(ml_dtypes.bfloat16), mask


def abs_ok(qx, kx):
    return kx < 10 if qx < WIN else kx >= 4


def bias_runs(half, qy):
    fine = (13 - qy) * 14
    pool = 384 + (6 - qy // 2) * WIN
    if half == 0:
        return [(0, 140, fine), (140, 49, pool)]
    return [(0, 84, fine + 56), (84, 49, pool), (136, 56, fine + 140)]


class Part:
    def __init__(self, devices, length):
        self.devices = devices
        self.length = length
        self.rows = -(-((length + 126) // 128 + 1) // 16) * 16
        self.buffer = -(-(self.start(devices - 1) + self.rows) // 8) * 8

    def start(self, device):
        return device * self.length // 128

    def lane(self, device):
        return lax.rem(device * self.length, 128)

    def padded(self, vector):
        extra = self.rows * 128 - self.length
        return jnp.pad(vector, (0, extra)).reshape(self.rows, 128)


def bit_order(n_dp, n_grp):
    dp_bits = [("dp", 2**b) for b in range(n_dp.bit_length() - 1)]
    grp_bits = [("grp", 2**b) for b in reversed(range(n_grp.bit_length() - 1))]
    return dp_bits[1:2] + grp_bits + dp_bits[2:] + dp_bits[:1]


def place_of(order, dp, grp):
    place = 0
    for k, (axis, stride) in enumerate(order):
        place = place + ((dp if axis == "dp" else grp) // stride) % 2 * 2**k
    return place


def partner_of(axis, stride, dp, grp):
    if axis == "dp":
        return (dp + (1 - 2 * ((dp // stride) % 2)) * stride, grp)
    return (dp, grp + (1 - 2 * ((grp // stride) % 2)) * stride)


def greet(partners):
    barrier = pltpu.get_barrier_semaphore()
    for partner in partners:
        pl.semaphore_signal(barrier, inc=1, device_id=partner, device_id_type=MESH)
    pl.semaphore_wait(barrier, len(partners))


def cube_partners(order, dp, grp):
    return [partner_of(axis, stride, dp, grp) for axis, stride in order]


def shift_lanes(values, amount, up):
    lane = lax.broadcasted_iota(jnp.int32, values.shape, 1)
    if up:
        turned = pltpu.roll(values, amount, 1)
        return jnp.where(lane >= amount, turned, pltpu.roll(turned, 1, 0))
    turned = pltpu.roll(values, lax.rem(128 - amount, 128), 1)
    return jnp.where(lane < 128 - amount, turned, pltpu.roll(turned, values.shape[0] - 1, 0))


def window_partner(dp, grp, k):
    low, high = dp % 2, dp // 2 % 2
    to = dp
    if k % 2:
        to = to + 1 - 2 * low
    if k // 2:
        to = to + 2 * (1 - 2 * high)
    return (to, grp)


def exchange_copies(source, target, dp, grp, own_sem, send_sems, recv_sems):
    rows = source.shape[0] // 4
    slot = dp % 4
    mine = pl.ds(pl.multiple_of(slot * rows, 16), rows)
    own = pltpu.make_async_copy(source.at[mine], target.at[mine], own_sem)
    sends = []
    for k in (3, 2, 1):
        to, _ = window_partner(dp, grp, k)
        theirs = pl.ds(pl.multiple_of(to % 4 * rows, 16), rows)
        sends.append(
            pltpu.make_async_remote_copy(
                src_ref=source.at[theirs],
                dst_ref=target.at[mine],
                send_sem=send_sems.at[k - 1],
                recv_sem=recv_sems.at[k - 1],
                device_id=(to, grp),
                device_id_type=MESH,
            )
        )
    return [own] + sends


def cube_copy(order, k, source, target, dp, grp, send_sems, recv_sems):
    axis, stride = order[k]
    return pltpu.make_async_remote_copy(
        src_ref=source,
        dst_ref=target,
        send_sem=send_sems.at[k],
        recv_sem=recv_sems.at[k],
        device_id=partner_of(axis, stride, dp, grp),
        device_id_type=MESH,
    )


def gather_copy(order, k, blocks, dp, grp, sems):
    place = place_of(order, dp, grp)
    held = blocks.at[pl.ds(place // 2**k * 2**k, 2**k)]
    return cube_copy(order, k, held, held, dp, grp, *sems)


def own_block(part, master_ref, own):
    device = lax.axis_index("dp") * lax.axis_size("grp") + lax.axis_index("grp")
    own[...] = shift_lanes(master_ref[...], part.lane(device), True).astype(BF16)


class CubeSum:
    def __init__(self, order, blocks, total, outgoing, arrived, sems):
        self.order, self.blocks, self.total = order, blocks, total
        self.outgoing, self.arrived, self.sems = outgoing, arrived, sems
        self.dp, self.grp = lax.axis_index("dp"), lax.axis_index("grp")
        self.place = place_of(order, self.dp, self.grp)
        self.last = len(order) - 1

    def mine(self, k):
        return self.place // 2**k % 2 * 2**k

    def copy(self, k):
        size = 2**k
        if k == self.last:
            source = self.blocks.at[pl.ds(size - self.mine(k), size)]
        else:
            source = self.outgoing.at[pl.ds(size, size)]
        target = self.arrived.at[pl.ds(size, size)]
        return cube_copy(self.order, k, source, target, self.dp, self.grp, *self.sems)

    def start(self, k):
        size = 2**k
        if k < self.last:
            other = size - self.mine(k)

            def fill(j, carry):
                self.outgoing[size + j] = self.total[other + j].astype(BF16)
                return carry

            lax.fori_loop(0, size, fill, 0)
        self.copy(k).start()

    def finish(self, k):
        size, mine = 2**k, self.mine(k)
        self.copy(k).wait()

        def add(j, carry):
            if k == self.last:
                held = self.blocks[mine + j].astype(F32)
            else:
                held = self.total[mine + j]
            self.total[j] = held + self.arrived[size + j].astype(F32)
            return carry

        lax.fori_loop(0, size, add, 0)

    @staticmethod
    def scratch(devices, rows, stages):
        return [
            pltpu.VMEM((devices // 2, rows, 128), F32),
            pltpu.VMEM((devices // 2, rows, 128), BF16),
            pltpu.VMEM((devices, rows, 128), BF16),
            pltpu.SemaphoreType.DMA((stages,)),
            pltpu.SemaphoreType.DMA((stages,)),
        ]


def gather_kernel(
    part, order, a_ref, tok_ref, out_ref, x_ref, own, own_sem, send, recv, x_sem, x_send, x_recv
):
    dp, grp = lax.axis_index("dp"), lax.axis_index("grp")
    own_block(part, a_ref, own)
    copy = pltpu.make_async_copy(own, out_ref.at[place_of(order, dp, grp)], own_sem)
    copy.start()
    greet(cube_partners(order, dp, grp) + [window_partner(dp, grp, 3)])
    copy.wait()
    exchange = exchange_copies(tok_ref, x_ref, dp, grp, x_sem, x_send, x_recv)
    for k in range(len(order)):
        stage = gather_copy(order, k, out_ref, dp, grp, (send, recv))
        stage.start()
        if k == 0:
            for c in exchange:
                c.start()
        stage.wait()
    for c in exchange:
        c.wait()


def gather_params(part, order, master, tok):
    stages = len(order)
    return pl.pallas_call(
        functools.partial(gather_kernel, part, order),
        out_shape=[
            jax.ShapeDtypeStruct((part.devices, part.rows, 128), BF16),
            jax.ShapeDtypeStruct(tok.shape, BF16),
        ],
        in_specs=[
            pl.BlockSpec(memory_space=pltpu.VMEM),
            pl.BlockSpec(memory_space=pl.ANY),
        ],
        out_specs=[pl.BlockSpec(memory_space=pl.ANY)] * 2,
        scratch_shapes=[
            pltpu.VMEM((part.rows, 128), BF16),
            pltpu.SemaphoreType.DMA,
            pltpu.SemaphoreType.DMA((stages,)),
            pltpu.SemaphoreType.DMA((stages,)),
            pltpu.SemaphoreType.DMA,
            pltpu.SemaphoreType.DMA((3,)),
            pltpu.SemaphoreType.DMA((3,)),
        ],
        compiler_params=pltpu.CompilerParams(
            collective_id=0, has_side_effects=True, vmem_limit_bytes=VMEM_LIMIT
        ),
        name="gather_params",
    )(part.padded(master), tok)


def chunk_copies(source, target, first, size, dp, grp, own_sem, send_sems, recv_sems, skip):
    slot = dp % 4
    into = target.at[slot, pl.ds(first, size)]
    rows = pl.ds(first - skip, size)
    copies = [pltpu.make_async_copy(source.at[slot, rows], into, own_sem)]
    for k in (3, 2, 1):
        to, _ = window_partner(dp, grp, k)
        copies.append(
            pltpu.make_async_remote_copy(
                src_ref=source.at[to % 4, rows],
                dst_ref=into,
                send_sem=send_sems.at[k - 1],
                recv_sem=recv_sems.at[k - 1],
                device_id=(to, grp),
                device_id_type=MESH,
            )
        )
    return copies


def sum_kernel(
    part,
    order,
    blocks,
    last_ref,
    dx_ref,
    grad_ref,
    dx_out,
    total,
    outgoing,
    arrived,
    send,
    recv,
    x_sem,
    x_send,
    x_recv,
):
    dp, grp = lax.axis_index("dp"), lax.axis_index("grp")
    greet(cube_partners(order, dp, grp) + [window_partner(dp, grp, 3)])
    cube = CubeSum(order, blocks, total, outgoing, arrived, (send, recv))
    first = dx_ref.shape[1] - last_ref.shape[1]
    exchange = chunk_copies(
        last_ref, dx_out, first, last_ref.shape[1], dp, grp, x_sem, x_send, x_recv, first
    )
    for k in reversed(range(len(order))):
        cube.start(k)
        if k == len(order) - 1:
            for c in exchange:
                c.start()
        cube.finish(k)
    device = dp * lax.axis_size("grp") + grp
    grad_ref[...] = shift_lanes(total[0], part.lane(device), False)
    for c in exchange:
        c.wait()


def sum_grads(part, order, blocks, last, dx):
    stages = len(order)
    hbm = pl.BlockSpec(memory_space=pl.ANY)
    vm = pl.BlockSpec(memory_space=pltpu.VMEM)
    grad, dx = pl.pallas_call(
        functools.partial(sum_kernel, part, order),
        out_shape=[
            jax.ShapeDtypeStruct((part.rows, 128), F32),
            jax.ShapeDtypeStruct(dx.shape, dx.dtype),
        ],
        in_specs=[vm, hbm, hbm],
        out_specs=[vm, hbm],
        input_output_aliases={2: 1},
        scratch_shapes=CubeSum.scratch(part.devices, part.rows, stages)
        + [
            pltpu.SemaphoreType.DMA,
            pltpu.SemaphoreType.DMA((3,)),
            pltpu.SemaphoreType.DMA((3,)),
        ],
        compiler_params=pltpu.CompilerParams(
            collective_id=1, has_side_effects=True, vmem_limit_bytes=VMEM_LIMIT
        ),
        name="sum_grads",
    )(blocks, last, dx)
    return grad.reshape(-1)[: part.length], dx


def place_list(order, n_dp, n_grp):
    return [place_of(order, d // n_grp, d % n_grp) for d in range(n_dp * n_grp)]


ATTN_VECTORS = (D * 3 * D + D * D + HEADS * FINE + HEADS * COARSE, 5)
TABLE_AT = D * 3 * D + D * D


def unflatten(part, places, blocks, flat):
    flat[...] = jnp.zeros_like(flat)
    for device, place in enumerate(places):
        at = part.start(device)
        flat[at : at + part.rows, :] += blocks[place].astype(F32)


def take_matrix(flat, first, target):
    rows, columns = target.shape
    count = columns // 128
    for j in range(count):
        target[:, j * 128 : (j + 1) * 128] = flat[pl.ds(first + j, rows, stride=count), :].astype(
            target.dtype
        )


def put_matrix(flat, first, source):
    rows, columns = source.shape
    count = columns // 128
    for j in range(count):
        flat[pl.ds(first + j, rows, stride=count), :] = source[:, j * 128 : (j + 1) * 128]


TABLES = ((TABLE_AT, FINE), (TABLE_AT + HEADS * FINE, COARSE))


def table_lines():
    for t, (first, length) in enumerate(TABLES):
        for h in range(HEADS):
            row, lane = divmod(first + h * length, 128)
            yield t, h, length, row, lane, -(-(lane + length) // 128)


def prep_kernel(
    part,
    places,
    blocks,
    one_fine,
    one_coarse,
    mask_ref,
    wqkv,
    wproj,
    vecs,
    bias,
    flat,
    tab_fine,
    tab_coarse,
    shifted,
    turned,
):
    unflatten(part, places, blocks, flat)
    take_matrix(flat, 0, wqkv)
    take_matrix(flat, 3456, wproj)
    vecs[...] = jnp.zeros_like(vecs)
    row, lane = divmod(ATTN_VECTORS[0], 128)
    rows = shift_lanes(flat[row : row + 16, :], lane, False)
    for v in range(5):
        for j in range(3):
            vecs[v : v + 1, j * 128 : (j + 1) * 128] = rows[3 * v + j : 3 * v + j + 1]
    tab_fine[...] = jnp.zeros_like(tab_fine)
    tab_coarse[...] = jnp.zeros_like(tab_coarse)
    for t, h, length, row, lane, count in table_lines():
        line = jnp.concatenate([flat[row + c : row + c + 1, :] for c in range(count)], axis=1)
        (tab_fine, tab_coarse)[t][h : h + 1, 0:length] = line[:, lane : lane + length]
    for qx in range(14):
        at = slice(qx * 16, qx * 16 + 16)
        moved = dot(tab_fine[...].astype(BF16), one_fine[qx])
        for c in range(3):
            shifted[c, at, :] = moved[:, c * 128 : (c + 1) * 128]
        shifted[3, at, :] = dot(tab_coarse[...].astype(BF16), one_coarse[qx])
    turned[...] = jnp.zeros_like(turned)
    for h in range(HEADS):
        table = jnp.concatenate(
            [shifted[c, pl.ds(h, 14, stride=16), :] for c in range(4)], axis=1
        )
        for half in range(2):
            for y in range(WIN):
                for at, length, source in bias_runs(half, WIN * half + y):
                    turned[half, y * 14 : y * 14 + 14, at : at + length] = table[
                        :, source : source + length
                    ]
            bias[h, half] = turned[half].T[0:KEYS] + mask_ref[half]


def prepare(part, places, blocks):
    fine, coarse, mask = bias_tables()
    vm = pl.BlockSpec(memory_space=pltpu.VMEM)
    return pl.pallas_call(
        functools.partial(prep_kernel, part, places),
        out_shape=[
            jax.ShapeDtypeStruct((D, 3 * D), BF16),
            jax.ShapeDtypeStruct((D, D), BF16),
            jax.ShapeDtypeStruct((8, D), F32),
            jax.ShapeDtypeStruct((HEADS, 2, KEYS, 128), F32),
        ],
        in_specs=[vm] * 4,
        out_specs=[vm] * 4,
        scratch_shapes=[
            pltpu.VMEM((part.buffer, 128), F32),
            pltpu.VMEM((16, 384), F32),
            pltpu.VMEM((16, 256), F32),
            pltpu.VMEM((4, 14 * 16, 128), F32),
            pltpu.VMEM((2, 128, 256), F32),
        ],
        compiler_params=pltpu.CompilerParams(vmem_limit_bytes=VMEM_LIMIT),
        name="prepare",
    )(blocks, jnp.asarray(fine), jnp.asarray(coarse), jnp.asarray(mask))


def prep_mlp_kernel(part, places, blocks, w1, w2, vecs, flat):
    unflatten(part, places, blocks, flat)
    take_matrix(flat, 0, w1)
    take_matrix(flat, 4608, w2)
    vecs[...] = jnp.zeros_like(vecs)
    for j in range(12):
        vecs[0:1, j * 128 : (j + 1) * 128] = flat[9216 + j : 9217 + j, :]
    for v in range(3):
        for j in range(3):
            at = 9228 + 3 * v + j
            vecs[1 + v : 2 + v, j * 128 : (j + 1) * 128] = flat[at : at + 1, :]


def prepare_mlp(part, places, blocks):
    vm = pl.BlockSpec(memory_space=pltpu.VMEM)
    return pl.pallas_call(
        functools.partial(prep_mlp_kernel, part, places),
        out_shape=[
            jax.ShapeDtypeStruct((D, FF), BF16),
            jax.ShapeDtypeStruct((FF, D), BF16),
            jax.ShapeDtypeStruct((8, FF), F32),
        ],
        in_specs=[vm],
        out_specs=[vm] * 3,
        scratch_shapes=[pltpu.VMEM((part.buffer, 128), F32)],
        compiler_params=pltpu.CompilerParams(vmem_limit_bytes=VMEM_LIMIT),
        name="prepare_mlp",
    )(blocks)


def dot(a, b):
    return jnp.dot(a, b, preferred_element_type=F32)


def dot_t(a, b):
    return lax.dot_general(a, b, (((1,), (1,)), ((), ())), preferred_element_type=F32)


def norm_parts(values):
    centered = values - jnp.mean(values, axis=-1, keepdims=True)
    scale = lax.rsqrt(jnp.mean(centered * centered, axis=-1, keepdims=True) + norm_eps)
    return centered * scale, scale


def norm_back(d_normed, xhat, scale, gain):
    dh = d_normed * gain
    return scale * (
        dh
        - jnp.mean(dh, axis=-1, keepdims=True)
        - xhat * jnp.mean(dh * xhat, axis=-1, keepdims=True)
    )


def lane_heads(j):
    lane = lax.broadcasted_iota(jnp.int32, (256, 128), 1)
    return (lane // HDIM) == j


def image_rows(ref, i, columns):
    at = pl.ds(pl.multiple_of(48 * i, 16), HALF)
    return jnp.concatenate([ref[w, at, columns] for w in range(4)], axis=0)


def put_image_rows(ref, i, columns, values):
    for w in range(4):
        part = values[w * HALF : (w + 1) * HALF]
        first = pl.ds(pl.multiple_of(48 * i, 16), 16)
        rest = pl.ds(pl.multiple_of(48 * i + 16, 16), HALF - 16)
        held = jnp.where(i > 0, ref[w, first, columns].astype(F32), 0.0)
        ref[w, first, columns] = (held + part[:16]).astype(ref.dtype)
        ref[w, rest, columns] = part[16:].astype(ref.dtype)


def spread(halves):
    columns = []
    for half, values in enumerate(halves):
        pieces = [values, jnp.zeros((64 - 56 * half, 128), F32)]
        if half:
            pieces = [jnp.zeros((56, 128), F32)] + pieces
        columns.append(jnp.concatenate(pieces, axis=0))
    return jnp.concatenate(columns, axis=1).astype(BF16)


def half_of(values, half):
    return values[56 * half : 56 * half + KEYS, 128 * half : 128 * half + 128]


def tile_of(h):
    return slice(h // 4 * 128, h // 4 * 128 + 128)


def attend_kernel(
    rows,
    part,
    order,
    x_buf,
    cot_ref,
    master_ref,
    wqkv,
    vecs,
    bias,
    keys_tab,
    query_tab,
    query_back,
    mixed,
    probs,
    ext,
    inverse,
    cot_out,
    blocks,
    normed,
    qkv,
    mixed_t,
    own,
    own_sem,
    send,
    recv,
    cot_sem,
    cot_send,
    cot_recv,
):
    i = pl.program_id(0)
    steps = pl.num_programs(0)
    dp, grp = lax.axis_index("dp"), lax.axis_index("grp")
    exchange = exchange_copies(cot_ref, cot_out, dp, grp, cot_sem, cot_send, cot_recv)
    stages = len(order)

    @pl.when(i == 0)
    def _():
        own_block(part, master_ref, own)
        copy = pltpu.make_async_copy(own, blocks.at[place_of(order, dp, grp)], own_sem)
        copy.start()
        greet(cube_partners(order, dp, grp) + [window_partner(dp, grp, 3)])
        copy.wait()

    for k in range(stages):

        @pl.when(i == k * steps // stages)
        def _(k=k):
            if k:
                gather_copy(order, k - 1, blocks, dp, grp, (send, recv)).wait()
            gather_copy(order, k, blocks, dp, grp, (send, recv)).start()

    @pl.when(i == 0)
    def _():
        for c in exchange:
            c.start()

        def project(w, carry):
            step = rows // 7

            def norm(c, inner):
                at = pl.multiple_of(c * step, 16)
                xhat, _ = norm_parts(x_buf[w, pl.ds(at, step), :].astype(F32))
                normed[pl.ds(at, step), :] = (xhat * vecs[0:1, :D] + vecs[1:2, :D]).astype(BF16)
                return inner

            lax.fori_loop(0, 7, norm, 0)
            q = dot(normed[...], wqkv[:, :D]) + vecs[2:3, :D]
            qkv[w, :, :D] = (q * HDIM ** (-0.5)).astype(BF16)
            qkv[w, :, D : 2 * D] = dot(normed[...], wqkv[:, D : 2 * D]).astype(BF16)
            v = dot(normed[...], wqkv[:, 2 * D :]) + vecs[3:4, :D]
            qkv[w, :, 2 * D :] = v.astype(BF16)
            return carry

        lax.fori_loop(0, 4, project, 0)

    q_ext = dot(query_tab[0], image_rows(qkv, i, slice(0, D))).astype(BF16)
    kv_ext = dot(keys_tab[0], image_rows(qkv, i, slice(D, 3 * D)))
    k_ext = kv_ext[:, :D].astype(BF16)
    v_ext = kv_ext[:, D:]
    v_t = v_ext.T.astype(BF16)
    ext[0, :, :D] = q_ext
    ext[0, :, D : 2 * D] = k_ext
    ext[0, :, 2 * D :] = v_ext.astype(BF16)

    def scores_of(h):
        q_head = jnp.where(lane_heads(h % 4), q_ext[:, tile_of(h)], 0)
        return dot_t(k_ext[:, tile_of(h)], q_head)

    inverse[0, HEADS:16, :] = jnp.zeros((16 - HEADS, 256), F32)
    scores = scores_of(0)
    for h in range(HEADS):
        ahead = scores_of(h + 1) if h + 1 < HEADS else None
        halves, inverses = [], []
        for half in range(2):
            s = half_of(scores, half) + bias[h, half]
            e = jnp.exp(s - jnp.max(s, axis=0, keepdims=True))
            inverses.append(1.0 / jnp.sum(e, axis=0, keepdims=True))
            halves.append(e)
        e = spread(halves)
        inv = jnp.concatenate(inverses, axis=1)
        probs[0, h] = e
        inverse[0, h : h + 1, :] = inv
        mixed_t[h * HDIM : (h + 1) * HDIM, :] = (
            dot(v_t[h * HDIM : (h + 1) * HDIM, :], e) * inv
        ).astype(BF16)
        scores = ahead
    put_image_rows(mixed, i, slice(0, D), dot_t(query_back[0], mixed_t[...]))

    @pl.when(i == steps - 1)
    def _():
        gather_copy(order, stages - 1, blocks, dp, grp, (send, recv)).wait()
        for c in exchange:
            c.wait()


def attend(part, order, x, cot, master, wqkv, vecs, bias, images):
    tokens = x.shape[0]
    stages = len(order)
    rows = tokens // 4
    keys_tab, query_tab, _, query_back = gather_tables(images)
    vm = pl.BlockSpec(memory_space=pltpu.VMEM)
    hbm = pl.BlockSpec(memory_space=pl.ANY)
    table = pl.BlockSpec((1, 256, 256), lambda i: (i, 0, 0))
    return pl.pallas_call(
        functools.partial(attend_kernel, rows, part, order),
        grid=(images,),
        out_shape=[
            jax.ShapeDtypeStruct((4, rows, D), BF16),
            jax.ShapeDtypeStruct((images, HEADS, 256, 256), BF16),
            jax.ShapeDtypeStruct((images, 256, 3 * D), BF16),
            jax.ShapeDtypeStruct((images, 16, 256), F32),
            jax.ShapeDtypeStruct((tokens, D), BF16),
            jax.ShapeDtypeStruct((part.devices, part.rows, 128), BF16),
        ],
        in_specs=[vm, hbm] + [vm] * 4 + [table] * 3,
        out_specs=[
            pl.BlockSpec((4, rows, D), lambda i: (0, 0, 0)),
            pl.BlockSpec((1, HEADS, 256, 256), lambda i: (i, 0, 0, 0)),
            pl.BlockSpec((1, 256, 3 * D), lambda i: (i, 0, 0)),
            pl.BlockSpec((1, 16, 256), lambda i: (i, 0, 0)),
            hbm,
            hbm,
        ],
        scratch_shapes=[
            pltpu.VMEM((rows, D), BF16),
            pltpu.VMEM((4, rows, 3 * D), BF16),
            pltpu.VMEM((D, 256), BF16),
            pltpu.VMEM((part.rows, 128), BF16),
            pltpu.SemaphoreType.DMA,
            pltpu.SemaphoreType.DMA((stages,)),
            pltpu.SemaphoreType.DMA((stages,)),
            pltpu.SemaphoreType.DMA,
            pltpu.SemaphoreType.DMA((3,)),
            pltpu.SemaphoreType.DMA((3,)),
        ],
        compiler_params=pltpu.CompilerParams(
            collective_id=2, has_side_effects=True, vmem_limit_bytes=VMEM_LIMIT
        ),
        name="attend",
    )(
        x.reshape(4, rows, D),
        cot,
        part.padded(master),
        wqkv,
        vecs,
        bias,
        keys_tab,
        query_tab,
        query_back,
    )


GELU_A = float(np.sqrt(2.0 / np.pi))
GELU_B = 0.044715


def mlp_kernel(
    cot_ref,
    mixed_ref,
    x_ref,
    wproj,
    w1,
    w2,
    vecs_a,
    vecs,
    out_ref,
    d_res_ref,
    d_mixed_ref,
    g_w1,
    g_w2t,
    g_proj,
    g_vec,
):
    i = pl.program_id(0)
    chunk = mixed_ref.shape[0]

    @pl.when(i == 0)
    def _():
        g_w1[...] = jnp.zeros_like(g_w1)
        g_w2t[...] = jnp.zeros_like(g_w2t)
        g_proj[...] = jnp.zeros_like(g_proj)
        g_vec[...] = jnp.zeros_like(g_vec)

    mix = mixed_ref[...]
    res = x_ref[...].astype(F32) + dot(mix, wproj[...]) + vecs_a[4:5, :]
    xhat, scale = norm_parts(res)
    gain = vecs[1:2, :D]
    normed = (xhat * gain + vecs[2:3, :D]).astype(BF16)
    grad = cot_ref[...]
    grad_t = grad.T
    normed_t = normed.T
    out = res + vecs[3:4, :D]
    d_normed = jnp.zeros((chunk, D), F32)
    for f in range(3):
        cols = slice(f * 512, f * 512 + 512)
        hidden = dot(normed, w1[:, cols]) + vecs[0:1, cols]
        square = hidden * hidden
        t = jnp.tanh(hidden * (GELU_A + (GELU_A * GELU_B) * square))
        half = 0.5 + 0.5 * t
        act = (hidden * half).astype(BF16)
        slope = half + (0.5 * hidden) * (1.0 - t * t) * (GELU_A + (3 * GELU_A * GELU_B) * square)
        out += dot(act, w2[cols, :])
        d_hidden32 = dot_t(grad, w2[cols, :]) * slope
        d_hidden = d_hidden32.astype(BF16)
        g_vec[0:1, cols] += jnp.sum(d_hidden32, axis=0, keepdims=True)
        d_normed += dot_t(d_hidden, w1[:, cols])
        g_w1[:, cols] += dot(normed_t, d_hidden)
        g_w2t[:, cols] += dot(grad_t, act)
    out_ref[...] = out.astype(BF16)
    grad32 = grad.astype(F32)
    d_res = grad32 + norm_back(d_normed, xhat, scale, gain)
    d_res_ref[...] = d_res
    d_attn = d_res.astype(BF16)
    d_mixed_ref[...] = dot_t(d_attn, wproj[...]).astype(BF16)
    g_proj[...] += dot(mix.T, d_attn)
    g_vec[1:2, :D] += jnp.sum(d_normed * xhat, axis=0, keepdims=True)
    g_vec[2:3, :D] += jnp.sum(d_normed, axis=0, keepdims=True)
    g_vec[3:4, :D] += jnp.sum(grad32, axis=0, keepdims=True)
    g_vec[4:5, :D] += jnp.sum(d_res, axis=0, keepdims=True)


def mlp(cot, mixed, x, wproj, w1, w2, vecs_a, vecs):
    tokens = x.shape[0]
    chunk = tokens // 7
    vm = pl.BlockSpec(memory_space=pltpu.VMEM)
    tile = pl.BlockSpec((chunk, D), lambda i: (i, 0))
    fixed = lambda *shape: pl.BlockSpec(shape, lambda i: (0, 0))
    return pl.pallas_call(
        mlp_kernel,
        grid=(7,),
        out_shape=[
            jax.ShapeDtypeStruct((tokens, D), BF16),
            jax.ShapeDtypeStruct((tokens, D), F32),
            jax.ShapeDtypeStruct((tokens, D), BF16),
            jax.ShapeDtypeStruct((D, FF), F32),
            jax.ShapeDtypeStruct((D, FF), F32),
            jax.ShapeDtypeStruct((D, D), F32),
            jax.ShapeDtypeStruct((8, FF), F32),
        ],
        in_specs=[tile] * 3 + [vm] * 5,
        out_specs=[tile] * 3 + [fixed(D, FF), fixed(D, FF), fixed(D, D), fixed(8, FF)],
        compiler_params=pltpu.CompilerParams(vmem_limit_bytes=VMEM_LIMIT),
        name="mlp",
    )(cot, mixed, x, wproj, w1, w2, vecs_a, vecs)


CHUNK = 192
LAST = 208


def head_tables():
    lanes = np.arange(D) // HDIM
    one = (np.arange(16)[:, None] == lanes[None, :]).astype(np.float32)
    return np.concatenate([one, one], axis=0).astype(ml_dtypes.bfloat16)


def split_float(values):
    high = values.astype(BF16)
    return high, (values - high.astype(F32)).astype(BF16)


def attend_back_kernel(
    part,
    order,
    ext,
    d_mixed,
    mixed,
    probs,
    inverse,
    head_tab,
    keys_back,
    query_tab,
    query_back,
    x_hbm,
    d_res_hbm,
    wqkv,
    vecs,
    blocks,
    out_src,
    g_bias,
    g_qkv,
    g_vec,
    dx_last,
    grad_ref,
    out_ref,
    dx_ref,
    d_query_t,
    d_key_value,
    d_qkv,
    d_in,
    x_buf,
    d_res_buf,
    load_sems,
    total,
    outgoing,
    arrived,
    send,
    recv,
    out_sem,
    out_send,
    out_recv,
    dx_sem0,
    dx_send0,
    dx_recv0,
    dx_sem1,
    dx_send1,
    dx_recv1,
    dx_sem2,
    dx_send2,
    dx_recv2,
):
    i = pl.program_id(0)
    steps = pl.num_programs(0)
    stages = len(order)
    dp, grp = lax.axis_index("dp"), lax.axis_index("grp")
    cube = CubeSum(order, blocks, total, outgoing, arrived, (send, recv))
    exchange = exchange_copies(out_src, out_ref, dp, grp, out_sem, out_send, out_recv)
    dx_sems = (
        (dx_sem0, dx_send0, dx_recv0),
        (dx_sem1, dx_send1, dx_recv1),
        (dx_sem2, dx_send2, dx_recv2),
    )
    loads = [
        pltpu.make_async_copy(x_hbm, x_buf, load_sems.at[0]),
        pltpu.make_async_copy(d_res_hbm, d_res_buf, load_sems.at[1]),
    ]

    def chunk(c):
        return chunk_copies(d_in, dx_ref, CHUNK * c, CHUNK, dp, grp, *dx_sems[c], 0)

    @pl.when(i == 0)
    def _():
        for c in loads:
            c.start()
        g_bias[...] = jnp.zeros_like(g_bias)
        g_qkv[...] = jnp.zeros_like(g_qkv)
        g_vec[...] = jnp.zeros_like(g_vec)
        greet(cube_partners(order, dp, grp) + [window_partner(dp, grp, 3)])

    for k in reversed(range(stages)):

        @pl.when(i == (stages - 1 - k) * steps // stages)
        def _(k=k):
            if k < stages - 1:
                cube.finish(k + 1)
            cube.start(k)

    @pl.when(i == 0)
    def _():
        for c in exchange:
            c.start()

    inv = inverse[0]
    inv_high, inv_low = split_float(inv)
    inv_t = jnp.concatenate([inv_high, inv_low], axis=0).astype(F32).T.astype(BF16)
    dm_rows = image_rows(d_mixed, i, slice(0, D))
    dm_ext = dot(query_tab[0], dm_rows) * dot(inv_t, head_tab[...])
    mixed_ext = dot(query_tab[0], image_rows(mixed, i, slice(0, D)))
    dm_ext = dm_ext.astype(BF16)
    high, low = split_float(dm_ext.astype(F32) * mixed_ext)
    sums = dot_t(head_tab[0:16, :], high) + dot_t(head_tab[0:16, :], low)
    q_ext = ext[0, :, :D]
    k_t = ext[0, :, D : 2 * D].astype(F32).T.astype(BF16)
    v_ext = ext[0, :, 2 * D :]

    def head_inputs(h):
        mine = lane_heads(h % 4)
        q_head = jnp.where(mine, q_ext[:, tile_of(h)], 0)
        dm_head = jnp.where(mine, dm_ext[:, tile_of(h)], 0)
        return q_head, dm_head, dot_t(v_ext[:, tile_of(h)], dm_head)

    current = head_inputs(0)
    for h in range(HEADS):
        q_head, dm_head, d_probs = current
        if h + 1 < HEADS:
            current = head_inputs(h + 1)
        if h % 4 == 0:
            d_key = jnp.zeros((256, 128), F32)
            d_value = jnp.zeros((256, 128), F32)
        e = probs[0, h]
        d_value += dot(e, dm_head)
        halves = []
        for half in range(2):
            lanes = slice(128 * half, 128 * half + 128)
            e32 = e[:, lanes].astype(F32)[56 * half : 56 * half + KEYS]
            ds = e32 * (half_of(d_probs, half) - sums[h : h + 1, lanes])
            g_bias[h, half] += ds
            halves.append(ds)
        ds = spread(halves)
        d_key += dot(ds, q_head)
        d_query_t[h * HDIM : (h + 1) * HDIM, :] = (
            dot(k_t[h * HDIM : (h + 1) * HDIM, :], ds) * HDIM ** (-0.5)
        ).astype(BF16)
        if h % 4 == 3:
            d_key_value[:, tile_of(h)] = d_key.astype(BF16)
            d_key_value[:, D + h // 4 * 128 : D + h // 4 * 128 + 128] = d_value.astype(BF16)
    put_image_rows(d_qkv, i, slice(0, D), dot_t(query_back[0], d_query_t[...]))
    put_image_rows(d_qkv, i, slice(D, 3 * D), dot(keys_back[0], d_key_value[...]))

    @pl.when(i == 3)
    def _():
        for c in loads:
            c.wait()

    @pl.when(lax.rem(i, 4) == 3)
    def _():
        c = i // 4
        at = pl.ds(pl.multiple_of(c * CHUNK, 16), LAST)
        xhat, scale = norm_parts(x_buf[:, at, :].reshape(4 * LAST, D).astype(F32))
        gain = vecs[0:1, :]
        normed = (xhat * gain + vecs[1:2, :]).astype(BF16)
        row = lax.rem(lax.broadcasted_iota(jnp.int32, (4 * LAST, 1), 0), LAST)
        counts = row < jnp.where(i == steps - 1, LAST, CHUNK)
        grads = d_qkv[:, at, :].reshape(4 * LAST, 3 * D)
        grads = jnp.where(counts, grads, 0)
        d_normed = dot_t(grads, wqkv[...])
        result = d_res_buf[:, at, :].reshape(4 * LAST, D) + norm_back(d_normed, xhat, scale, gain)
        result = result.astype(BF16).reshape(4, LAST, D)
        d_in[:, at, :] = result
        dx_last[...] = result
        g_qkv[...] += dot(normed.T, grads)
        g_vec[0:1, :] += jnp.sum(grads.astype(F32), axis=0, keepdims=True)
        g_vec[1:2, :D] += jnp.sum(d_normed * xhat, axis=0, keepdims=True)
        g_vec[2:3, :D] += jnp.sum(d_normed, axis=0, keepdims=True)

    for c in range(3):

        @pl.when(i == 4 * c + 3)
        def _(c=c):
            for copy in chunk(c):
                copy.start()

    @pl.when(i == steps - 1)
    def _():
        cube.finish(0)
        device = dp * lax.axis_size("grp") + grp
        grad_ref[...] = shift_lanes(total[0], part.lane(device), False)
        for c in exchange:
            c.wait()
        for c in range(3):
            for copy in chunk(c):
                copy.wait()


def attend_back(
    part, order, ext, d_mixed, mixed, probs, inverse, x, d_res, wqkv, vecs, blocks, out
):
    images = ext.shape[0]
    tokens = out.shape[0]
    rows = tokens // 4
    stages = len(order)
    _, query_tab, keys_back, query_back = gather_tables(images)
    vm = pl.BlockSpec(memory_space=pltpu.VMEM)
    hbm = pl.BlockSpec(memory_space=pl.ANY)
    table = pl.BlockSpec((1, 256, 256), lambda i: (i, 0, 0))
    by_window = lambda array: array.reshape(4, rows, -1)
    outs = pl.pallas_call(
        functools.partial(attend_back_kernel, part, order),
        grid=(images,),
        out_shape=[
            jax.ShapeDtypeStruct((HEADS, 2, KEYS, 128), F32),
            jax.ShapeDtypeStruct((D, 3 * D), F32),
            jax.ShapeDtypeStruct((8, 3 * D), F32),
            jax.ShapeDtypeStruct((4, LAST, D), BF16),
            jax.ShapeDtypeStruct((part.rows, 128), F32),
            jax.ShapeDtypeStruct((tokens, D), BF16),
            jax.ShapeDtypeStruct((4, rows, D), BF16),
        ],
        in_specs=[
            pl.BlockSpec((1, 256, 3 * D), lambda i: (i, 0, 0)),
            vm,
            vm,
            pl.BlockSpec((1, HEADS, 256, 256), lambda i: (i, 0, 0, 0)),
            pl.BlockSpec((1, 16, 256), lambda i: (i, 0, 0)),
            vm,
        ]
        + [table] * 3
        + [hbm, hbm, vm, vm, vm, hbm],
        out_specs=[
            pl.BlockSpec((HEADS, 2, KEYS, 128), lambda i: (0, 0, 0, 0)),
            pl.BlockSpec((D, 3 * D), lambda i: (0, 0)),
            pl.BlockSpec((8, 3 * D), lambda i: (0, 0)),
            pl.BlockSpec((4, LAST, D), lambda i: (0, 0, 0)),
            pl.BlockSpec((part.rows, 128), lambda i: (0, 0)),
            hbm,
            hbm,
        ],
        scratch_shapes=[
            pltpu.VMEM((D, 256), BF16),
            pltpu.VMEM((256, 2 * D), BF16),
            pltpu.VMEM((4, rows, 3 * D), BF16),
            pltpu.VMEM((4, rows, D), BF16),
            pltpu.VMEM((4, rows, D), BF16),
            pltpu.VMEM((4, rows, D), F32),
            pltpu.SemaphoreType.DMA((2,)),
        ]
        + CubeSum.scratch(part.devices, part.rows, stages)
        + [
            pltpu.SemaphoreType.DMA,
            pltpu.SemaphoreType.DMA((3,)),
            pltpu.SemaphoreType.DMA((3,)),
        ]
        * 4,
        compiler_params=pltpu.CompilerParams(
            collective_id=3, has_side_effects=True, vmem_limit_bytes=VMEM_LIMIT
        ),
        name="attend_back",
    )(
        ext,
        by_window(d_mixed),
        by_window(mixed),
        probs,
        inverse,
        jnp.asarray(head_tables()),
        keys_back,
        query_tab,
        query_back,
        by_window(x),
        by_window(d_res),
        wqkv,
        vecs,
        blocks,
        out,
    )
    grad = outs[4].reshape(-1)[: part.length]
    return (*outs[:4], grad, *outs[5:])


def to_blocks(part, places, flat, out):
    for device, place in enumerate(places):
        at = part.start(device)
        out[place] = flat[at : at + part.rows, :].astype(BF16)


def pack_mlp_kernel(part, places, g_w1, g_w2t, g_vec, out, flat):
    flat[...] = jnp.zeros_like(flat)
    put_matrix(flat, 0, g_w1)
    for j in range(3):
        flat[pl.ds(4608 + j, FF, stride=3), :] = g_w2t[j * 128 : (j + 1) * 128, :].T
    for j in range(12):
        flat[9216 + j : 9217 + j, :] = g_vec[0:1, j * 128 : (j + 1) * 128]
    for v in range(3):
        for j in range(3):
            at = 9228 + 3 * v + j
            flat[at : at + 1, :] = g_vec[1 + v : 2 + v, j * 128 : (j + 1) * 128]
    to_blocks(part, places, flat, out)


def pack_mlp(part, places, g_w1, g_w2t, g_vec):
    vm = pl.BlockSpec(memory_space=pltpu.VMEM)
    return pl.pallas_call(
        functools.partial(pack_mlp_kernel, part, places),
        out_shape=jax.ShapeDtypeStruct((part.devices, part.rows, 128), BF16),
        in_specs=[vm] * 3,
        out_specs=vm,
        scratch_shapes=[pltpu.VMEM((part.buffer, 128), F32)],
        compiler_params=pltpu.CompilerParams(vmem_limit_bytes=VMEM_LIMIT),
        name="pack_mlp",
    )(g_w1, g_w2t, g_vec)


def pack_kernel(
    part,
    places,
    one_fine,
    one_coarse,
    g_bias,
    g_qkv,
    g_vec1,
    g_proj,
    g_vec2,
    out,
    flat,
    table,
    shifted,
    line,
):
    flat[...] = jnp.zeros_like(flat)
    put_matrix(flat, 0, g_qkv)
    put_matrix(flat, 3456, g_proj)
    vectors = [
        g_vec1[1:2, :D],
        g_vec1[2:3, :D],
        g_vec1[0:1, :D],
        g_vec1[0:1, 2 * D :],
        g_vec2[4:5, :D],
    ]
    pieces = [v[:, j * 128 : (j + 1) * 128] for v in vectors for j in range(3)]
    pieces += [jnp.zeros((1, 128), F32)]
    row, lane = divmod(ATTN_VECTORS[0], 128)
    flat[row : row + 16, :] += shift_lanes(jnp.concatenate(pieces, axis=0), lane, True)
    for h in range(HEADS):
        table[...] = jnp.zeros_like(table)
        for half in range(2):
            turned = g_bias[h, half].T
            for y in range(WIN):
                for at, length, source in bias_runs(half, WIN * half + y):
                    table[0:14, source : source + length] += turned[
                        y * 14 : y * 14 + 14, at : at + length
                    ]
        for c in range(4):
            shifted[c, pl.ds(h, 14, stride=16), :] = table[0:14, c * 128 : (c + 1) * 128]
    g_fine = jnp.zeros((16, 384), F32)
    g_coarse = jnp.zeros((16, 256), F32)
    for qx in range(14):
        at = slice(qx * 16, qx * 16 + 16)
        gathered = jnp.concatenate([shifted[c, at, :] for c in range(4)], axis=1)
        high = gathered.astype(BF16)
        low = (gathered - high.astype(F32)).astype(BF16)
        g_fine += dot_t(high[:, :384], one_fine[qx]) + dot_t(low[:, :384], one_fine[qx])
        g_coarse += dot_t(high[:, 384:], one_coarse[qx]) + dot_t(low[:, 384:], one_coarse[qx])
    for t, h, length, row, lane, count in table_lines():
        line[...] = jnp.zeros_like(line)
        line[0:1, lane : lane + length] = (g_fine, g_coarse)[t][h : h + 1, :length]
        for c in range(count):
            flat[row + c : row + c + 1, :] += line[0:1, c * 128 : (c + 1) * 128]
    to_blocks(part, places, flat, out)


def pack(part, places, g_bias, g_qkv, g_vec1, g_proj, g_vec2):
    fine, coarse, _ = bias_tables()
    vm = pl.BlockSpec(memory_space=pltpu.VMEM)
    return pl.pallas_call(
        functools.partial(pack_kernel, part, places),
        out_shape=jax.ShapeDtypeStruct((part.devices, part.rows, 128), BF16),
        in_specs=[vm] * 7,
        out_specs=vm,
        scratch_shapes=[
            pltpu.VMEM((part.buffer, 128), F32),
            pltpu.VMEM((16, 512), F32),
            pltpu.VMEM((4, 14 * 16, 128), F32),
            pltpu.VMEM((8, 512), F32),
        ],
        compiler_params=pltpu.CompilerParams(vmem_limit_bytes=VMEM_LIMIT),
        name="pack",
    )(jnp.asarray(fine), jnp.asarray(coarse), g_bias, g_qkv, g_vec1, g_proj, g_vec2)


def adamw(master, first, second, grads):
    first_new = beta_one * first + (1.0 - beta_one) * grads
    second_new = beta_two * second + (1.0 - beta_two) * grads * grads
    first_hat = first_new / (1.0 - beta_one**STEP)
    second_hat = second_new / (1.0 - beta_two**STEP)
    master_new = master - learn_rate * (
        first_hat / (jnp.sqrt(second_hat) + adam_eps) + decay_rate * master
    )
    return (first_new, second_new, master_new)


def body(
    tokens, cotangent, attn_master, attn_first, attn_second, mlp_master, mlp_first, mlp_second
):
    n_dp, n_grp = lax.axis_size("dp"), lax.axis_size("grp")
    order = bit_order(n_dp, n_grp)
    places = place_list(order, n_dp, n_grp)
    part_a = Part(n_dp * n_grp, attn_master.shape[0])
    part_b = Part(n_dp * n_grp, mlp_master.shape[0])
    images = tokens.shape[1] // 4 // SEQ
    blocks_a, x = gather_params(part_a, order, attn_master, tokens[0])
    wqkv, wproj, vecs_a, bias = prepare(part_a, places, blocks_a)
    mixed, probs, ext, inverse, cot, blocks_b = attend(
        part_b, order, x, cotangent[0], mlp_master, wqkv, vecs_a, bias, images
    )
    mixed = mixed.reshape(-1, D)
    w1, w2, vecs_b = prepare_mlp(part_b, places, blocks_b)
    out, d_res, d_mixed, g_w1, g_w2t, g_proj, g_vec2 = mlp(
        cot, mixed, x, wproj, w1, w2, vecs_a, vecs_b
    )
    sums_b = pack_mlp(part_b, places, g_w1, g_w2t, g_vec2)
    g_bias, g_qkv, g_vec1, dx_last, grad_b, output, dx = attend_back(
        part_b,
        order,
        ext,
        d_mixed,
        mixed,
        probs,
        inverse,
        x,
        d_res,
        wqkv,
        vecs_a,
        sums_b,
        out,
    )
    sums_a = pack(part_a, places, g_bias, g_qkv, g_vec1, g_proj, g_vec2)
    grad_a, dx = sum_grads(part_a, order, sums_a, dx_last, dx)
    attn_new = adamw(attn_master, attn_first, attn_second, grad_a)
    mlp_new = adamw(mlp_master, mlp_first, mlp_second, grad_b)
    input_grad = dx.reshape(-1, D).astype(F32)
    return (output[None], input_grad[None], *attn_new, *mlp_new)


def solution(mesh):
    flat_spec = P(("dp", "grp"))
    token_spec = P("dp", "grp", None)
    placed = (token_spec, token_spec) + (flat_spec,) * 6
    return jax.shard_map(
        body, mesh=mesh, in_specs=placed, out_specs=placed, check_vma=False
    )
```

time: 381 us -> 289 us (0.76)
  Pallas kernels: 358 us -> 275 us
  waiting for transfers between devices: 9.79 us -> 0 us
  other arithmetic: 3.43 us -> 7.71 us
    pallas_call x10 -> x9, Pallas kernels: 358 us -> 275 us  [the longest x1 67.8 us: attend(): pl.pallas_call(functools.partial(attend_kernel, rows, part, order), grid=...]
    ppermute x6 -> x0, waiting for transfers between devices: 9.79 us -> none  [swap(): return lax.ppermute(value, 'dp', pairs)]
    convert_element_type x0 -> x1, other arithmetic: none -> 4.36 us  [body(): input_grad = dx.reshape(-1, D).astype(F32)]
  transfers between devices with their start and end apart: 6 -> 0, of which waited for: 1 -> 0; matrix products, arithmetic and copies ran while one was open for 1% -> 0% of each run, Pallas kernels for 40% -> 0%
where the time goes in v3:
time: 289 us; the launch traced here: 288 us
  Pallas kernels  275 us (95%)
  other arithmetic  7.71 us (3%)
  local copies, waits for them, and re-layouts  4.56 us (2%)
    pallas_call x1, Pallas kernels, attend(): pl.pallas_call(functools.partial(attend_kernel, rows, part, order), grid=...  67.8 us
    pallas_call x1, Pallas kernels, attend_back(): pl.pallas_call(functools.partial(attend_back_kernel, part, order), grid=(...  67.3 us
    pallas_call x1, Pallas kernels, mlp(): pl.pallas_call(mlp_kernel, grid=(7,), out_shape=[jax.ShapeDtypeStruct((to...  47.9 us
    pallas_call x1, Pallas kernels, gather_params(): pl.pallas_call(functools.partial(gather_kernel, part, order), out_shape=[...  34.1 us
    pallas_call x1, Pallas kernels, sum_grads(): pl.pallas_call(functools.partial(sum_kernel, part, order), out_shape=[jax...  29.9 us
    pallas_call x1, Pallas kernels, pack(): pl.pallas_call(functools.partial(pack_kernel, part, places), out_shape=ja...  10.9 us
    pallas_call x1, Pallas kernels, prepare(): pl.pallas_call(functools.partial(prep_kernel, part, places), out_shape=[j...  8.42 us

profile of v3, /device:TPU:0, one launch (start us, length us, event | category | flops | bytes accessed | tf_op | source)
XLA Modules:
  0.0 288.2 jit_solution(5298833455966883665)
XLA Ops:
  0.6 1.5 pad_bitcast_fusion.1.a_ref
  2.2 1.6 pad_bitcast_fusion.master_ref
  3.7 34.1 %gather_params.1 = (bf16[32,160,128]{2,1,0:T(8,128)(2,1)}, bf16[3136,384]{1,0:T(8,128)(2,1)}) custom-call(f32[160,128]{1,0:T(8,128)} %pad_bitcast_fusion.1.a_ref, bf16[3136,384]{1,0:T(8,128)(2,1)} %bitcast.23), custom_call_target="tpu_custom_call" | custom-call | tf_op jit(solution)/shard_map/gather_params/pallas_call | solution.py:298
  37.8 8.4 %prepare.1 = (bf16[384,1152]{1,0:T(8,128)(2,1)}, bf16[384,384]{1,0:T(8,128)(2,1)}, f32[8,384]{1,0:T(8,128)}, f32[12,2,192,128]{3,2,1,0:T(8,128)}) custom-call(bf16[32,160,128]{2,1,0:T(8,128)(2,1)} %get-tuple-element.40.blocks, bf16[14,384,384]{2,1,0:T(8,128)(2,1)} %constant.14.clone.one_fine, bf16[14,256,128]{2,1,0:T(8,128)(2,1)} %constant.15.clone.one_coarse, ...), custom_call_target="tpu_custom_call" | custom-call | tf_op jit(solution)/shard_map/prepare/pallas_call | solution.py:503
  46.2 67.8 %attend.1 = (bf16[4,784,384]{2,1,0:T(8,128)(2,1)}, bf16[16,12,256,256]{3,2,1,0:T(8,128)(2,1)}, bf16[16,256,1152]{2,1,0:T(8,128)(2,1)}, f32[16,16,256]{2,1,0:T(8,...) custom-call(bf16[4,784,384]{2,1,0:T(8,128)(2,1)} %bitcast.17, bf16[3136,384]{1,0:T(8,128)(2,1)} %bitcast.25, ...), custom_call_target="tpu_custom_call" | custom-call | tf_op jit(solution)/shard_map/attend/pallas_call | solution.py:740
  114.0 3.8 %prepare_mlp.1 = (bf16[384,1536]{1,0:T(8,128)(2,1)}, bf16[1536,384]{1,0:T(8,128)(2,1)}, f32[8,1536]{1,0:T(8,128)}) custom-call(bf16[32,304,128]{2,1,0:T(8,128)(2,1)} %get-tuple-element.48.blocks), custom_call_target="tpu_custom_call" | custom-call | tf_op jit(solution)/shard_map/prepare_mlp/pallas_call | solution.py:540
  117.9 47.9 %mlp.1 = (bf16[3136,384]{1,0:T(8,128)(2,1)}, f32[3136,384]{1,0:T(8,128)}, bf16[3136,384]{1,0:T(8,128)(2,1)}, f32[384,1536]{1,0:T(8,128)}, f32[384,1536]{1,0:T(8,...) custom-call(bf16[3136,384]{1,0:T(8,128)(2,1)} %get-tuple-element.45.cot_ref, bf16[3136,384]{1,0:T(8,128)(2,1)} %bitcast.19, ...), custom_call_target="tpu_custom_call" | custom-call | tf_op jit(solution)/shard_map/mlp/pallas_call | solution.py:864
  165.8 5.1 %pack_mlp.1.blocks = bf16[32,304,128]{2,1,0:T(8,128)(2,1)} custom-call(f32[384,1536]{1,0:T(8,128)} %get-tuple-element.56.g_w1, f32[384,1536]{1,0:T(8,128)} %get-tuple-element.57.g_w2t, f32[8,1536]{1,0:T(8,128)} %get-tuple-element.58.g_vec.g_vec2), custom_call_target="tpu_custom_call" | custom-call | tf_op jit(solution)/shard_map/pack_mlp/pallas_call | solution.py:1187
  170.9 0.0 copy-start.1
  170.9 0.0 copy-start.3
  170.9 0.0 copy-start.4
  170.9 67.3 %attend_back.1 = (f32[12,2,192,128]{3,2,1,0:T(8,128)}, f32[384,1152]{1,0:T(8,128)}, f32[8,1152]{1,0:T(8,128)}, bf16[4,208,384]{2,1,0:T(8,128)(2,1)}, f32[304,128...) custom-call(bf16[16,256,1152]{2,1,0:T(8,128)(2,1)} %get-tuple-element.44.ext, ...), custom_call_target="tpu_custom_call" | custom-call | tf_op jit(solution)/shard_map/attend_back/pallas_call | solution.py:1093
  238.2 0.0 copy-done.1
  238.2 0.0 copy-done.3
  238.2 0.0 copy-done.4
  238.2 1.8 multiply_subtract_fusion
  239.9 10.9 %pack.1.blocks = bf16[32,160,128]{2,1,0:T(8,128)(2,1)} custom-call(bf16[14,384,384]{2,1,0:T(8,128)(2,1)} %constant.14.clone.one_fine, bf16[14,256,128]{2,1,0:T(8,128)(2,1)} %constant.15.clone.one_coarse, f32[12,2,192,128]{3,2,1,0:T(8,128)} %get-tuple-element.61.g_bias, f32[384,1152]{1,0:T(8,128)} %get-tuple-element.62.g_qkv, ...), custom_call_target="tpu_custom_call" | custom-call | tf_op jit(solution)/shard_map/pack/pallas_call | solution.py:1259
  250.9 0.0 copy-start.2
  250.9 0.0 copy-start.5
  250.9 0.0 copy-start.6
  250.9 29.9 %sum_grads.1 = (f32[160,128]{1,0:T(8,128)}, bf16[4,784,384]{2,1,0:T(8,128)(2,1)}) custom-call(bf16[32,160,128]{2,1,0:T(8,128)(2,1)} %pack.1.blocks, bf16[4,208,384]{2,1,0:T(8,128)(2,1)} %get-tuple-element.65.last_ref, bf16[4,784,384]{2,1,0:T(8,128)(2,1)} %get-tuple-element.66.dx_ref), custom_call_target="tpu_custom_call", output_to_operand_aliasing={{1}: (2, {})} | custom-call | tf_op jit(solution)/shard_map/sum_grads/pallas_call | solution.py:385
  280.8 0.0 copy-done.2
  280.8 0.0 copy-done.5
  280.8 0.0 copy-done.6
  280.8 1.6 multiply_subtract_fusion.1
  282.4 0.0 copy-start
  282.4 4.4 %bitcast_convert_fusion = f32[1,3136,384]{2,1,0:T(8,128)} fusion(bf16[1,3136,384]{2,1,0:T(8,128)(2,1)} %bitcast.20), kind=kLoop, calls=%fused_computation | loop fusion | flops 1204224 | bytes 7225344 | tf_op jit(solution)/shard_map/convert_element_type | solution.py:1325
  286.8 0.0 copy-done
  286.8 1.4 copy.27
Async XLA Ops:
  170.9 67.3 %copy-start.1 = (f32[36952]{0:T(1024)S(1)}, f32[36952]{0:T(1024)}, u32[]{:S(2)}) copy-start(f32[36952]{0:T(1024)} %param.21) | copy-start | bytes 443428
  170.9 67.3 %copy-start.3 = (f32[36952]{0:T(1024)S(1)}, f32[36952]{0:T(1024)}, u32[]{:S(2)}) copy-start(f32[36952]{0:T(1024)} %param.23) | copy-start | bytes 443428
  170.9 67.3 %copy-start.4 = (f32[36952]{0:T(1024)S(1)}, f32[36952]{0:T(1024)}, u32[]{:S(2)}) copy-start(f32[36952]{0:T(1024)} %param.22) | copy-start | bytes 443428
  250.9 29.9 %copy-start.2 = (f32[18696]{0:T(1024)S(1)}, f32[18696]{0:T(1024)}, u32[]{:S(2)}) copy-start(f32[18696]{0:T(1024)} %param.18) | copy-start | bytes 224356
  250.9 29.9 %copy-start.5 = (f32[18696]{0:T(1024)S(1)}, f32[18696]{0:T(1024)}, u32[]{:S(2)}) copy-start(f32[18696]{0:T(1024)} %param.20) | copy-start | bytes 224356
  250.9 29.9 %copy-start.6 = (f32[18696]{0:T(1024)S(1)}, f32[18696]{0:T(1024)}, u32[]{:S(2)}) copy-start(f32[18696]{0:T(1024)} %param.19) | copy-start | bytes 224356
  282.4 4.4 %copy-start = (bf16[3136,384]{1,0:T(8,128)(2,1)S(1)}, bf16[3136,384]{1,0:T(8,128)(2,1)}, u32[]{:S(2)}) copy-start(bf16[3136,384]{1,0:T(8,128)(2,1)} %get-tuple-element.60) | copy-start | bytes 7225348

commit v4 on v3

--- a/solution.py
+++ b/solution.py
@@ -62,17 +62,14 @@
 
 @functools.cache
 def bias_tables():
-    fine = np.zeros((14, 384, 384), np.float32)
-    coarse = np.zeros((14, 256, 128), np.float32)
-    for qx in range(14):
-        for a in range(27):
-            for kx in range(14):
-                col = kx - qx + 9
-                if 4 <= a <= 22 and 0 <= col <= 18:
-                    fine[qx, 19 * (a - 4) + col, a * 14 + kx] = 1.0
-        for p in range(13):
-            for s in range(WIN):
-                coarse[qx, 13 * p + s - qx // 2 + 6, p * WIN + s] = 1.0
+    fine = np.zeros((384, 384), np.float32)
+    coarse = np.zeros((256, 128), np.float32)
+    for a in range(4, 23):
+        for kx in range(14):
+            fine[19 * (a - 4) + kx + 9, a * 14 + kx] = 1.0
+    for p in range(13):
+        for x in range(WIN):
+            coarse[13 * p + x + 6, p * WIN + x] = 1.0
     mask = np.zeros((2, KEYS, 128), np.float32)
     for half in range(2):
         for q in range(98):
@@ -121,10 +118,30 @@
         return jnp.pad(vector, (0, extra)).reshape(self.rows, 128)
 
 
+GATHER_STEPS = 16
+SUM_STEPS = 15
+
+
 def bit_order(n_dp, n_grp):
     dp_bits = [("dp", 2**b) for b in range(n_dp.bit_length() - 1)]
     grp_bits = [("grp", 2**b) for b in reversed(range(n_grp.bit_length() - 1))]
     return dp_bits[1:2] + grp_bits + dp_bits[2:] + dp_bits[:1]
+
+
+def stage_weights(order):
+    weights = []
+    for k, (axis, stride) in enumerate(order):
+        relative = 0.35 if (axis, stride) == ("dp", 1) else 2 if (axis == "grp" and stride > 1) else 1
+        weights.append(relative * 2**k)
+    return weights
+
+
+def starts_of(weights, steps):
+    done, starts = 0.0, []
+    for weight in weights:
+        starts.append(min(int(np.ceil(steps * done / sum(weights))), steps - 1))
+        done += weight
+    return starts
 
 
 def place_of(order, dp, grp):
@@ -477,12 +494,13 @@
     for t, h, length, row, lane, count in table_lines():
         line = jnp.concatenate([flat[row + c : row + c + 1, :] for c in range(count)], axis=1)
         (tab_fine, tab_coarse)[t][h : h + 1, 0:length] = line[:, lane : lane + length]
-    for qx in range(14):
-        at = slice(qx * 16, qx * 16 + 16)
-        moved = dot(tab_fine[...].astype(BF16), one_fine[qx])
-        for c in range(3):
-            shifted[c, at, :] = moved[:, c * 128 : (c + 1) * 128]
-        shifted[3, at, :] = dot(tab_coarse[...].astype(BF16), one_coarse[qx])
+    fine, coarse = tab_fine[...], tab_coarse[...]
+    fine = jnp.concatenate([pltpu.roll(fine, qx, 1) for qx in range(14)], axis=0)
+    coarse = jnp.concatenate([pltpu.roll(coarse, qx // 2, 1) for qx in range(14)], axis=0)
+    fine = dot(fine.astype(BF16), one_fine[...])
+    for c in range(3):
+        shifted[c] = fine[:, c * 128 : (c + 1) * 128]
+    shifted[3] = dot(coarse.astype(BF16), one_coarse[...])
     turned[...] = jnp.zeros_like(turned)
     for h in range(HEADS):
         table = jnp.concatenate(
@@ -575,11 +593,6 @@
     )
 
 
-def lane_heads(j):
-    lane = lax.broadcasted_iota(jnp.int32, (256, 128), 1)
-    return (lane // HDIM) == j
-
-
 def image_rows(ref, i, columns):
     at = pl.ds(pl.multiple_of(48 * i, 16), HALF)
     return jnp.concatenate([ref[w, at, columns] for w in range(4)], axis=0)
@@ -603,6 +616,12 @@
             pieces = [jnp.zeros((56, 128), F32)] + pieces
         columns.append(jnp.concatenate(pieces, axis=0))
     return jnp.concatenate(columns, axis=1).astype(BF16)
+
+
+def only_head(turned, h):
+    pieces = [jnp.zeros((HDIM, 256), BF16)] * 4
+    pieces[h % 4] = turned[h * HDIM : (h + 1) * HDIM, :]
+    return jnp.concatenate(pieces, axis=0)
 
 
 def half_of(values, half):
@@ -628,13 +647,15 @@
     query_back,
     mixed,
     probs,
-    ext,
+    query_out,
+    key_out,
+    value_out,
+    mixed_out,
     inverse,
     cot_out,
     blocks,
     normed,
     qkv,
-    mixed_t,
     own,
     own_sem,
     send,
@@ -657,9 +678,9 @@
         greet(cube_partners(order, dp, grp) + [window_partner(dp, grp, 3)])
         copy.wait()
 
-    for k in range(stages):
-
-        @pl.when(i == k * steps // stages)
+    for k, start in enumerate(starts_of(stage_weights(order), GATHER_STEPS)):
+
+        @pl.when(i == start)
         def _(k=k):
             if k:
                 gather_copy(order, k - 1, blocks, dp, grp, (send, recv)).wait()
@@ -670,42 +691,39 @@
         for c in exchange:
             c.start()
 
-        def project(w, carry):
-            step = rows // 7
-
-            def norm(c, inner):
-                at = pl.multiple_of(c * step, 16)
-                xhat, _ = norm_parts(x_buf[w, pl.ds(at, step), :].astype(F32))
-                normed[pl.ds(at, step), :] = (xhat * vecs[0:1, :D] + vecs[1:2, :D]).astype(BF16)
-                return inner
-
-            lax.fori_loop(0, 7, norm, 0)
-            q = dot(normed[...], wqkv[:, :D]) + vecs[2:3, :D]
+        step = rows // 7
+
+        def norm(w):
+            for c in range(7):
+                at = slice(c * step, (c + 1) * step)
+                xhat, _ = norm_parts(x_buf[w, at, :].astype(F32))
+                normed[w % 2, at, :] = (xhat * vecs[0:1, :] + vecs[1:2, :]).astype(BF16)
+
+        norm(0)
+        for w in range(4):
+            q = dot(normed[w % 2], wqkv[:, :D]) + vecs[2:3, :]
             qkv[w, :, :D] = (q * HDIM ** (-0.5)).astype(BF16)
-            qkv[w, :, D : 2 * D] = dot(normed[...], wqkv[:, D : 2 * D]).astype(BF16)
-            v = dot(normed[...], wqkv[:, 2 * D :]) + vecs[3:4, :D]
+            if w < 3:
+                norm(w + 1)
+            qkv[w, :, D : 2 * D] = dot(normed[w % 2], wqkv[:, D : 2 * D]).astype(BF16)
+            v = dot(normed[w % 2], wqkv[:, 2 * D :]) + vecs[3:4, :]
             qkv[w, :, 2 * D :] = v.astype(BF16)
-            return carry
-
-        lax.fori_loop(0, 4, project, 0)
-
-    q_ext = dot(query_tab[0], image_rows(qkv, i, slice(0, D))).astype(BF16)
+
+    q_ext = dot(query_tab[0], image_rows(qkv, i, slice(0, D)))
     kv_ext = dot(keys_tab[0], image_rows(qkv, i, slice(D, 3 * D)))
+    q_t = q_ext.T.astype(BF16)
     k_ext = kv_ext[:, :D].astype(BF16)
-    v_ext = kv_ext[:, D:]
-    v_t = v_ext.T.astype(BF16)
-    ext[0, :, :D] = q_ext
-    ext[0, :, D : 2 * D] = k_ext
-    ext[0, :, 2 * D :] = v_ext.astype(BF16)
+    v_t = kv_ext[:, D:].T.astype(BF16)
+    query_out[0] = q_t
+    key_out[0] = kv_ext[:, :D].T.astype(BF16)
+    value_out[0] = kv_ext[:, D:].astype(BF16)
+    inverse[0, HEADS:16, :] = jnp.zeros((16 - HEADS, 256), F32)
 
     def scores_of(h):
-        q_head = jnp.where(lane_heads(h % 4), q_ext[:, tile_of(h)], 0)
-        return dot_t(k_ext[:, tile_of(h)], q_head)
-
-    inverse[0, HEADS:16, :] = jnp.zeros((16 - HEADS, 256), F32)
-    scores = scores_of(0)
-    for h in range(HEADS):
-        ahead = scores_of(h + 1) if h + 1 < HEADS else None
+        heads = jnp.concatenate([only_head(q_t, h), only_head(q_t, h + 1)], axis=1)
+        return dot(k_ext[:, tile_of(h)], heads)
+
+    def softmax(scores, h):
         halves, inverses = [], []
         for half in range(2):
             s = half_of(scores, half) + bias[h, half]
@@ -716,11 +734,25 @@
         inv = jnp.concatenate(inverses, axis=1)
         probs[0, h] = e
         inverse[0, h : h + 1, :] = inv
-        mixed_t[h * HDIM : (h + 1) * HDIM, :] = (
-            dot(v_t[h * HDIM : (h + 1) * HDIM, :], e) * inv
-        ).astype(BF16)
-        scores = ahead
-    put_image_rows(mixed, i, slice(0, D), dot_t(query_back[0], mixed_t[...]))
+        return e, inv
+
+    def mix(h, e, inv):
+        own = slice(h * HDIM, (h + 1) * HDIM)
+        mixed_out[0, own, :] = (dot(v_t[own, :], e) * inv).astype(BF16)
+
+    ahead = scores_of(0)
+    waiting = []
+    for h in range(0, HEADS, 2):
+        now = ahead
+        if h + 2 < HEADS:
+            ahead = scores_of(h + 2)
+        for c in range(2):
+            waiting.append((h + c, *softmax(now[:, c * 256 : (c + 1) * 256], h + c)))
+        while len(waiting) > 1:
+            mix(*waiting.pop(0))
+    for last in waiting:
+        mix(*last)
+    put_image_rows(mixed, i, slice(0, D), dot_t(query_back[0], mixed_out[0]))
 
     @pl.when(i == steps - 1)
     def _():
@@ -736,14 +768,18 @@
     keys_tab, query_tab, _, query_back = gather_tables(images)
     vm = pl.BlockSpec(memory_space=pltpu.VMEM)
     hbm = pl.BlockSpec(memory_space=pl.ANY)
-    table = pl.BlockSpec((1, 256, 256), lambda i: (i, 0, 0))
+    image = lambda *shape: pl.BlockSpec((1, *shape), lambda i: (i, 0, 0))
+    table = image(256, 256)
     return pl.pallas_call(
         functools.partial(attend_kernel, rows, part, order),
         grid=(images,),
         out_shape=[
             jax.ShapeDtypeStruct((4, rows, D), BF16),
             jax.ShapeDtypeStruct((images, HEADS, 256, 256), BF16),
-            jax.ShapeDtypeStruct((images, 256, 3 * D), BF16),
+            jax.ShapeDtypeStruct((images, D, 256), BF16),
+            jax.ShapeDtypeStruct((images, D, 256), BF16),
+            jax.ShapeDtypeStruct((images, 256, D), BF16),
+            jax.ShapeDtypeStruct((images, D, 256), BF16),
             jax.ShapeDtypeStruct((images, 16, 256), F32),
             jax.ShapeDtypeStruct((tokens, D), BF16),
             jax.ShapeDtypeStruct((part.devices, part.rows, 128), BF16),
@@ -752,15 +788,17 @@
         out_specs=[
             pl.BlockSpec((4, rows, D), lambda i: (0, 0, 0)),
             pl.BlockSpec((1, HEADS, 256, 256), lambda i: (i, 0, 0, 0)),
-            pl.BlockSpec((1, 256, 3 * D), lambda i: (i, 0, 0)),
-            pl.BlockSpec((1, 16, 256), lambda i: (i, 0, 0)),
+            image(D, 256),
+            image(D, 256),
+            image(256, D),
+            image(D, 256),
+            image(16, 256),
             hbm,
             hbm,
         ],
         scratch_shapes=[
-            pltpu.VMEM((rows, D), BF16),
+            pltpu.VMEM((2, rows, D), BF16),
             pltpu.VMEM((4, rows, 3 * D), BF16),
-            pltpu.VMEM((D, 256), BF16),
             pltpu.VMEM((part.rows, 128), BF16),
             pltpu.SemaphoreType.DMA,
             pltpu.SemaphoreType.DMA((stages,)),
@@ -884,12 +922,6 @@
 LAST = 208
 
 
-def head_tables():
-    lanes = np.arange(D) // HDIM
-    one = (np.arange(16)[:, None] == lanes[None, :]).astype(np.float32)
-    return np.concatenate([one, one], axis=0).astype(ml_dtypes.bfloat16)
-
-
 def split_float(values):
     high = values.astype(BF16)
     return high, (values - high.astype(F32)).astype(BF16)
@@ -898,12 +930,13 @@
 def attend_back_kernel(
     part,
     order,
-    ext,
+    q_ref,
+    k_ref,
+    v_ref,
+    mixed_ref,
     d_mixed,
-    mixed,
     probs,
     inverse,
-    head_tab,
     keys_back,
     query_tab,
     query_back,
@@ -921,7 +954,7 @@
     out_ref,
     dx_ref,
     d_query_t,
-    d_key_value,
+    d_key_value_t,
     d_qkv,
     d_in,
     x_buf,
@@ -973,9 +1006,10 @@
         g_vec[...] = jnp.zeros_like(g_vec)
         greet(cube_partners(order, dp, grp) + [window_partner(dp, grp, 3)])
 
-    for k in reversed(range(stages)):
-
-        @pl.when(i == (stages - 1 - k) * steps // stages)
+    starts = starts_of(stage_weights(order)[::-1], SUM_STEPS)
+    for k, start in zip(reversed(range(stages)), starts):
+
+        @pl.when(i == start)
         def _(k=k):
             if k < stages - 1:
                 cube.finish(k + 1)
@@ -986,52 +1020,53 @@
         for c in exchange:
             c.start()
 
-    inv = inverse[0]
-    inv_high, inv_low = split_float(inv)
-    inv_t = jnp.concatenate([inv_high, inv_low], axis=0).astype(F32).T.astype(BF16)
-    dm_rows = image_rows(d_mixed, i, slice(0, D))
-    dm_ext = dot(query_tab[0], dm_rows) * dot(inv_t, head_tab[...])
-    mixed_ext = dot(query_tab[0], image_rows(mixed, i, slice(0, D)))
-    dm_ext = dm_ext.astype(BF16)
-    high, low = split_float(dm_ext.astype(F32) * mixed_ext)
-    sums = dot_t(head_tab[0:16, :], high) + dot_t(head_tab[0:16, :], low)
-    q_ext = ext[0, :, :D]
-    k_t = ext[0, :, D : 2 * D].astype(F32).T.astype(BF16)
-    v_ext = ext[0, :, 2 * D :]
-
-    def head_inputs(h):
-        mine = lane_heads(h % 4)
-        q_head = jnp.where(mine, q_ext[:, tile_of(h)], 0)
-        dm_head = jnp.where(mine, dm_ext[:, tile_of(h)], 0)
-        return q_head, dm_head, dot_t(v_ext[:, tile_of(h)], dm_head)
-
-    current = head_inputs(0)
-    for h in range(HEADS):
-        q_head, dm_head, d_probs = current
-        if h + 1 < HEADS:
-            current = head_inputs(h + 1)
-        if h % 4 == 0:
-            d_key = jnp.zeros((256, 128), F32)
-            d_value = jnp.zeros((256, 128), F32)
+    dm_t = dot(query_tab[0], image_rows(d_mixed, i, slice(0, D))).T
+    spread_heads = lambda ref: jnp.concatenate(
+        [jnp.broadcast_to(ref[h : h + 1], (HDIM, 256)) for h in range(HEADS)], axis=0
+    )
+    dm_t = (dm_t * spread_heads(inverse[0])).astype(BF16)
+    products = dm_t.astype(F32) * mixed_ref[0].astype(F32)
+    q_t, k_t, v_ext = q_ref[0], k_ref[0], v_ref[0]
+
+    def d_probs_of(h):
+        heads = jnp.concatenate([only_head(dm_t, h), only_head(dm_t, h + 1)], axis=1)
+        return dot(v_ext[:, tile_of(h)], heads)
+
+    def softmax_back(d_probs, h):
         e = probs[0, h]
-        d_value += dot(e, dm_head)
+        own = slice(h * HDIM, (h + 1) * HDIM)
+        sums = jnp.sum(products[own], axis=0, keepdims=True)
         halves = []
         for half in range(2):
             lanes = slice(128 * half, 128 * half + 128)
             e32 = e[:, lanes].astype(F32)[56 * half : 56 * half + KEYS]
-            ds = e32 * (half_of(d_probs, half) - sums[h : h + 1, lanes])
+            ds = e32 * (half_of(d_probs, half) - sums[:, lanes])
             g_bias[h, half] += ds
             halves.append(ds)
-        ds = spread(halves)
-        d_key += dot(ds, q_head)
-        d_query_t[h * HDIM : (h + 1) * HDIM, :] = (
-            dot(k_t[h * HDIM : (h + 1) * HDIM, :], ds) * HDIM ** (-0.5)
+        return spread(halves)
+
+    def gather_back(h, ds):
+        own = slice(h * HDIM, (h + 1) * HDIM)
+        d_query_t[own, :] = (dot(k_t[own, :], ds) * HDIM ** (-0.5)).astype(BF16)
+        d_key_value_t[own, :] = dot_t(q_t[own, :], ds).astype(BF16)
+        d_key_value_t[D + h * HDIM : D + (h + 1) * HDIM, :] = dot_t(
+            dm_t[own, :], probs[0, h]
         ).astype(BF16)
-        if h % 4 == 3:
-            d_key_value[:, tile_of(h)] = d_key.astype(BF16)
-            d_key_value[:, D + h // 4 * 128 : D + h // 4 * 128 + 128] = d_value.astype(BF16)
+
+    ahead = d_probs_of(0)
+    waiting = []
+    for h in range(0, HEADS, 2):
+        now = ahead
+        if h + 2 < HEADS:
+            ahead = d_probs_of(h + 2)
+        for c in range(2):
+            waiting.append((h + c, softmax_back(now[:, c * 256 : (c + 1) * 256], h + c)))
+        while len(waiting) > 1:
+            gather_back(*waiting.pop(0))
+    for last in waiting:
+        gather_back(*last)
     put_image_rows(d_qkv, i, slice(0, D), dot_t(query_back[0], d_query_t[...]))
-    put_image_rows(d_qkv, i, slice(D, 3 * D), dot(keys_back[0], d_key_value[...]))
+    put_image_rows(d_qkv, i, slice(D, 3 * D), dot_t(keys_back[0], d_key_value_t[...]))
 
     @pl.when(i == 3)
     def _():
@@ -1079,16 +1114,17 @@
 
 
 def attend_back(
-    part, order, ext, d_mixed, mixed, probs, inverse, x, d_res, wqkv, vecs, blocks, out
+    part, order, saved, d_mixed, probs, inverse, x, d_res, wqkv, vecs, blocks, out
 ):
-    images = ext.shape[0]
+    images = probs.shape[0]
     tokens = out.shape[0]
     rows = tokens // 4
     stages = len(order)
     _, query_tab, keys_back, query_back = gather_tables(images)
     vm = pl.BlockSpec(memory_space=pltpu.VMEM)
     hbm = pl.BlockSpec(memory_space=pl.ANY)
-    table = pl.BlockSpec((1, 256, 256), lambda i: (i, 0, 0))
+    image = lambda *shape: pl.BlockSpec((1, *shape), lambda i: (i, 0, 0))
+    table = image(256, 256)
     by_window = lambda array: array.reshape(4, rows, -1)
     outs = pl.pallas_call(
         functools.partial(attend_back_kernel, part, order),
@@ -1103,12 +1139,13 @@
             jax.ShapeDtypeStruct((4, rows, D), BF16),
         ],
         in_specs=[
-            pl.BlockSpec((1, 256, 3 * D), lambda i: (i, 0, 0)),
-            vm,
+            image(D, 256),
+            image(D, 256),
+            image(256, D),
+            image(D, 256),
             vm,
             pl.BlockSpec((1, HEADS, 256, 256), lambda i: (i, 0, 0, 0)),
-            pl.BlockSpec((1, 16, 256), lambda i: (i, 0, 0)),
-            vm,
+            image(16, 256),
         ]
         + [table] * 3
         + [hbm, hbm, vm, vm, vm, hbm],
@@ -1123,7 +1160,7 @@
         ],
         scratch_shapes=[
             pltpu.VMEM((D, 256), BF16),
-            pltpu.VMEM((256, 2 * D), BF16),
+            pltpu.VMEM((2 * D, 256), BF16),
             pltpu.VMEM((4, rows, 3 * D), BF16),
             pltpu.VMEM((4, rows, D), BF16),
             pltpu.VMEM((4, rows, D), BF16),
@@ -1142,12 +1179,10 @@
         ),
         name="attend_back",
     )(
-        ext,
+        *saved,
         by_window(d_mixed),
-        by_window(mixed),
         probs,
         inverse,
-        jnp.asarray(head_tables()),
         keys_back,
         query_tab,
         query_back,
@@ -1236,15 +1271,16 @@
                     ]
         for c in range(4):
             shifted[c, pl.ds(h, 14, stride=16), :] = table[0:14, c * 128 : (c + 1) * 128]
+    high, low = split_float(jnp.concatenate([shifted[c] for c in range(3)], axis=1))
+    moved_fine = dot_t(high, one_fine[...]) + dot_t(low, one_fine[...])
+    high, low = split_float(shifted[3])
+    moved_coarse = dot_t(high, one_coarse[...]) + dot_t(low, one_coarse[...])
     g_fine = jnp.zeros((16, 384), F32)
     g_coarse = jnp.zeros((16, 256), F32)
     for qx in range(14):
         at = slice(qx * 16, qx * 16 + 16)
-        gathered = jnp.concatenate([shifted[c, at, :] for c in range(4)], axis=1)
-        high = gathered.astype(BF16)
-        low = (gathered - high.astype(F32)).astype(BF16)
-        g_fine += dot_t(high[:, :384], one_fine[qx]) + dot_t(low[:, :384], one_fine[qx])
-        g_coarse += dot_t(high[:, 384:], one_coarse[qx]) + dot_t(low[:, 384:], one_coarse[qx])
+        g_fine += pltpu.roll(moved_fine[at], (384 - qx) % 384, 1)
+        g_coarse += pltpu.roll(moved_coarse[at], (256 - qx // 2) % 256, 1)
     for t, h, length, row, lane, count in table_lines():
         line[...] = jnp.zeros_like(line)
         line[0:1, lane : lane + length] = (g_fine, g_coarse)[t][h : h + 1, :length]
@@ -1294,7 +1330,7 @@
     images = tokens.shape[1] // 4 // SEQ
     blocks_a, x = gather_params(part_a, order, attn_master, tokens[0])
     wqkv, wproj, vecs_a, bias = prepare(part_a, places, blocks_a)
-    mixed, probs, ext, inverse, cot, blocks_b = attend(
+    mixed, probs, *saved, inverse, cot, blocks_b = attend(
         part_b, order, x, cotangent[0], mlp_master, wqkv, vecs_a, bias, images
     )
     mixed = mixed.reshape(-1, D)
@@ -1306,9 +1342,8 @@
     g_bias, g_qkv, g_vec1, dx_last, grad_b, output, dx = attend_back(
         part_b,
         order,
-        ext,
+        saved,
         d_mixed,
-        mixed,
         probs,
         inverse,
         x,

time: 289 us -> 258 us (0.89)
  Pallas kernels: 275 us -> 245 us
    pallas_call x1, Pallas kernels: 67.8 us -> 50.6 us  [attend(): pl.pallas_call(functools.partial(attend_kernel, rows, part, order), grid=...]
    pallas_call x1, Pallas kernels: 67.3 us -> 62.4 us  [attend_back(): pl.pallas_call(functools.partial(attend_back_kernel, part, order), grid=(...]
    pallas_call x1, Pallas kernels: 10.9 us -> 7.22 us  [pack(): pl.pallas_call(functools.partial(pack_kernel, part, places), out_shape=ja...]
where the time goes in v4:
time: 258 us
  Pallas kernels  245 us (95%)
  other arithmetic  7.71 us (3%)
  local copies, waits for them, and re-layouts  4.56 us (2%)
    pallas_call x1, Pallas kernels, attend_back(): pl.pallas_call(functools.partial(attend_back_kernel, part, order), grid=(...  62.4 us
    pallas_call x1, Pallas kernels, attend(): pl.pallas_call(functools.partial(attend_kernel, rows, part, order), grid=...  50.6 us
    pallas_call x1, Pallas kernels, mlp(): pl.pallas_call(mlp_kernel, grid=(7,), out_shape=[jax.ShapeDtypeStruct((to...  48.1 us
    pallas_call x1, Pallas kernels, gather_params(): pl.pallas_call(functools.partial(gather_kernel, part, order), out_shape=[...  34.1 us
    pallas_call x1, Pallas kernels, sum_grads(): pl.pallas_call(functools.partial(sum_kernel, part, order), out_shape=[jax...  27.1 us
    pallas_call x1, Pallas kernels, pack(): pl.pallas_call(functools.partial(pack_kernel, part, places), out_shape=ja...  7.22 us
    pallas_call x1, Pallas kernels, prepare(): pl.pallas_call(functools.partial(prep_kernel, part, places), out_shape=[j...  6.63 us

profile of v4, /device:TPU:0, one launch (start us, length us, event | category | flops | bytes accessed | tf_op | source)
XLA Modules:
  0.0 258.1 jit_solution(11503055138833071208)
XLA Ops:
  0.6 1.5 pad_bitcast_fusion.1.a_ref
  2.2 1.6 pad_bitcast_fusion.master_ref
  3.7 34.1 %gather_params.1 = (bf16[32,160,128]{2,1,0:T(8,128)(2,1)}, bf16[3136,384]{1,0:T(8,128)(2,1)}) custom-call(f32[160,128]{1,0:T(8,128)} %pad_bitcast_fusion.1.a_ref, bf16[3136,384]{1,0:T(8,128)(2,1)} %bitcast.21), custom_call_target="tpu_custom_call" | custom-call | tf_op jit(solution)/shard_map/gather_params/pallas_call | solution.py:315
  37.8 6.6 %prepare.1 = (bf16[384,1152]{1,0:T(8,128)(2,1)}, bf16[384,384]{1,0:T(8,128)(2,1)}, f32[8,384]{1,0:T(8,128)}, f32[12,2,192,128]{3,2,1,0:T(8,128)}) custom-call(bf16[32,160,128]{2,1,0:T(8,128)(2,1)} %get-tuple-element.43.blocks, bf16[384,384]{1,0:T(8,128)(2,1)} %constant.13.clone.one_fine, bf16[256,128]{1,0:T(8,128)(2,1)} %constant.14.clone.one_coarse, ...), custom_call_target="tpu_custom_call" | custom-call | tf_op jit(solution)/shard_map/prepare/pallas_call | solution.py:521
  44.5 50.6 %attend.1 = (bf16[4,784,384]{2,1,0:T(8,128)(2,1)}, bf16[16,12,256,256]{3,2,1,0:T(8,128)(2,1)}, bf16[16,384,256]{2,1,0:T(8,128)(2,1)}, bf16[16,384,256]{2,1,0:T(8...) custom-call(bf16[4,784,384]{2,1,0:T(8,128)(2,1)} %bitcast.17, ...), custom_call_target="tpu_custom_call" | custom-call | tf_op jit(solution)/shard_map/attend/pallas_call | solution.py:773
  95.1 3.9 %prepare_mlp.1 = (bf16[384,1536]{1,0:T(8,128)(2,1)}, bf16[1536,384]{1,0:T(8,128)(2,1)}, f32[8,1536]{1,0:T(8,128)}) custom-call(bf16[32,304,128]{2,1,0:T(8,128)(2,1)} %get-tuple-element.54.blocks), custom_call_target="tpu_custom_call" | custom-call | tf_op jit(solution)/shard_map/prepare_mlp/pallas_call | solution.py:558
  98.9 48.1 %mlp.1 = (bf16[3136,384]{1,0:T(8,128)(2,1)}, f32[3136,384]{1,0:T(8,128)}, bf16[3136,384]{1,0:T(8,128)(2,1)}, f32[384,1536]{1,0:T(8,128)}, f32[384,1536]{1,0:T(8,...) custom-call(bf16[3136,384]{1,0:T(8,128)(2,1)} %get-tuple-element.51.cot_ref, bf16[3136,384]{1,0:T(8,128)(2,1)} %bitcast.24, ...), custom_call_target="tpu_custom_call" | custom-call | tf_op jit(solution)/shard_map/mlp/pallas_call | solution.py:902
  147.1 5.1 %pack_mlp.1.blocks = bf16[32,304,128]{2,1,0:T(8,128)(2,1)} custom-call(f32[384,1536]{1,0:T(8,128)} %get-tuple-element.62.g_w1, f32[384,1536]{1,0:T(8,128)} %get-tuple-element.63.g_w2t, f32[8,1536]{1,0:T(8,128)} %get-tuple-element.64.g_vec.g_vec2), custom_call_target="tpu_custom_call" | custom-call | tf_op jit(solution)/shard_map/pack_mlp/pallas_call | solution.py:1222
  152.2 0.0 copy-start.1
  152.2 0.0 copy-start.3
  152.2 0.0 copy-start.4
  152.2 62.4 %attend_back.1 = (f32[12,2,192,128]{3,2,1,0:T(8,128)}, f32[384,1152]{1,0:T(8,128)}, f32[8,1152]{1,0:T(8,128)}, bf16[4,208,384]{2,1,0:T(8,128)(2,1)}, f32[304,128...) custom-call(bf16[16,384,256]{2,1,0:T(8,128)(2,1)} %get-tuple-element.47.q_ref, ...), custom_call_target="tpu_custom_call" | custom-call | tf_op jit(solution)/shard_map/attend_back/pallas_call | solution.py:1129
  214.5 0.0 copy-done.1
  214.5 0.0 copy-done.3
  214.6 0.0 copy-done.4
  214.6 1.8 multiply_subtract_fusion
  216.3 7.2 %pack.1.blocks = bf16[32,160,128]{2,1,0:T(8,128)(2,1)} custom-call(bf16[384,384]{1,0:T(8,128)(2,1)} %constant.13.clone.one_fine, bf16[256,128]{1,0:T(8,128)(2,1)} %constant.14.clone.one_coarse, f32[12,2,192,128]{3,2,1,0:T(8,128)} %get-tuple-element.67.g_bias, f32[384,1152]{1,0:T(8,128)} %get-tuple-element.68.g_qkv, f32[8,1152]{1,0:T(8,128)} %get-tuple-element.69.g_vec1, ...), custom_call_target="tpu_custom_call" | custom-call | tf_op jit(solution)/shard_map/pack/pallas_call | solution.py:1295
  223.5 0.0 copy-start.2
  223.5 0.0 copy-start.5
  223.5 0.0 copy-start.6
  223.6 27.1 %sum_grads.1 = (f32[160,128]{1,0:T(8,128)}, bf16[4,784,384]{2,1,0:T(8,128)(2,1)}) custom-call(bf16[32,160,128]{2,1,0:T(8,128)(2,1)} %pack.1.blocks, bf16[4,208,384]{2,1,0:T(8,128)(2,1)} %get-tuple-element.71.last_ref, bf16[4,784,384]{2,1,0:T(8,128)(2,1)} %get-tuple-element.72.dx_ref), custom_call_target="tpu_custom_call", output_to_operand_aliasing={{1}: (2, {})} | custom-call | tf_op jit(solution)/shard_map/sum_grads/pallas_call | solution.py:402
  250.7 0.0 copy-done.2
  250.7 0.0 copy-done.5
  250.7 0.0 copy-done.6
  250.7 1.6 multiply_subtract_fusion.1
  252.3 0.0 copy-start
  252.3 4.4 %bitcast_convert_fusion = f32[1,3136,384]{2,1,0:T(8,128)} fusion(bf16[1,3136,384]{2,1,0:T(8,128)(2,1)} %bitcast.19), kind=kLoop, calls=%fused_computation | loop fusion | flops 1204224 | bytes 7225344 | tf_op jit(solution)/shard_map/convert_element_type | solution.py:1360
  256.6 0.0 copy-done
  256.6 1.4 copy.26
Async XLA Ops:
  152.2 62.4 %copy-start.1 = (f32[36952]{0:T(1024)S(1)}, f32[36952]{0:T(1024)}, u32[]{:S(2)}) copy-start(f32[36952]{0:T(1024)} %param.20) | copy-start | bytes 443428
  152.2 62.4 %copy-start.3 = (f32[36952]{0:T(1024)S(1)}, f32[36952]{0:T(1024)}, u32[]{:S(2)}) copy-start(f32[36952]{0:T(1024)} %param.22) | copy-start | bytes 443428
  152.2 62.4 %copy-start.4 = (f32[36952]{0:T(1024)S(1)}, f32[36952]{0:T(1024)}, u32[]{:S(2)}) copy-start(f32[36952]{0:T(1024)} %param.21) | copy-start | bytes 443428
  223.5 27.1 %copy-start.2 = (f32[18696]{0:T(1024)S(1)}, f32[18696]{0:T(1024)}, u32[]{:S(2)}) copy-start(f32[18696]{0:T(1024)} %param.17) | copy-start | bytes 224356
  223.5 27.1 %copy-start.5 = (f32[18696]{0:T(1024)S(1)}, f32[18696]{0:T(1024)}, u32[]{:S(2)}) copy-start(f32[18696]{0:T(1024)} %param.19) | copy-start | bytes 224356
  223.5 27.1 %copy-start.6 = (f32[18696]{0:T(1024)S(1)}, f32[18696]{0:T(1024)}, u32[]{:S(2)}) copy-start(f32[18696]{0:T(1024)} %param.18) | copy-start | bytes 224356
  252.3 4.4 %copy-start = (bf16[3136,384]{1,0:T(8,128)(2,1)S(1)}, bf16[3136,384]{1,0:T(8,128)(2,1)}, u32[]{:S(2)}) copy-start(bf16[3136,384]{1,0:T(8,128)(2,1)} %get-tuple-element.66) | copy-start | bytes 7225348

commit v5 on v4

--- a/solution.py
+++ b/solution.py
@@ -118,7 +118,7 @@
         return jnp.pad(vector, (0, extra)).reshape(self.rows, 128)
 
 
-GATHER_STEPS = 16
+GATHER_STEPS = 12
 SUM_STEPS = 15
 
 
@@ -227,11 +227,6 @@
     return cube_copy(order, k, held, held, dp, grp, *sems)
 
 
-def own_block(part, master_ref, own):
-    device = lax.axis_index("dp") * lax.axis_size("grp") + lax.axis_index("grp")
-    own[...] = shift_lanes(master_ref[...], part.lane(device), True).astype(BF16)
-
-
 class CubeSum:
     def __init__(self, order, blocks, total, outgoing, arrived, sems):
         self.order, self.blocks, self.total = order, blocks, total
@@ -287,56 +282,6 @@
             pltpu.SemaphoreType.DMA((stages,)),
             pltpu.SemaphoreType.DMA((stages,)),
         ]
-
-
-def gather_kernel(
-    part, order, a_ref, tok_ref, out_ref, x_ref, own, own_sem, send, recv, x_sem, x_send, x_recv
-):
-    dp, grp = lax.axis_index("dp"), lax.axis_index("grp")
-    own_block(part, a_ref, own)
-    copy = pltpu.make_async_copy(own, out_ref.at[place_of(order, dp, grp)], own_sem)
-    copy.start()
-    greet(cube_partners(order, dp, grp) + [window_partner(dp, grp, 3)])
-    copy.wait()
-    exchange = exchange_copies(tok_ref, x_ref, dp, grp, x_sem, x_send, x_recv)
-    for k in range(len(order)):
-        stage = gather_copy(order, k, out_ref, dp, grp, (send, recv))
-        stage.start()
-        if k == 0:
-            for c in exchange:
-                c.start()
-        stage.wait()
-    for c in exchange:
-        c.wait()
-
-
-def gather_params(part, order, master, tok):
-    stages = len(order)
-    return pl.pallas_call(
-        functools.partial(gather_kernel, part, order),
-        out_shape=[
-            jax.ShapeDtypeStruct((part.devices, part.rows, 128), BF16),
-            jax.ShapeDtypeStruct(tok.shape, BF16),
-        ],
-        in_specs=[
-            pl.BlockSpec(memory_space=pltpu.VMEM),
-            pl.BlockSpec(memory_space=pl.ANY),
-        ],
-        out_specs=[pl.BlockSpec(memory_space=pl.ANY)] * 2,
-        scratch_shapes=[
-            pltpu.VMEM((part.rows, 128), BF16),
-            pltpu.SemaphoreType.DMA,
-            pltpu.SemaphoreType.DMA((stages,)),
-            pltpu.SemaphoreType.DMA((stages,)),
-            pltpu.SemaphoreType.DMA,
-            pltpu.SemaphoreType.DMA((3,)),
-            pltpu.SemaphoreType.DMA((3,)),
-        ],
-        compiler_params=pltpu.CompilerParams(
-            collective_id=0, has_side_effects=True, vmem_limit_bytes=VMEM_LIMIT
-        ),
-        name="gather_params",
-    )(part.padded(master), tok)
 
 
 def chunk_copies(source, target, first, size, dp, grp, own_sem, send_sems, recv_sems, skip):
@@ -431,10 +376,12 @@
 
 
 def unflatten(part, places, blocks, flat):
-    flat[...] = jnp.zeros_like(flat)
     for device, place in enumerate(places):
         at = part.start(device)
-        flat[at : at + part.rows, :] += blocks[place].astype(F32)
+        block = blocks[place].astype(F32)
+        first = block[0:1] + flat[at : at + 1, :] if device else block[0:1]
+        flat[at : at + part.rows, :] = block
+        flat[at : at + 1, :] = first
 
 
 def take_matrix(flat, first, target):
@@ -463,27 +410,13 @@
             yield t, h, length, row, lane, -(-(lane + length) // 128)
 
 
-def prep_kernel(
-    part,
-    places,
-    blocks,
-    one_fine,
-    one_coarse,
-    mask_ref,
-    wqkv,
-    wproj,
-    vecs,
-    bias,
-    flat,
-    tab_fine,
-    tab_coarse,
-    shifted,
-    turned,
+def prepare(
+    part, places, blocks, one_fine, one_coarse, mask_ref,
+    wqkv, wproj, vecs, bias, flat, tab_fine, tab_coarse, shifted, turned,
 ):
     unflatten(part, places, blocks, flat)
     take_matrix(flat, 0, wqkv)
     take_matrix(flat, 3456, wproj)
-    vecs[...] = jnp.zeros_like(vecs)
     row, lane = divmod(ATTN_VECTORS[0], 128)
     rows = shift_lanes(flat[row : row + 16, :], lane, False)
     for v in range(5):
@@ -515,59 +448,129 @@
             bias[h, half] = turned[half].T[0:KEYS] + mask_ref[half]
 
 
-def prepare(part, places, blocks):
+def early_stages(order):
+    return 1 + sum(axis == "grp" for axis, _ in order)
+
+
+def gather_kernel(
+    part_a,
+    part_b,
+    order,
+    places,
+    a_ref,
+    b_ref,
+    one_fine,
+    one_coarse,
+    mask_ref,
+    tok_ref,
+    wqkv,
+    wproj,
+    vecs,
+    bias,
+    x_ref,
+    blocks_b,
+    blocks_a,
+    own,
+    flat,
+    tab_fine,
+    tab_coarse,
+    shifted,
+    turned,
+    own_sem,
+    send_a,
+    recv_a,
+    send_b,
+    recv_b,
+    x_sem,
+    x_send,
+    x_recv,
+):
+    dp, grp = lax.axis_index("dp"), lax.axis_index("grp")
+    place = place_of(order, dp, grp)
+    device = dp * lax.axis_size("grp") + grp
+    own[...] = shift_lanes(b_ref[...], part_b.lane(device), True).astype(BF16)
+    copy = pltpu.make_async_copy(own, blocks_b.at[place], own_sem)
+    copy.start()
+    blocks_a[place] = shift_lanes(a_ref[...], part_a.lane(device), True).astype(BF16)
+    vecs[...] = jnp.zeros_like(vecs)
+    greet(cube_partners(order, dp, grp) + [window_partner(dp, grp, 3)])
+    copy.wait()
+    exchange = exchange_copies(tok_ref, x_ref, dp, grp, x_sem, x_send, x_recv)
+    first = [
+        gather_copy(order, k, blocks_a, dp, grp, (send_a, recv_a)) for k in range(len(order))
+    ]
+    early = early_stages(order)
+    second = [gather_copy(order, k, blocks_b, dp, grp, (send_b, recv_b)) for k in range(early)]
+    for k, stage in enumerate(first):
+        stage.start()
+        if k == 0:
+            second[0].start()
+            for c in exchange:
+                c.start()
+        if early <= k < 2 * early:
+            second[k - early].wait()
+            if k - early + 1 < early:
+                second[k - early + 1].start()
+        stage.wait()
+    prepare(
+        part_a, places, blocks_a, one_fine, one_coarse, mask_ref,
+        wqkv, wproj, vecs, bias, flat, tab_fine, tab_coarse, shifted, turned,
+    )
+    for k in range(len(order) - early, early):
+        second[k].wait()
+        if k + 1 < early:
+            second[k + 1].start()
+    for c in exchange:
+        c.wait()
+
+
+def gather_params(part_a, part_b, order, places, master_a, master_b, tok):
+    stages = len(order)
+    early = early_stages(order)
     fine, coarse, mask = bias_tables()
     vm = pl.BlockSpec(memory_space=pltpu.VMEM)
+    hbm = pl.BlockSpec(memory_space=pl.ANY)
     return pl.pallas_call(
-        functools.partial(prep_kernel, part, places),
+        functools.partial(gather_kernel, part_a, part_b, order, places),
         out_shape=[
             jax.ShapeDtypeStruct((D, 3 * D), BF16),
             jax.ShapeDtypeStruct((D, D), BF16),
             jax.ShapeDtypeStruct((8, D), F32),
             jax.ShapeDtypeStruct((HEADS, 2, KEYS, 128), F32),
+            jax.ShapeDtypeStruct(tok.shape, BF16),
+            jax.ShapeDtypeStruct((part_b.devices, part_b.rows, 128), BF16),
         ],
-        in_specs=[vm] * 4,
-        out_specs=[vm] * 4,
+        in_specs=[vm] * 5 + [hbm],
+        out_specs=[vm] * 4 + [hbm] * 2,
         scratch_shapes=[
-            pltpu.VMEM((part.buffer, 128), F32),
+            pltpu.VMEM((part_a.devices, part_a.rows, 128), BF16),
+            pltpu.VMEM((part_b.rows, 128), BF16),
+            pltpu.VMEM((part_a.buffer, 128), F32),
             pltpu.VMEM((16, 384), F32),
             pltpu.VMEM((16, 256), F32),
             pltpu.VMEM((4, 14 * 16, 128), F32),
             pltpu.VMEM((2, 128, 256), F32),
+            pltpu.SemaphoreType.DMA,
+            pltpu.SemaphoreType.DMA((stages,)),
+            pltpu.SemaphoreType.DMA((stages,)),
+            pltpu.SemaphoreType.DMA((early,)),
+            pltpu.SemaphoreType.DMA((early,)),
+            pltpu.SemaphoreType.DMA,
+            pltpu.SemaphoreType.DMA((3,)),
+            pltpu.SemaphoreType.DMA((3,)),
         ],
-        compiler_params=pltpu.CompilerParams(vmem_limit_bytes=VMEM_LIMIT),
-        name="prepare",
-    )(blocks, jnp.asarray(fine), jnp.asarray(coarse), jnp.asarray(mask))
-
-
-def prep_mlp_kernel(part, places, blocks, w1, w2, vecs, flat):
-    unflatten(part, places, blocks, flat)
-    take_matrix(flat, 0, w1)
-    take_matrix(flat, 4608, w2)
-    vecs[...] = jnp.zeros_like(vecs)
-    for j in range(12):
-        vecs[0:1, j * 128 : (j + 1) * 128] = flat[9216 + j : 9217 + j, :]
-    for v in range(3):
-        for j in range(3):
-            at = 9228 + 3 * v + j
-            vecs[1 + v : 2 + v, j * 128 : (j + 1) * 128] = flat[at : at + 1, :]
-
-
-def prepare_mlp(part, places, blocks):
-    vm = pl.BlockSpec(memory_space=pltpu.VMEM)
-    return pl.pallas_call(
-        functools.partial(prep_mlp_kernel, part, places),
-        out_shape=[
-            jax.ShapeDtypeStruct((D, FF), BF16),
-            jax.ShapeDtypeStruct((FF, D), BF16),
-            jax.ShapeDtypeStruct((8, FF), F32),
-        ],
-        in_specs=[vm],
-        out_specs=[vm] * 3,
-        scratch_shapes=[pltpu.VMEM((part.buffer, 128), F32)],
-        compiler_params=pltpu.CompilerParams(vmem_limit_bytes=VMEM_LIMIT),
-        name="prepare_mlp",
-    )(blocks)
+        compiler_params=pltpu.CompilerParams(
+            collective_id=0, has_side_effects=True, vmem_limit_bytes=VMEM_LIMIT
+        ),
+        name="gather_params",
+    )(
+        part_a.padded(master_a),
+        part_b.padded(master_b),
+        jnp.asarray(fine),
+        jnp.asarray(coarse),
+        jnp.asarray(mask),
+        tok,
+    )
 
 
 def dot(a, b):
@@ -634,11 +637,10 @@
 
 def attend_kernel(
     rows,
-    part,
     order,
     x_buf,
     cot_ref,
-    master_ref,
+    blocks_in,
     wqkv,
     vecs,
     bias,
@@ -656,8 +658,6 @@
     blocks,
     normed,
     qkv,
-    own,
-    own_sem,
     send,
     recv,
     cot_sem,
@@ -668,23 +668,22 @@
     steps = pl.num_programs(0)
     dp, grp = lax.axis_index("dp"), lax.axis_index("grp")
     exchange = exchange_copies(cot_ref, cot_out, dp, grp, cot_sem, cot_send, cot_recv)
-    stages = len(order)
+    early = early_stages(order)
+    late = [
+        gather_copy(order, k, blocks, dp, grp, (send, recv)) for k in range(early, len(order))
+    ]
 
     @pl.when(i == 0)
     def _():
-        own_block(part, master_ref, own)
-        copy = pltpu.make_async_copy(own, blocks.at[place_of(order, dp, grp)], own_sem)
-        copy.start()
         greet(cube_partners(order, dp, grp) + [window_partner(dp, grp, 3)])
-        copy.wait()
-
-    for k, start in enumerate(starts_of(stage_weights(order), GATHER_STEPS)):
+
+    for k, start in enumerate(starts_of(stage_weights(order)[early:], GATHER_STEPS)):
 
         @pl.when(i == start)
         def _(k=k):
             if k:
-                gather_copy(order, k - 1, blocks, dp, grp, (send, recv)).wait()
-            gather_copy(order, k, blocks, dp, grp, (send, recv)).start()
+                late[k - 1].wait()
+            late[k].start()
 
     @pl.when(i == 0)
     def _():
@@ -756,12 +755,12 @@
 
     @pl.when(i == steps - 1)
     def _():
-        gather_copy(order, stages - 1, blocks, dp, grp, (send, recv)).wait()
+        late[-1].wait()
         for c in exchange:
             c.wait()
 
 
-def attend(part, order, x, cot, master, wqkv, vecs, bias, images):
+def attend(order, x, cot, blocks, wqkv, vecs, bias, images):
     tokens = x.shape[0]
     stages = len(order)
     rows = tokens // 4
@@ -771,7 +770,7 @@
     image = lambda *shape: pl.BlockSpec((1, *shape), lambda i: (i, 0, 0))
     table = image(256, 256)
     return pl.pallas_call(
-        functools.partial(attend_kernel, rows, part, order),
+        functools.partial(attend_kernel, rows, order),
         grid=(images,),
         out_shape=[
             jax.ShapeDtypeStruct((4, rows, D), BF16),
@@ -782,9 +781,9 @@
             jax.ShapeDtypeStruct((images, D, 256), BF16),
             jax.ShapeDtypeStruct((images, 16, 256), F32),
             jax.ShapeDtypeStruct((tokens, D), BF16),
-            jax.ShapeDtypeStruct((part.devices, part.rows, 128), BF16),
+            jax.ShapeDtypeStruct(blocks.shape, BF16),
         ],
-        in_specs=[vm, hbm] + [vm] * 4 + [table] * 3,
+        in_specs=[vm, hbm, hbm] + [vm] * 3 + [table] * 3,
         out_specs=[
             pl.BlockSpec((4, rows, D), lambda i: (0, 0, 0)),
             pl.BlockSpec((1, HEADS, 256, 256), lambda i: (i, 0, 0, 0)),
@@ -799,14 +798,13 @@
         scratch_shapes=[
             pltpu.VMEM((2, rows, D), BF16),
             pltpu.VMEM((4, rows, 3 * D), BF16),
-            pltpu.VMEM((part.rows, 128), BF16),
-            pltpu.SemaphoreType.DMA,
             pltpu.SemaphoreType.DMA((stages,)),
             pltpu.SemaphoreType.DMA((stages,)),
             pltpu.SemaphoreType.DMA,
             pltpu.SemaphoreType.DMA((3,)),
             pltpu.SemaphoreType.DMA((3,)),
         ],
+        input_output_aliases={2: 8},
         compiler_params=pltpu.CompilerParams(
             collective_id=2, has_side_effects=True, vmem_limit_bytes=VMEM_LIMIT
         ),
@@ -814,7 +812,7 @@
     )(
         x.reshape(4, rows, D),
         cot,
-        part.padded(master),
+        blocks,
         wqkv,
         vecs,
         bias,
@@ -828,56 +826,92 @@
 GELU_B = 0.044715
 
 
+def unpack_mlp(part, places, blocks, flat, w1, w2, vecs):
+    unflatten(part, places, blocks, flat)
+    take_matrix(flat, 0, w1)
+    take_matrix(flat, 4608, w2)
+    for j in range(12):
+        vecs[0:1, j * 128 : (j + 1) * 128] = flat[9216 + j : 9217 + j, :]
+    for v in range(3):
+        for j in range(3):
+            at = 9228 + 3 * v + j
+            vecs[1 + v : 2 + v, j * 128 : (j + 1) * 128] = flat[at : at + 1, :]
+
+
+def pack_mlp(part, places, g_w1, g_w2t, g_vec, flat, out):
+    put_matrix(flat, 0, g_w1)
+    for j in range(3):
+        flat[pl.ds(4608 + j, FF, stride=3), :] = g_w2t[j * 128 : (j + 1) * 128, :].T
+    for j in range(12):
+        flat[9216 + j : 9217 + j, :] = g_vec[0:1, j * 128 : (j + 1) * 128]
+    for v in range(3):
+        for j in range(3):
+            at = 9228 + 3 * v + j
+            flat[at : at + 1, :] = g_vec[1 + v : 2 + v, j * 128 : (j + 1) * 128]
+    flat[9237:, :] = jnp.zeros((flat.shape[0] - 9237, 128), F32)
+    to_blocks(part, places, flat, out)
+
+
 def mlp_kernel(
+    part,
+    places,
     cot_ref,
     mixed_ref,
     x_ref,
     wproj,
-    w1,
-    w2,
     vecs_a,
-    vecs,
+    blocks,
     out_ref,
     d_res_ref,
     d_mixed_ref,
+    sums,
+    g_proj,
+    g_vec,
+    w1,
+    w2,
+    vecs,
     g_w1,
     g_w2t,
-    g_proj,
-    g_vec,
+    flat,
 ):
     i = pl.program_id(0)
-    chunk = mixed_ref.shape[0]
 
     @pl.when(i == 0)
     def _():
+        unpack_mlp(part, places, blocks, flat, w1, w2, vecs)
         g_w1[...] = jnp.zeros_like(g_w1)
         g_w2t[...] = jnp.zeros_like(g_w2t)
         g_proj[...] = jnp.zeros_like(g_proj)
         g_vec[...] = jnp.zeros_like(g_vec)
 
     mix = mixed_ref[...]
+    grad = cot_ref[...]
+    columns = [slice(0, FF // 2), slice(FF // 2, FF)]
     res = x_ref[...].astype(F32) + dot(mix, wproj[...]) + vecs_a[4:5, :]
+    d_act = dot_t(grad, w2[columns[0], :])
     xhat, scale = norm_parts(res)
     gain = vecs[1:2, :D]
     normed = (xhat * gain + vecs[2:3, :D]).astype(BF16)
-    grad = cot_ref[...]
     grad_t = grad.T
     normed_t = normed.T
-    out = res + vecs[3:4, :D]
-    d_normed = jnp.zeros((chunk, D), F32)
-    for f in range(3):
-        cols = slice(f * 512, f * 512 + 512)
-        hidden = dot(normed, w1[:, cols]) + vecs[0:1, cols]
-        square = hidden * hidden
-        t = jnp.tanh(hidden * (GELU_A + (GELU_A * GELU_B) * square))
+    hidden = dot(normed, w1[:, columns[0]])
+    out, d_normed = res + vecs[3:4, :D], None
+    for f, cols in enumerate(columns):
+        value, d_value = hidden + vecs[0:1, cols], d_act
+        if f == 0:
+            hidden = dot(normed, w1[:, columns[f + 1]])
+            d_act = dot_t(grad, w2[columns[f + 1], :])
+        square = value * value
+        t = jnp.tanh(value * (GELU_A + (GELU_A * GELU_B) * square))
         half = 0.5 + 0.5 * t
-        act = (hidden * half).astype(BF16)
-        slope = half + (0.5 * hidden) * (1.0 - t * t) * (GELU_A + (3 * GELU_A * GELU_B) * square)
-        out += dot(act, w2[cols, :])
-        d_hidden32 = dot_t(grad, w2[cols, :]) * slope
+        act = (value * half).astype(BF16)
+        slope = half + (0.5 * value) * (1.0 - t * t) * (GELU_A + (3 * GELU_A * GELU_B) * square)
+        d_hidden32 = d_value * slope
         d_hidden = d_hidden32.astype(BF16)
         g_vec[0:1, cols] += jnp.sum(d_hidden32, axis=0, keepdims=True)
-        d_normed += dot_t(d_hidden, w1[:, cols])
+        out += dot(act, w2[cols, :])
+        back = dot_t(d_hidden, w1[:, cols])
+        d_normed = back if d_normed is None else d_normed + back
         g_w1[:, cols] += dot(normed_t, d_hidden)
         g_w2t[:, cols] += dot(grad_t, act)
     out_ref[...] = out.astype(BF16)
@@ -892,30 +926,41 @@
     g_vec[3:4, :D] += jnp.sum(grad32, axis=0, keepdims=True)
     g_vec[4:5, :D] += jnp.sum(d_res, axis=0, keepdims=True)
 
-
-def mlp(cot, mixed, x, wproj, w1, w2, vecs_a, vecs):
+    @pl.when(i == pl.num_programs(0) - 1)
+    def _():
+        pack_mlp(part, places, g_w1, g_w2t, g_vec, flat, sums)
+
+
+def mlp(part, places, cot, mixed, x, wproj, vecs_a, blocks):
     tokens = x.shape[0]
     chunk = tokens // 7
     vm = pl.BlockSpec(memory_space=pltpu.VMEM)
     tile = pl.BlockSpec((chunk, D), lambda i: (i, 0))
-    fixed = lambda *shape: pl.BlockSpec(shape, lambda i: (0, 0))
+    fixed = lambda *shape: pl.BlockSpec(shape, lambda i: (0,) * len(shape))
     return pl.pallas_call(
-        mlp_kernel,
+        functools.partial(mlp_kernel, part, places),
         grid=(7,),
         out_shape=[
             jax.ShapeDtypeStruct((tokens, D), BF16),
             jax.ShapeDtypeStruct((tokens, D), F32),
             jax.ShapeDtypeStruct((tokens, D), BF16),
-            jax.ShapeDtypeStruct((D, FF), F32),
-            jax.ShapeDtypeStruct((D, FF), F32),
+            jax.ShapeDtypeStruct((part.devices, part.rows, 128), BF16),
             jax.ShapeDtypeStruct((D, D), F32),
             jax.ShapeDtypeStruct((8, FF), F32),
         ],
-        in_specs=[tile] * 3 + [vm] * 5,
-        out_specs=[tile] * 3 + [fixed(D, FF), fixed(D, FF), fixed(D, D), fixed(8, FF)],
+        in_specs=[tile] * 3 + [vm] * 3,
+        out_specs=[tile] * 3 + [fixed(part.devices, part.rows, 128), fixed(D, D), fixed(8, FF)],
+        scratch_shapes=[
+            pltpu.VMEM((D, FF), BF16),
+            pltpu.VMEM((FF, D), BF16),
+            pltpu.VMEM((8, FF), F32),
+            pltpu.VMEM((D, FF), F32),
+            pltpu.VMEM((D, FF), F32),
+            pltpu.VMEM((part.buffer, 128), F32),
+        ],
         compiler_params=pltpu.CompilerParams(vmem_limit_bytes=VMEM_LIMIT),
         name="mlp",
-    )(cot, mixed, x, wproj, w1, w2, vecs_a, vecs)
+    )(cot, mixed, x, wproj, vecs_a, blocks)
 
 
 CHUNK = 192
@@ -1203,33 +1248,6 @@
         out[place] = flat[at : at + part.rows, :].astype(BF16)
 
 
-def pack_mlp_kernel(part, places, g_w1, g_w2t, g_vec, out, flat):
-    flat[...] = jnp.zeros_like(flat)
-    put_matrix(flat, 0, g_w1)
-    for j in range(3):
-        flat[pl.ds(4608 + j, FF, stride=3), :] = g_w2t[j * 128 : (j + 1) * 128, :].T
-    for j in range(12):
-        flat[9216 + j : 9217 + j, :] = g_vec[0:1, j * 128 : (j + 1) * 128]
-    for v in range(3):
-        for j in range(3):
-            at = 9228 + 3 * v + j
-            flat[at : at + 1, :] = g_vec[1 + v : 2 + v, j * 128 : (j + 1) * 128]
-    to_blocks(part, places, flat, out)
-
-
-def pack_mlp(part, places, g_w1, g_w2t, g_vec):
-    vm = pl.BlockSpec(memory_space=pltpu.VMEM)
-    return pl.pallas_call(
-        functools.partial(pack_mlp_kernel, part, places),
-        out_shape=jax.ShapeDtypeStruct((part.devices, part.rows, 128), BF16),
-        in_specs=[vm] * 3,
-        out_specs=vm,
-        scratch_shapes=[pltpu.VMEM((part.buffer, 128), F32)],
-        compiler_params=pltpu.CompilerParams(vmem_limit_bytes=VMEM_LIMIT),
-        name="pack_mlp",
-    )(g_w1, g_w2t, g_vec)
-
-
 def pack_kernel(
     part,
     places,
@@ -1328,17 +1346,16 @@
     part_a = Part(n_dp * n_grp, attn_master.shape[0])
     part_b = Part(n_dp * n_grp, mlp_master.shape[0])
     images = tokens.shape[1] // 4 // SEQ
-    blocks_a, x = gather_params(part_a, order, attn_master, tokens[0])
-    wqkv, wproj, vecs_a, bias = prepare(part_a, places, blocks_a)
+    wqkv, wproj, vecs_a, bias, x, blocks_b = gather_params(
+        part_a, part_b, order, places, attn_master, mlp_master, tokens[0]
+    )
     mixed, probs, *saved, inverse, cot, blocks_b = attend(
-        part_b, order, x, cotangent[0], mlp_master, wqkv, vecs_a, bias, images
+        order, x, cotangent[0], blocks_b, wqkv, vecs_a, bias, images
     )
     mixed = mixed.reshape(-1, D)
-    w1, w2, vecs_b = prepare_mlp(part_b, places, blocks_b)
-    out, d_res, d_mixed, g_w1, g_w2t, g_proj, g_vec2 = mlp(
-        cot, mixed, x, wproj, w1, w2, vecs_a, vecs_b
-    )
-    sums_b = pack_mlp(part_b, places, g_w1, g_w2t, g_vec2)
+    out, d_res, d_mixed, sums_b, g_proj, g_vec2 = mlp(
+        part_b, places, cot, mixed, x, wproj, vecs_a, blocks_b
+    )
     g_bias, g_qkv, g_vec1, dx_last, grad_b, output, dx = attend_back(
         part_b,
         order,

time: 258 us -> 231 us (0.90)
  Pallas kernels: 245 us -> 218 us
    pallas_call x6 -> x3, Pallas kernels: 148 us -> 121 us  [the longest x1 44.8 us: mlp(): pl.pallas_call(functools.partial(mlp_kernel, part, places), grid=(7,), ou...]
where the time goes in v5:
time: 231 us
  Pallas kernels  218 us (94%)
  other arithmetic  7.71 us (3%)
  local copies, waits for them, and re-layouts  4.57 us (2%)
    pallas_call x1, Pallas kernels, attend_back(): pl.pallas_call(functools.partial(attend_back_kernel, part, order), grid=(...  61.6 us
    pallas_call x1, Pallas kernels, mlp(): pl.pallas_call(functools.partial(mlp_kernel, part, places), grid=(7,), ou...  44.8 us
    pallas_call x1, Pallas kernels, attend(): pl.pallas_call(functools.partial(attend_kernel, rows, order), grid=(image...  38.6 us
    pallas_call x1, Pallas kernels, gather_params(): pl.pallas_call(functools.partial(gather_kernel, part_a, part_b, order, pl...  37.7 us
    pallas_call x1, Pallas kernels, sum_grads(): pl.pallas_call(functools.partial(sum_kernel, part, order), out_shape=[jax...  28.3 us
    pallas_call x1, Pallas kernels, pack(): pl.pallas_call(functools.partial(pack_kernel, part, places), out_shape=ja...  7.22 us

profile of v5, /device:TPU:0, one launch (start us, length us, event | category | flops | bytes accessed | tf_op | source)
XLA Modules:
  0.0 231.2 jit_solution(13010490586612044024)
XLA Ops:
  0.6 1.5 pad_bitcast_fusion.1.a_ref
  2.2 1.6 pad_bitcast_fusion.b_ref
  3.7 37.7 %gather_params.1 = (bf16[384,1152]{1,0:T(8,128)(2,1)}, bf16[384,384]{1,0:T(8,128)(2,1)}, f32[8,384]{1,0:T(8,128)}, f32[12,2,192,128]{3,2,1,0:T(8,128)}, bf16[313...) custom-call(f32[160,128]{1,0:T(8,128)} %pad_bitcast_fusion.1.a_ref, f32[304,128]{1,0:T(8,128)} %pad_bitcast_fusion.b_ref, ...), custom_call_target="tpu_custom_call" | custom-call | tf_op jit(solution)/shard_map/gather_params/pallas_call | solution.py:533
  41.5 38.6 %attend.1 = (bf16[4,784,384]{2,1,0:T(8,128)(2,1)}, bf16[16,12,256,256]{3,2,1,0:T(8,128)(2,1)}, bf16[16,384,256]{2,1,0:T(8,128)(2,1)}, bf16[16,384,256]{2,1,0:T(8...) custom-call(bf16[4,784,384]{2,1,0:T(8,128)(2,1)} %bitcast.17, ...), custom_call_target="tpu_custom_call", output_to_operand_aliasing={{8}: (2, {})} | custom-call | tf_op jit(solution)/shard_map/attend/pallas_call | solution.py:772
  80.0 44.8 %mlp.1 = (bf16[3136,384]{1,0:T(8,128)(2,1)}, f32[3136,384]{1,0:T(8,128)}, bf16[3136,384]{1,0:T(8,128)(2,1)}, bf16[32,304,128]{2,1,0:T(8,128)(2,1)}, f32[384,384]{1,0:T(8,128)}, /*index=5*/f32[8,1536]{1,0:T(8,128)}) custom-call(bf16[3136,384]{1,0:T(8,128)(2,1)} %get-tuple-element.47.cot_ref, bf16[3136,384]{1,0:T(8,128)(2,1)} %bitcast.24, ...), custom_call_target="tpu_custom_call" | custom-call | tf_op jit(solution)/shard_map/mlp/pallas_call | solution.py:940
  124.8 0.0 copy-start.1
  124.8 0.0 copy-start.3
  124.9 0.0 copy-start.4
  124.9 61.6 %attend_back.1 = (f32[12,2,192,128]{3,2,1,0:T(8,128)}, f32[384,1152]{1,0:T(8,128)}, f32[8,1152]{1,0:T(8,128)}, bf16[4,208,384]{2,1,0:T(8,128)(2,1)}, f32[304,128...) custom-call(bf16[16,384,256]{2,1,0:T(8,128)(2,1)} %get-tuple-element.43.q_ref, ...), custom_call_target="tpu_custom_call" | custom-call | tf_op jit(solution)/shard_map/attend_back/pallas_call | solution.py:1174
  186.5 0.0 copy-done.1
  186.5 0.0 copy-done.3
  186.5 0.0 copy-done.4
  186.5 1.8 multiply_subtract_fusion
  188.2 7.2 %pack.1.blocks = bf16[32,160,128]{2,1,0:T(8,128)(2,1)} custom-call(bf16[384,384]{1,0:T(8,128)(2,1)} %constant.13.clone.one_fine, bf16[256,128]{1,0:T(8,128)(2,1)} %constant.14.clone.one_coarse, f32[12,2,192,128]{3,2,1,0:T(8,128)} %get-tuple-element.58.g_bias, f32[384,1152]{1,0:T(8,128)} %get-tuple-element.59.g_qkv, f32[8,1152]{1,0:T(8,128)} %get-tuple-element.60.g_vec1, ...), custom_call_target="tpu_custom_call" | custom-call | tf_op jit(solution)/shard_map/pack/pallas_call | solution.py:1313
  195.5 0.0 copy-start.2
  195.5 0.0 copy-start.5
  195.5 0.0 copy-start.6
  195.5 28.3 %sum_grads.1 = (f32[160,128]{1,0:T(8,128)}, bf16[4,784,384]{2,1,0:T(8,128)(2,1)}) custom-call(bf16[32,160,128]{2,1,0:T(8,128)(2,1)} %pack.1.blocks, bf16[4,208,384]{2,1,0:T(8,128)(2,1)} %get-tuple-element.63.last_ref, bf16[4,784,384]{2,1,0:T(8,128)(2,1)} %get-tuple-element.64.dx_ref), custom_call_target="tpu_custom_call", output_to_operand_aliasing={{1}: (2, {})} | custom-call | tf_op jit(solution)/shard_map/sum_grads/pallas_call | solution.py:347
  223.7 0.0 copy-done.2
  223.8 0.0 copy-done.5
  223.8 0.0 copy-done.6
  223.8 1.6 multiply_subtract_fusion.1
  225.4 0.0 copy-start
  225.4 4.4 %bitcast_convert_fusion = f32[1,3136,384]{2,1,0:T(8,128)} fusion(bf16[1,3136,384]{2,1,0:T(8,128)(2,1)} %bitcast.19), kind=kLoop, calls=%fused_computation | loop fusion | flops 1204224 | bytes 7225344 | tf_op jit(solution)/shard_map/convert_element_type | solution.py:1377
  229.7 0.0 copy-done
  229.7 1.4 copy.28
Async XLA Ops:
  124.8 61.6 %copy-start.1 = (f32[36952]{0:T(1024)S(1)}, f32[36952]{0:T(1024)}, u32[]{:S(2)}) copy-start(f32[36952]{0:T(1024)} %param.20) | copy-start | bytes 443428
  124.8 61.6 %copy-start.3 = (f32[36952]{0:T(1024)S(1)}, f32[36952]{0:T(1024)}, u32[]{:S(2)}) copy-start(f32[36952]{0:T(1024)} %param.22) | copy-start | bytes 443428
  124.9 61.6 %copy-start.4 = (f32[36952]{0:T(1024)S(1)}, f32[36952]{0:T(1024)}, u32[]{:S(2)}) copy-start(f32[36952]{0:T(1024)} %param.21) | copy-start | bytes 443428
  195.5 28.3 %copy-start.2 = (f32[18696]{0:T(1024)S(1)}, f32[18696]{0:T(1024)}, u32[]{:S(2)}) copy-start(f32[18696]{0:T(1024)} %param.17) | copy-start | bytes 224356
  195.5 28.3 %copy-start.5 = (f32[18696]{0:T(1024)S(1)}, f32[18696]{0:T(1024)}, u32[]{:S(2)}) copy-start(f32[18696]{0:T(1024)} %param.19) | copy-start | bytes 224356
  195.5 28.3 %copy-start.6 = (f32[18696]{0:T(1024)S(1)}, f32[18696]{0:T(1024)}, u32[]{:S(2)}) copy-start(f32[18696]{0:T(1024)} %param.18) | copy-start | bytes 224356
  225.4 4.4 %copy-start = (bf16[3136,384]{1,0:T(8,128)(2,1)S(1)}, bf16[3136,384]{1,0:T(8,128)(2,1)}, u32[]{:S(2)}) copy-start(bf16[3136,384]{1,0:T(8,128)(2,1)} %get-tuple-element.57) | copy-start | bytes 7225348

commit v6 on v5

--- a/solution.py
+++ b/solution.py
@@ -32,7 +32,7 @@
 F32 = jnp.float32
 BF16 = jnp.bfloat16
 MESH = pl.DeviceIdType.MESH
-VMEM_LIMIT = 56 * 2**20
+VMEM_LIMIT = 60 * 2**20
 
 
 def token_place(gy, gx):
@@ -113,19 +113,31 @@
     def lane(self, device):
         return lax.rem(device * self.length, 128)
 
+    def split(self, share):
+        first = max(16, min(self.rows - 16, round(self.rows * share / 16) * 16))
+        return first, self.rows - first
+
     def padded(self, vector):
         extra = self.rows * 128 - self.length
         return jnp.pad(vector, (0, extra)).reshape(self.rows, 128)
 
 
+GATHER_SHARE = 0.7
+SUM_SHARE = 0.5
 GATHER_STEPS = 12
-SUM_STEPS = 15
+SUM_STEPS = 16
 
 
 def bit_order(n_dp, n_grp):
     dp_bits = [("dp", 2**b) for b in range(n_dp.bit_length() - 1)]
     grp_bits = [("grp", 2**b) for b in reversed(range(n_grp.bit_length() - 1))]
     return dp_bits[1:2] + grp_bits + dp_bits[2:] + dp_bits[:1]
+
+
+def other_order(order):
+    grp_bits = [stage for stage in order if stage[0] == "grp"]
+    dp_bits = [stage for stage in order if stage[0] == "dp"]
+    return dp_bits[:-1] + grp_bits + dp_bits[-1:]
 
 
 def stage_weights(order):
@@ -248,30 +260,30 @@
         return cube_copy(self.order, k, source, target, self.dp, self.grp, *self.sems)
 
     def start(self, k):
-        size = 2**k
-        if k < self.last:
-            other = size - self.mine(k)
-
-            def fill(j, carry):
-                self.outgoing[size + j] = self.total[other + j].astype(BF16)
-                return carry
-
-            lax.fori_loop(0, size, fill, 0)
         self.copy(k).start()
 
     def finish(self, k):
         size, mine = 2**k, self.mine(k)
         self.copy(k).wait()
 
-        def add(j, carry):
+        def added(j):
             if k == self.last:
                 held = self.blocks[mine + j].astype(F32)
             else:
                 held = self.total[mine + j]
-            self.total[j] = held + self.arrived[size + j].astype(F32)
+            return held + self.arrived[size + j].astype(F32)
+
+        keep = size // 2 if k else 1
+        kept = self.mine(k - 1) if k else 0
+
+        def add(j, carry):
+            value = added(kept + j)
+            if k:
+                self.outgoing[keep + j] = added(keep - kept + j).astype(BF16)
+            self.total[kept + j] = value
             return carry
 
-        lax.fori_loop(0, size, add, 0)
+        lax.fori_loop(0, keep, add, 0)
 
     @staticmethod
     def scratch(devices, rows, stages):
@@ -304,69 +316,6 @@
     return copies
 
 
-def sum_kernel(
-    part,
-    order,
-    blocks,
-    last_ref,
-    dx_ref,
-    grad_ref,
-    dx_out,
-    total,
-    outgoing,
-    arrived,
-    send,
-    recv,
-    x_sem,
-    x_send,
-    x_recv,
-):
-    dp, grp = lax.axis_index("dp"), lax.axis_index("grp")
-    greet(cube_partners(order, dp, grp) + [window_partner(dp, grp, 3)])
-    cube = CubeSum(order, blocks, total, outgoing, arrived, (send, recv))
-    first = dx_ref.shape[1] - last_ref.shape[1]
-    exchange = chunk_copies(
-        last_ref, dx_out, first, last_ref.shape[1], dp, grp, x_sem, x_send, x_recv, first
-    )
-    for k in reversed(range(len(order))):
-        cube.start(k)
-        if k == len(order) - 1:
-            for c in exchange:
-                c.start()
-        cube.finish(k)
-    device = dp * lax.axis_size("grp") + grp
-    grad_ref[...] = shift_lanes(total[0], part.lane(device), False)
-    for c in exchange:
-        c.wait()
-
-
-def sum_grads(part, order, blocks, last, dx):
-    stages = len(order)
-    hbm = pl.BlockSpec(memory_space=pl.ANY)
-    vm = pl.BlockSpec(memory_space=pltpu.VMEM)
-    grad, dx = pl.pallas_call(
-        functools.partial(sum_kernel, part, order),
-        out_shape=[
-            jax.ShapeDtypeStruct((part.rows, 128), F32),
-            jax.ShapeDtypeStruct(dx.shape, dx.dtype),
-        ],
-        in_specs=[vm, hbm, hbm],
-        out_specs=[vm, hbm],
-        input_output_aliases={2: 1},
-        scratch_shapes=CubeSum.scratch(part.devices, part.rows, stages)
-        + [
-            pltpu.SemaphoreType.DMA,
-            pltpu.SemaphoreType.DMA((3,)),
-            pltpu.SemaphoreType.DMA((3,)),
-        ],
-        compiler_params=pltpu.CompilerParams(
-            collective_id=1, has_side_effects=True, vmem_limit_bytes=VMEM_LIMIT
-        ),
-        name="sum_grads",
-    )(blocks, last, dx)
-    return grad.reshape(-1)[: part.length], dx
-
-
 def place_list(order, n_dp, n_grp):
     return [place_of(order, d // n_grp, d % n_grp) for d in range(n_dp * n_grp)]
 
@@ -375,10 +324,11 @@
 TABLE_AT = D * 3 * D + D * D
 
 
-def unflatten(part, places, blocks, flat):
-    for device, place in enumerate(places):
+def unflatten(part, chains, flat):
+    for device in range(part.devices):
         at = part.start(device)
-        block = blocks[place].astype(F32)
+        pieces = [blocks[places[device]].astype(F32) for places, blocks in chains]
+        block = jnp.concatenate(pieces, axis=0) if len(pieces) > 1 else pieces[0]
         first = block[0:1] + flat[at : at + 1, :] if device else block[0:1]
         flat[at : at + part.rows, :] = block
         flat[at : at + 1, :] = first
@@ -411,10 +361,10 @@
 
 
 def prepare(
-    part, places, blocks, one_fine, one_coarse, mask_ref,
+    part, chains, one_fine, one_coarse, mask_ref,
     wqkv, wproj, vecs, bias, flat, tab_fine, tab_coarse, shifted, turned,
 ):
-    unflatten(part, places, blocks, flat)
+    unflatten(part, chains, flat)
     take_matrix(flat, 0, wqkv)
     take_matrix(flat, 3456, wproj)
     row, lane = divmod(ATTN_VECTORS[0], 128)
@@ -456,7 +406,7 @@
     part_a,
     part_b,
     order,
-    places,
+    chain_places,
     a_ref,
     b_ref,
     one_fine,
@@ -469,7 +419,8 @@
     bias,
     x_ref,
     blocks_b,
-    blocks_a,
+    blocks_a1,
+    blocks_a2,
     own,
     flat,
     tab_fine,
@@ -477,8 +428,10 @@
     shifted,
     turned,
     own_sem,
-    send_a,
-    recv_a,
+    send_a1,
+    recv_a1,
+    send_a2,
+    recv_a2,
     send_b,
     recv_b,
     x_sem,
@@ -491,18 +444,29 @@
     own[...] = shift_lanes(b_ref[...], part_b.lane(device), True).astype(BF16)
     copy = pltpu.make_async_copy(own, blocks_b.at[place], own_sem)
     copy.start()
-    blocks_a[place] = shift_lanes(a_ref[...], part_a.lane(device), True).astype(BF16)
+    mine = shift_lanes(a_ref[...], part_a.lane(device), True)
+    orders = (order, other_order(order))
+    chains = ((blocks_a1, (send_a1, recv_a1)), (blocks_a2, (send_a2, recv_a2)))
+    at = 0
+    for chain_order, (blocks, _) in zip(orders, chains):
+        blocks[place_of(chain_order, dp, grp)] = mine[at : at + blocks.shape[1]].astype(BF16)
+        at += blocks.shape[1]
     vecs[...] = jnp.zeros_like(vecs)
     greet(cube_partners(order, dp, grp) + [window_partner(dp, grp, 3)])
     copy.wait()
     exchange = exchange_copies(tok_ref, x_ref, dp, grp, x_sem, x_send, x_recv)
     first = [
-        gather_copy(order, k, blocks_a, dp, grp, (send_a, recv_a)) for k in range(len(order))
+        [
+            gather_copy(chain_order, k, blocks, dp, grp, sems)
+            for chain_order, (blocks, sems) in zip(orders, chains)
+        ]
+        for k in range(len(order))
     ]
     early = early_stages(order)
     second = [gather_copy(order, k, blocks_b, dp, grp, (send_b, recv_b)) for k in range(early)]
     for k, stage in enumerate(first):
-        stage.start()
+        for c in stage:
+            c.start()
         if k == 0:
             second[0].start()
             for c in exchange:
@@ -511,9 +475,10 @@
             second[k - early].wait()
             if k - early + 1 < early:
                 second[k - early + 1].start()
-        stage.wait()
+        for c in stage:
+            c.wait()
     prepare(
-        part_a, places, blocks_a, one_fine, one_coarse, mask_ref,
+        part_a, list(zip(chain_places, (blocks_a1, blocks_a2))), one_fine, one_coarse, mask_ref,
         wqkv, wproj, vecs, bias, flat, tab_fine, tab_coarse, shifted, turned,
     )
     for k in range(len(order) - early, early):
@@ -524,14 +489,15 @@
         c.wait()
 
 
-def gather_params(part_a, part_b, order, places, master_a, master_b, tok):
+def gather_params(part_a, part_b, order, chain_places, master_a, master_b, tok):
     stages = len(order)
+    rows = part_a.split(GATHER_SHARE)
     early = early_stages(order)
     fine, coarse, mask = bias_tables()
     vm = pl.BlockSpec(memory_space=pltpu.VMEM)
     hbm = pl.BlockSpec(memory_space=pl.ANY)
     return pl.pallas_call(
-        functools.partial(gather_kernel, part_a, part_b, order, places),
+        functools.partial(gather_kernel, part_a, part_b, order, chain_places),
         out_shape=[
             jax.ShapeDtypeStruct((D, 3 * D), BF16),
             jax.ShapeDtypeStruct((D, D), BF16),
@@ -543,7 +509,8 @@
         in_specs=[vm] * 5 + [hbm],
         out_specs=[vm] * 4 + [hbm] * 2,
         scratch_shapes=[
-            pltpu.VMEM((part_a.devices, part_a.rows, 128), BF16),
+            pltpu.VMEM((part_a.devices, rows[0], 128), BF16),
+            pltpu.VMEM((part_a.devices, rows[1], 128), BF16),
             pltpu.VMEM((part_b.rows, 128), BF16),
             pltpu.VMEM((part_a.buffer, 128), F32),
             pltpu.VMEM((16, 384), F32),
@@ -551,6 +518,8 @@
             pltpu.VMEM((4, 14 * 16, 128), F32),
             pltpu.VMEM((2, 128, 256), F32),
             pltpu.SemaphoreType.DMA,
+            pltpu.SemaphoreType.DMA((stages,)),
+            pltpu.SemaphoreType.DMA((stages,)),
             pltpu.SemaphoreType.DMA((stages,)),
             pltpu.SemaphoreType.DMA((stages,)),
             pltpu.SemaphoreType.DMA((early,)),
@@ -827,7 +796,7 @@
 
 
 def unpack_mlp(part, places, blocks, flat, w1, w2, vecs):
-    unflatten(part, places, blocks, flat)
+    unflatten(part, [(places, blocks)], flat)
     take_matrix(flat, 0, w1)
     take_matrix(flat, 4608, w2)
     for j in range(12):
@@ -849,7 +818,7 @@
             at = 9228 + 3 * v + j
             flat[at : at + 1, :] = g_vec[1 + v : 2 + v, j * 128 : (j + 1) * 128]
     flat[9237:, :] = jnp.zeros((flat.shape[0] - 9237, 128), F32)
-    to_blocks(part, places, flat, out)
+    to_blocks(part, [(places, out)], flat)
 
 
 def mlp_kernel(
@@ -973,8 +942,10 @@
 
 
 def attend_back_kernel(
+    part_a,
     part,
     order,
+    chain_places,
     q_ref,
     k_ref,
     v_ref,
@@ -991,13 +962,21 @@
     vecs,
     blocks,
     out_src,
+    g_proj,
+    g_vec2,
+    one_fine,
+    one_coarse,
+    grad_a_ref,
+    grad_ref,
+    out_ref,
+    dx_ref,
     g_bias,
     g_qkv,
     g_vec,
-    dx_last,
-    grad_ref,
-    out_ref,
-    dx_ref,
+    flat,
+    table,
+    shifted,
+    line,
     d_query_t,
     d_key_value_t,
     d_qkv,
@@ -1022,6 +1001,10 @@
     dx_sem2,
     dx_send2,
     dx_recv2,
+    dx_sem3,
+    dx_send3,
+    dx_recv3,
+    *chain_scratch,
 ):
     i = pl.program_id(0)
     steps = pl.num_programs(0)
@@ -1033,6 +1016,7 @@
         (dx_sem0, dx_send0, dx_recv0),
         (dx_sem1, dx_send1, dx_recv1),
         (dx_sem2, dx_send2, dx_recv2),
+        (dx_sem3, dx_send3, dx_recv3),
     )
     loads = [
         pltpu.make_async_copy(x_hbm, x_buf, load_sems.at[0]),
@@ -1040,7 +1024,8 @@
     ]
 
     def chunk(c):
-        return chunk_copies(d_in, dx_ref, CHUNK * c, CHUNK, dp, grp, *dx_sems[c], 0)
+        size = LAST if c == 3 else CHUNK
+        return chunk_copies(d_in, dx_ref, CHUNK * c, size, dp, grp, *dx_sems[c], 0)
 
     @pl.when(i == 0)
     def _():
@@ -1059,6 +1044,10 @@
             if k < stages - 1:
                 cube.finish(k + 1)
             cube.start(k)
+
+    @pl.when(i == min(SUM_STEPS, steps - 1))
+    def _():
+        cube.finish(0)
 
     @pl.when(i == 0)
     def _():
@@ -1133,13 +1122,12 @@
         result = d_res_buf[:, at, :].reshape(4 * LAST, D) + norm_back(d_normed, xhat, scale, gain)
         result = result.astype(BF16).reshape(4, LAST, D)
         d_in[:, at, :] = result
-        dx_last[...] = result
         g_qkv[...] += dot(normed.T, grads)
         g_vec[0:1, :] += jnp.sum(grads.astype(F32), axis=0, keepdims=True)
         g_vec[1:2, :D] += jnp.sum(d_normed * xhat, axis=0, keepdims=True)
         g_vec[2:3, :D] += jnp.sum(d_normed, axis=0, keepdims=True)
 
-    for c in range(3):
+    for c in range(4):
 
         @pl.when(i == 4 * c + 3)
         def _(c=c):
@@ -1148,37 +1136,55 @@
 
     @pl.when(i == steps - 1)
     def _():
-        cube.finish(0)
         device = dp * lax.axis_size("grp") + grp
         grad_ref[...] = shift_lanes(total[0], part.lane(device), False)
+        half = len(chain_scratch) // 2
+        sums = (chain_scratch[0], chain_scratch[half])
+        pack(
+            part_a, list(zip(chain_places, sums)), one_fine, one_coarse,
+            g_bias, g_qkv, g_vec, g_proj, g_vec2, flat, table, shifted, line,
+        )
+        cubes = []
+        for c, chain_order in enumerate((order, other_order(order))):
+            own, *buffers, sent, received = chain_scratch[c * half : (c + 1) * half]
+            cubes.append(CubeSum(chain_order, own, *buffers, (sent, received)))
+        for k in reversed(range(stages)):
+            for chain in cubes:
+                chain.start(k)
+            for chain in cubes:
+                chain.finish(k)
+        grad_a = jnp.concatenate([chain.total[0] for chain in cubes], axis=0)
+        grad_a_ref[...] = shift_lanes(grad_a, part_a.lane(device), False)
         for c in exchange:
             c.wait()
-        for c in range(3):
+        for c in range(4):
             for copy in chunk(c):
                 copy.wait()
 
 
 def attend_back(
-    part, order, saved, d_mixed, probs, inverse, x, d_res, wqkv, vecs, blocks, out
+    part_a, part, order, chain_places, saved, d_mixed, probs, inverse, x, d_res, wqkv, vecs, blocks,
+    out, g_proj, g_vec2,
 ):
     images = probs.shape[0]
     tokens = out.shape[0]
     rows = tokens // 4
     stages = len(order)
     _, query_tab, keys_back, query_back = gather_tables(images)
+    fine, coarse, _ = bias_tables()
     vm = pl.BlockSpec(memory_space=pltpu.VMEM)
     hbm = pl.BlockSpec(memory_space=pl.ANY)
     image = lambda *shape: pl.BlockSpec((1, *shape), lambda i: (i, 0, 0))
-    table = image(256, 256)
     by_window = lambda array: array.reshape(4, rows, -1)
-    outs = pl.pallas_call(
-        functools.partial(attend_back_kernel, part, order),
+    chain_scratch = []
+    for count in part_a.split(SUM_SHARE):
+        chain_scratch.append(pltpu.VMEM((part.devices, count, 128), BF16))
+        chain_scratch += CubeSum.scratch(part.devices, count, stages)
+    grad_a, grad_b, output, dx = pl.pallas_call(
+        functools.partial(attend_back_kernel, part_a, part, order, chain_places),
         grid=(images,),
         out_shape=[
-            jax.ShapeDtypeStruct((HEADS, 2, KEYS, 128), F32),
-            jax.ShapeDtypeStruct((D, 3 * D), F32),
-            jax.ShapeDtypeStruct((8, 3 * D), F32),
-            jax.ShapeDtypeStruct((4, LAST, D), BF16),
+            jax.ShapeDtypeStruct((part_a.rows, 128), F32),
             jax.ShapeDtypeStruct((part.rows, 128), F32),
             jax.ShapeDtypeStruct((tokens, D), BF16),
             jax.ShapeDtypeStruct((4, rows, D), BF16),
@@ -1192,18 +1198,22 @@
             pl.BlockSpec((1, HEADS, 256, 256), lambda i: (i, 0, 0, 0)),
             image(16, 256),
         ]
-        + [table] * 3
-        + [hbm, hbm, vm, vm, vm, hbm],
+        + [image(256, 256)] * 3
+        + [hbm, hbm, vm, vm, vm, hbm, vm, vm, vm, vm],
         out_specs=[
-            pl.BlockSpec((HEADS, 2, KEYS, 128), lambda i: (0, 0, 0, 0)),
-            pl.BlockSpec((D, 3 * D), lambda i: (0, 0)),
-            pl.BlockSpec((8, 3 * D), lambda i: (0, 0)),
-            pl.BlockSpec((4, LAST, D), lambda i: (0, 0, 0)),
+            pl.BlockSpec((part_a.rows, 128), lambda i: (0, 0)),
             pl.BlockSpec((part.rows, 128), lambda i: (0, 0)),
             hbm,
             hbm,
         ],
         scratch_shapes=[
+            pltpu.VMEM((HEADS, 2, KEYS, 128), F32),
+            pltpu.VMEM((D, 3 * D), F32),
+            pltpu.VMEM((8, 3 * D), F32),
+            pltpu.VMEM((part_a.buffer, 128), F32),
+            pltpu.VMEM((16, 512), F32),
+            pltpu.VMEM((4, 14 * 16, 128), F32),
+            pltpu.VMEM((8, 512), F32),
             pltpu.VMEM((D, 256), BF16),
             pltpu.VMEM((2 * D, 256), BF16),
             pltpu.VMEM((4, rows, 3 * D), BF16),
@@ -1218,7 +1228,8 @@
             pltpu.SemaphoreType.DMA((3,)),
             pltpu.SemaphoreType.DMA((3,)),
         ]
-        * 4,
+        * 5
+        + chain_scratch,
         compiler_params=pltpu.CompilerParams(
             collective_id=3, has_side_effects=True, vmem_limit_bytes=VMEM_LIMIT
         ),
@@ -1237,34 +1248,30 @@
         vecs,
         blocks,
         out,
-    )
-    grad = outs[4].reshape(-1)[: part.length]
-    return (*outs[:4], grad, *outs[5:])
-
-
-def to_blocks(part, places, flat, out):
-    for device, place in enumerate(places):
+        g_proj,
+        g_vec2,
+        jnp.asarray(fine),
+        jnp.asarray(coarse),
+    )
+    grad_a = grad_a.reshape(-1)[: part_a.length]
+    grad_b = grad_b.reshape(-1)[: part.length]
+    return grad_a, grad_b, output, dx
+
+
+def to_blocks(part, chains, flat):
+    for device in range(part.devices):
         at = part.start(device)
-        out[place] = flat[at : at + part.rows, :].astype(BF16)
-
-
-def pack_kernel(
-    part,
-    places,
-    one_fine,
-    one_coarse,
-    g_bias,
-    g_qkv,
-    g_vec1,
-    g_proj,
-    g_vec2,
-    out,
-    flat,
-    table,
-    shifted,
-    line,
+        for places, out in chains:
+            out[places[device]] = flat[at : at + out.shape[1], :].astype(BF16)
+            at += out.shape[1]
+
+
+def pack(
+    part, chains, one_fine, one_coarse,
+    g_bias, g_qkv, g_vec1, g_proj, g_vec2, flat, table, shifted, line,
 ):
-    flat[...] = jnp.zeros_like(flat)
+    row, lane = divmod(ATTN_VECTORS[0], 128)
+    flat[4608:, :] = jnp.zeros((flat.shape[0] - 4608, 128), F32)
     put_matrix(flat, 0, g_qkv)
     put_matrix(flat, 3456, g_proj)
     vectors = [
@@ -1276,7 +1283,6 @@
     ]
     pieces = [v[:, j * 128 : (j + 1) * 128] for v in vectors for j in range(3)]
     pieces += [jnp.zeros((1, 128), F32)]
-    row, lane = divmod(ATTN_VECTORS[0], 128)
     flat[row : row + 16, :] += shift_lanes(jnp.concatenate(pieces, axis=0), lane, True)
     for h in range(HEADS):
         table[...] = jnp.zeros_like(table)
@@ -1304,26 +1310,7 @@
         line[0:1, lane : lane + length] = (g_fine, g_coarse)[t][h : h + 1, :length]
         for c in range(count):
             flat[row + c : row + c + 1, :] += line[0:1, c * 128 : (c + 1) * 128]
-    to_blocks(part, places, flat, out)
-
-
-def pack(part, places, g_bias, g_qkv, g_vec1, g_proj, g_vec2):
-    fine, coarse, _ = bias_tables()
-    vm = pl.BlockSpec(memory_space=pltpu.VMEM)
-    return pl.pallas_call(
-        functools.partial(pack_kernel, part, places),
-        out_shape=jax.ShapeDtypeStruct((part.devices, part.rows, 128), BF16),
-        in_specs=[vm] * 7,
-        out_specs=vm,
-        scratch_shapes=[
-            pltpu.VMEM((part.buffer, 128), F32),
-            pltpu.VMEM((16, 512), F32),
-            pltpu.VMEM((4, 14 * 16, 128), F32),
-            pltpu.VMEM((8, 512), F32),
-        ],
-        compiler_params=pltpu.CompilerParams(vmem_limit_bytes=VMEM_LIMIT),
-        name="pack",
-    )(jnp.asarray(fine), jnp.asarray(coarse), g_bias, g_qkv, g_vec1, g_proj, g_vec2)
+    to_blocks(part, chains, flat)
 
 
 def adamw(master, first, second, grads):
@@ -1342,36 +1329,24 @@
 ):
     n_dp, n_grp = lax.axis_size("dp"), lax.axis_size("grp")
     order = bit_order(n_dp, n_grp)
-    places = place_list(order, n_dp, n_grp)
+    chain_places = [place_list(o, n_dp, n_grp) for o in (order, other_order(order))]
     part_a = Part(n_dp * n_grp, attn_master.shape[0])
     part_b = Part(n_dp * n_grp, mlp_master.shape[0])
     images = tokens.shape[1] // 4 // SEQ
     wqkv, wproj, vecs_a, bias, x, blocks_b = gather_params(
-        part_a, part_b, order, places, attn_master, mlp_master, tokens[0]
+        part_a, part_b, order, chain_places, attn_master, mlp_master, tokens[0]
     )
     mixed, probs, *saved, inverse, cot, blocks_b = attend(
         order, x, cotangent[0], blocks_b, wqkv, vecs_a, bias, images
     )
     mixed = mixed.reshape(-1, D)
     out, d_res, d_mixed, sums_b, g_proj, g_vec2 = mlp(
-        part_b, places, cot, mixed, x, wproj, vecs_a, blocks_b
-    )
-    g_bias, g_qkv, g_vec1, dx_last, grad_b, output, dx = attend_back(
-        part_b,
-        order,
-        saved,
-        d_mixed,
-        probs,
-        inverse,
-        x,
-        d_res,
-        wqkv,
-        vecs_a,
-        sums_b,
-        out,
-    )
-    sums_a = pack(part_a, places, g_bias, g_qkv, g_vec1, g_proj, g_vec2)
-    grad_a, dx = sum_grads(part_a, order, sums_a, dx_last, dx)
+        part_b, chain_places[0], cot, mixed, x, wproj, vecs_a, blocks_b
+    )
+    grad_a, grad_b, output, dx = attend_back(
+        part_a, part_b, order, chain_places, saved, d_mixed, probs, inverse, x, d_res, wqkv,
+        vecs_a, sums_b, out, g_proj, g_vec2,
+    )
     attn_new = adamw(attn_master, attn_first, attn_second, grad_a)
     mlp_new = adamw(mlp_master, mlp_first, mlp_second, grad_b)
     input_grad = dx.reshape(-1, D).astype(F32)

time: 231 us -> 222 us (0.961)
  Pallas kernels: 218 us -> 209 us
    pallas_call x4 -> x2, Pallas kernels: 135 us -> 126 us  [the longest x1 87.8 us: attend_back(): pl.pallas_call(functools.partial(attend_back_kernel, part_a, part, order,...]
where the time goes in v6:
time: 222 us
  Pallas kernels  209 us (94%)
  other arithmetic  7.7 us (3%)
  local copies, waits for them, and re-layouts  4.58 us (2%)
    pallas_call x1, Pallas kernels, attend_back(): pl.pallas_call(functools.partial(attend_back_kernel, part_a, part, order,...  87.8 us
    pallas_call x1, Pallas kernels, mlp(): pl.pallas_call(functools.partial(mlp_kernel, part, places), grid=(7,), ou...  44.7 us
    pallas_call x1, Pallas kernels, attend(): pl.pallas_call(functools.partial(attend_kernel, rows, order), grid=(image...  38.6 us
    pallas_call x1, Pallas kernels, gather_params(): pl.pallas_call(functools.partial(gather_kernel, part_a, part_b, order, ch...  37.8 us

profile of v6, /device:TPU:0, one launch (start us, length us, event | category | flops | bytes accessed | tf_op | source)
XLA Modules:
  0.0 222.0 jit_solution(11743144003863417776)
XLA Ops:
  0.6 1.5 pad_bitcast_fusion.1.a_ref
  2.2 1.6 pad_bitcast_fusion.b_ref
  3.7 37.8 %gather_params.1 = (bf16[384,1152]{1,0:T(8,128)(2,1)}, bf16[384,384]{1,0:T(8,128)(2,1)}, f32[8,384]{1,0:T(8,128)}, f32[12,2,192,128]{3,2,1,0:T(8,128)}, bf16[313...) custom-call(f32[160,128]{1,0:T(8,128)} %pad_bitcast_fusion.1.a_ref, f32[304,128]{1,0:T(8,128)} %pad_bitcast_fusion.b_ref, ...), custom_call_target="tpu_custom_call" | custom-call | tf_op jit(solution)/shard_map/gather_params/pallas_call | solution.py:499
  41.5 38.6 %attend.1 = (bf16[4,784,384]{2,1,0:T(8,128)(2,1)}, bf16[16,12,256,256]{3,2,1,0:T(8,128)(2,1)}, bf16[16,384,256]{2,1,0:T(8,128)(2,1)}, bf16[16,384,256]{2,1,0:T(8...) custom-call(bf16[4,784,384]{2,1,0:T(8,128)(2,1)} %bitcast.17, ...), custom_call_target="tpu_custom_call", output_to_operand_aliasing={{8}: (2, {})} | custom-call | tf_op jit(solution)/shard_map/attend/pallas_call | solution.py:741
  80.1 44.7 %mlp.1 = (bf16[3136,384]{1,0:T(8,128)(2,1)}, f32[3136,384]{1,0:T(8,128)}, bf16[3136,384]{1,0:T(8,128)(2,1)}, bf16[32,304,128]{2,1,0:T(8,128)(2,1)}, f32[384,384]{1,0:T(8,128)}, /*index=5*/f32[8,1536]{1,0:T(8,128)}) custom-call(bf16[3136,384]{1,0:T(8,128)(2,1)} %get-tuple-element.42.cot_ref, bf16[3136,384]{1,0:T(8,128)(2,1)} %bitcast.24, ...), custom_call_target="tpu_custom_call" | custom-call | tf_op jit(solution)/shard_map/mlp/pallas_call | solution.py:909
  124.9 0.0 copy-start.2
  124.9 0.0 copy-start.5
  124.9 0.0 copy-start.6
  124.9 0.0 copy-start.1
  124.9 0.0 copy-start.3
  124.9 0.0 copy-start.4
  125.0 87.8 %attend_back.1 = (f32[160,128]{1,0:T(8,128)}, f32[304,128]{1,0:T(8,128)}, bf16[3136,384]{1,0:T(8,128)(2,1)}, bf16[4,784,384]{2,1,0:T(8,128)(2,1)}) custom-call(bf16[16,384,256]{2,1,0:T(8,128)(2,1)} %get-tuple-element.38.q_ref, bf16[16,384,256]{2,1,0:T(8,128)(2,1)} %get-tuple-element.39.k_ref, bf16[16,256,384]{2,1,0:T(8,128)(2,1)} %get-tuple-element.40.v_ref, ...), custom_call_target="tpu_custom_call" | custom-call | tf_op jit(solution)/shard_map/attend_back/pallas_call | solution.py:1183
  212.8 0.0 copy-done.2
  212.8 0.0 copy-done.5
  212.8 0.0 copy-done.6
  212.8 1.6 multiply_subtract_fusion.1
  214.4 0.0 copy-done.1
  214.5 0.0 copy-done.3
  214.5 0.0 copy-done.4
  214.5 1.7 multiply_subtract_fusion
  216.2 0.0 copy-start
  216.2 4.4 %bitcast_convert_fusion = f32[1,3136,384]{2,1,0:T(8,128)} fusion(bf16[1,3136,384]{2,1,0:T(8,128)(2,1)} %bitcast.20), kind=kLoop, calls=%fused_computation | loop fusion | flops 1204224 | bytes 7225344 | tf_op jit(solution)/shard_map/convert_element_type | solution.py:1352
  220.6 0.0 copy-done
  220.6 1.4 copy.26
Async XLA Ops:
  124.9 87.9 %copy-start.2 = (f32[18696]{0:T(1024)S(1)}, f32[18696]{0:T(1024)}, u32[]{:S(2)}) copy-start(f32[18696]{0:T(1024)} %param.17) | copy-start | bytes 224356
  124.9 87.9 %copy-start.5 = (f32[18696]{0:T(1024)S(1)}, f32[18696]{0:T(1024)}, u32[]{:S(2)}) copy-start(f32[18696]{0:T(1024)} %param.19) | copy-start | bytes 224356
  124.9 87.9 %copy-start.6 = (f32[18696]{0:T(1024)S(1)}, f32[18696]{0:T(1024)}, u32[]{:S(2)}) copy-start(f32[18696]{0:T(1024)} %param.18) | copy-start | bytes 224356
  124.9 89.5 %copy-start.1 = (f32[36952]{0:T(1024)S(1)}, f32[36952]{0:T(1024)}, u32[]{:S(2)}) copy-start(f32[36952]{0:T(1024)} %param.20) | copy-start | bytes 443428
  124.9 89.5 %copy-start.3 = (f32[36952]{0:T(1024)S(1)}, f32[36952]{0:T(1024)}, u32[]{:S(2)}) copy-start(f32[36952]{0:T(1024)} %param.22) | copy-start | bytes 443428
  124.9 89.5 %copy-start.4 = (f32[36952]{0:T(1024)S(1)}, f32[36952]{0:T(1024)}, u32[]{:S(2)}) copy-start(f32[36952]{0:T(1024)} %param.21) | copy-start | bytes 443428
  216.2 4.4 %copy-start = (bf16[3136,384]{1,0:T(8,128)(2,1)S(1)}, bf16[3136,384]{1,0:T(8,128)(2,1)}, u32[]{:S(2)}) copy-start(bf16[3136,384]{1,0:T(8,128)(2,1)} %get-tuple-element.54) | copy-start | bytes 7225348

commit v7 on v6

--- a/solution.py
+++ b/solution.py
@@ -1,4 +1,5 @@
 import functools
+import itertools
 
 import jax
 import jax.numpy as jnp
@@ -32,7 +33,7 @@
 F32 = jnp.float32
 BF16 = jnp.bfloat16
 MESH = pl.DeviceIdType.MESH
-VMEM_LIMIT = 60 * 2**20
+VMEM_LIMIT = 58 * 2**20
 
 
 def token_place(gy, gx):
@@ -124,8 +125,8 @@
 
 GATHER_SHARE = 0.7
 SUM_SHARE = 0.5
-GATHER_STEPS = 12
-SUM_STEPS = 16
+GATHER_STEPS = 7
+SUM_STEPS = 12
 
 
 def bit_order(n_dp, n_grp):
@@ -151,7 +152,7 @@
 def starts_of(weights, steps):
     done, starts = 0.0, []
     for weight in weights:
-        starts.append(min(int(np.ceil(steps * done / sum(weights))), steps - 1))
+        starts.append(int(steps * done / sum(weights)))
         done += weight
     return starts
 
@@ -604,6 +605,11 @@
     return slice(h // 4 * 128, h // 4 * 128 + 128)
 
 
+def interleave(first, second):
+    for _ in itertools.zip_longest(first, second):
+        pass
+
+
 def attend_kernel(
     rows,
     order,
@@ -677,50 +683,57 @@
             v = dot(normed[w % 2], wqkv[:, 2 * D :]) + vecs[3:4, :]
             qkv[w, :, 2 * D :] = v.astype(BF16)
 
-    q_ext = dot(query_tab[0], image_rows(qkv, i, slice(0, D)))
-    kv_ext = dot(keys_tab[0], image_rows(qkv, i, slice(D, 3 * D)))
-    q_t = q_ext.T.astype(BF16)
-    k_ext = kv_ext[:, :D].astype(BF16)
-    v_t = kv_ext[:, D:].T.astype(BF16)
-    query_out[0] = q_t
-    key_out[0] = kv_ext[:, :D].T.astype(BF16)
-    value_out[0] = kv_ext[:, D:].astype(BF16)
-    inverse[0, HEADS:16, :] = jnp.zeros((16 - HEADS, 256), F32)
-
-    def scores_of(h):
-        heads = jnp.concatenate([only_head(q_t, h), only_head(q_t, h + 1)], axis=1)
-        return dot(k_ext[:, tile_of(h)], heads)
-
-    def softmax(scores, h):
-        halves, inverses = [], []
-        for half in range(2):
-            s = half_of(scores, half) + bias[h, half]
-            e = jnp.exp(s - jnp.max(s, axis=0, keepdims=True))
-            inverses.append(1.0 / jnp.sum(e, axis=0, keepdims=True))
-            halves.append(e)
-        e = spread(halves)
-        inv = jnp.concatenate(inverses, axis=1)
-        probs[0, h] = e
-        inverse[0, h : h + 1, :] = inv
-        return e, inv
-
-    def mix(h, e, inv):
-        own = slice(h * HDIM, (h + 1) * HDIM)
-        mixed_out[0, own, :] = (dot(v_t[own, :], e) * inv).astype(BF16)
-
-    ahead = scores_of(0)
-    waiting = []
-    for h in range(0, HEADS, 2):
-        now = ahead
-        if h + 2 < HEADS:
-            ahead = scores_of(h + 2)
-        for c in range(2):
-            waiting.append((h + c, *softmax(now[:, c * 256 : (c + 1) * 256], h + c)))
-        while len(waiting) > 1:
-            mix(*waiting.pop(0))
-    for last in waiting:
-        mix(*last)
-    put_image_rows(mixed, i, slice(0, D), dot_t(query_back[0], mixed_out[0]))
+    def image(b):
+        at = 2 * i + b
+        q_ext = dot(query_tab[b], image_rows(qkv, at, slice(0, D)))
+        kv_ext = dot(keys_tab[b], image_rows(qkv, at, slice(D, 3 * D)))
+        q_t = q_ext.T.astype(BF16)
+        k_ext = kv_ext[:, :D].astype(BF16)
+        v_t = kv_ext[:, D:].T.astype(BF16)
+        query_out[b] = q_t
+        key_out[b] = kv_ext[:, :D].T.astype(BF16)
+        value_out[b] = kv_ext[:, D:].astype(BF16)
+        inverse[b, HEADS:16, :] = jnp.zeros((16 - HEADS, 256), F32)
+
+        def scores_of(h):
+            heads = jnp.concatenate([only_head(q_t, h), only_head(q_t, h + 1)], axis=1)
+            return dot(k_ext[:, tile_of(h)], heads)
+
+        def softmax(scores, h):
+            halves, inverses = [], []
+            for half in range(2):
+                s = half_of(scores, half) + bias[h, half]
+                e = jnp.exp(s - jnp.max(s, axis=0, keepdims=True))
+                inverses.append(1.0 / jnp.sum(e, axis=0, keepdims=True))
+                halves.append(e)
+            e = spread(halves)
+            inv = jnp.concatenate(inverses, axis=1)
+            probs[b, h] = e
+            inverse[b, h : h + 1, :] = inv
+            return e, inv
+
+        def mix(h, e, inv):
+            own = slice(h * HDIM, (h + 1) * HDIM)
+            mixed_out[b, own, :] = (dot(v_t[own, :], e) * inv).astype(BF16)
+
+        ahead = scores_of(0)
+        yield
+        waiting = []
+        for h in range(0, HEADS, 2):
+            now = ahead
+            if h + 2 < HEADS:
+                ahead = scores_of(h + 2)
+            for c in range(2):
+                waiting.append((h + c, *softmax(now[:, c * 256 : (c + 1) * 256], h + c)))
+            while len(waiting) > 1:
+                mix(*waiting.pop(0))
+            yield
+        for last in waiting:
+            mix(*last)
+        yield
+        put_image_rows(mixed, at, slice(0, D), dot_t(query_back[b], mixed_out[b]))
+
+    interleave(image(0), image(1))
 
     @pl.when(i == steps - 1)
     def _():
@@ -736,11 +749,11 @@
     keys_tab, query_tab, _, query_back = gather_tables(images)
     vm = pl.BlockSpec(memory_space=pltpu.VMEM)
     hbm = pl.BlockSpec(memory_space=pl.ANY)
-    image = lambda *shape: pl.BlockSpec((1, *shape), lambda i: (i, 0, 0))
+    image = lambda *shape: pl.BlockSpec((2, *shape), lambda i: (i, 0, 0))
     table = image(256, 256)
     return pl.pallas_call(
         functools.partial(attend_kernel, rows, order),
-        grid=(images,),
+        grid=(images // 2,),
         out_shape=[
             jax.ShapeDtypeStruct((4, rows, D), BF16),
             jax.ShapeDtypeStruct((images, HEADS, 256, 256), BF16),
@@ -755,7 +768,7 @@
         in_specs=[vm, hbm, hbm] + [vm] * 3 + [table] * 3,
         out_specs=[
             pl.BlockSpec((4, rows, D), lambda i: (0, 0, 0)),
-            pl.BlockSpec((1, HEADS, 256, 256), lambda i: (i, 0, 0, 0)),
+            pl.BlockSpec((2, HEADS, 256, 256), lambda i: (i, 0, 0, 0)),
             image(D, 256),
             image(D, 256),
             image(256, D),
@@ -807,7 +820,7 @@
             vecs[1 + v : 2 + v, j * 128 : (j + 1) * 128] = flat[at : at + 1, :]
 
 
-def pack_mlp(part, places, g_w1, g_w2t, g_vec, flat, out):
+def pack_mlp(part, chains, g_w1, g_w2t, g_vec, flat):
     put_matrix(flat, 0, g_w1)
     for j in range(3):
         flat[pl.ds(4608 + j, FF, stride=3), :] = g_w2t[j * 128 : (j + 1) * 128, :].T
@@ -818,12 +831,12 @@
             at = 9228 + 3 * v + j
             flat[at : at + 1, :] = g_vec[1 + v : 2 + v, j * 128 : (j + 1) * 128]
     flat[9237:, :] = jnp.zeros((flat.shape[0] - 9237, 128), F32)
-    to_blocks(part, [(places, out)], flat)
+    to_blocks(part, chains, flat)
 
 
 def mlp_kernel(
     part,
-    places,
+    chain_places,
     cot_ref,
     mixed_ref,
     x_ref,
@@ -833,7 +846,8 @@
     out_ref,
     d_res_ref,
     d_mixed_ref,
-    sums,
+    sums1,
+    sums2,
     g_proj,
     g_vec,
     w1,
@@ -847,7 +861,7 @@
 
     @pl.when(i == 0)
     def _():
-        unpack_mlp(part, places, blocks, flat, w1, w2, vecs)
+        unpack_mlp(part, chain_places[0], blocks, flat, w1, w2, vecs)
         g_w1[...] = jnp.zeros_like(g_w1)
         g_w2t[...] = jnp.zeros_like(g_w2t)
         g_proj[...] = jnp.zeros_like(g_proj)
@@ -897,28 +911,30 @@
 
     @pl.when(i == pl.num_programs(0) - 1)
     def _():
-        pack_mlp(part, places, g_w1, g_w2t, g_vec, flat, sums)
-
-
-def mlp(part, places, cot, mixed, x, wproj, vecs_a, blocks):
+        pack_mlp(part, list(zip(chain_places, (sums1, sums2))), g_w1, g_w2t, g_vec, flat)
+
+
+def mlp(part, chain_places, cot, mixed, x, wproj, vecs_a, blocks):
+    sums = [(part.devices, rows, 128) for rows in part.split(SUM_SHARE)]
     tokens = x.shape[0]
     chunk = tokens // 7
     vm = pl.BlockSpec(memory_space=pltpu.VMEM)
     tile = pl.BlockSpec((chunk, D), lambda i: (i, 0))
     fixed = lambda *shape: pl.BlockSpec(shape, lambda i: (0,) * len(shape))
     return pl.pallas_call(
-        functools.partial(mlp_kernel, part, places),
+        functools.partial(mlp_kernel, part, chain_places),
         grid=(7,),
         out_shape=[
             jax.ShapeDtypeStruct((tokens, D), BF16),
             jax.ShapeDtypeStruct((tokens, D), F32),
             jax.ShapeDtypeStruct((tokens, D), BF16),
-            jax.ShapeDtypeStruct((part.devices, part.rows, 128), BF16),
+            jax.ShapeDtypeStruct(sums[0], BF16),
+            jax.ShapeDtypeStruct(sums[1], BF16),
             jax.ShapeDtypeStruct((D, D), F32),
             jax.ShapeDtypeStruct((8, FF), F32),
         ],
         in_specs=[tile] * 3 + [vm] * 3,
-        out_specs=[tile] * 3 + [fixed(part.devices, part.rows, 128), fixed(D, D), fixed(8, FF)],
+        out_specs=[tile] * 3 + [fixed(*sums[0]), fixed(*sums[1]), fixed(D, D), fixed(8, FF)],
         scratch_shapes=[
             pltpu.VMEM((D, FF), BF16),
             pltpu.VMEM((FF, D), BF16),
@@ -932,8 +948,12 @@
     )(cot, mixed, x, wproj, vecs_a, blocks)
 
 
-CHUNK = 192
-LAST = 208
+def row_chunks(rows, steps):
+    after = [steps * 3 // 8, steps * 5 // 8, steps * 7 // 8, steps]
+    ends = [rows * done // steps // 16 * 16 for done in after]
+    return [
+        (done - 1, first, end - first) for done, first, end in zip(after, [0] + ends[:-1], ends)
+    ]
 
 
 def split_float(values):
@@ -946,6 +966,7 @@
     part,
     order,
     chain_places,
+    images,
     q_ref,
     k_ref,
     v_ref,
@@ -960,7 +981,8 @@
     d_res_hbm,
     wqkv,
     vecs,
-    blocks,
+    blocks1,
+    blocks2,
     out_src,
     g_proj,
     g_vec2,
@@ -984,11 +1006,6 @@
     x_buf,
     d_res_buf,
     load_sems,
-    total,
-    outgoing,
-    arrived,
-    send,
-    recv,
     out_sem,
     out_send,
     out_recv,
@@ -1010,7 +1027,23 @@
     steps = pl.num_programs(0)
     stages = len(order)
     dp, grp = lax.axis_index("dp"), lax.axis_index("grp")
-    cube = CubeSum(order, blocks, total, outgoing, arrived, (send, recv))
+    orders = (order, other_order(order))
+
+    sums_a, arrived_a, sems_a = chain_scratch[:2], chain_scratch[2:4], chain_scratch[4:8]
+    cubes_a, cubes_b = [], []
+    for c, blocks in enumerate((blocks1, blocks2)):
+        total, outgoing, arrived, *sems = chain_scratch[8 + 5 * c : 13 + 5 * c]
+        cubes_b.append(CubeSum(orders[c], blocks, total, outgoing, arrived, sems))
+        rows = pl.ds(0, arrived_a[c].shape[1])
+        local = (total.at[:, rows], outgoing.at[:, rows])
+        cubes_a.append(
+            CubeSum(orders[c], sums_a[c], *local, arrived_a[c], sems_a[2 * c : 2 * c + 2])
+        )
+    def put_result(p, cubes, ref):
+        device = dp * lax.axis_size("grp") + grp
+        result = jnp.concatenate([cube.total[0] for cube in cubes], axis=0)
+        ref[...] = shift_lanes(result, p.lane(device), False)
+
     exchange = exchange_copies(out_src, out_ref, dp, grp, out_sem, out_send, out_recv)
     dx_sems = (
         (dx_sem0, dx_send0, dx_recv0),
@@ -1023,9 +1056,10 @@
         pltpu.make_async_copy(d_res_hbm, d_res_buf, load_sems.at[1]),
     ]
 
+    chunks = row_chunks(d_in.shape[1], images)
+
     def chunk(c):
-        size = LAST if c == 3 else CHUNK
-        return chunk_copies(d_in, dx_ref, CHUNK * c, size, dp, grp, *dx_sems[c], 0)
+        return chunk_copies(d_in, dx_ref, *chunks[c][1:], dp, grp, *dx_sems[c], 0)
 
     @pl.when(i == 0)
     def _():
@@ -1041,120 +1075,114 @@
 
         @pl.when(i == start)
         def _(k=k):
-            if k < stages - 1:
-                cube.finish(k + 1)
-            cube.start(k)
-
-    @pl.when(i == min(SUM_STEPS, steps - 1))
+            for cube in cubes_b:
+                if k < stages - 1:
+                    cube.finish(k + 1)
+                cube.start(k)
+
+    @pl.when(i == steps - 1)
     def _():
-        cube.finish(0)
+        for cube in cubes_b:
+            cube.finish(0)
+        put_result(part, cubes_b, grad_ref)
 
     @pl.when(i == 0)
     def _():
         for c in exchange:
             c.start()
 
-    dm_t = dot(query_tab[0], image_rows(d_mixed, i, slice(0, D))).T
-    spread_heads = lambda ref: jnp.concatenate(
-        [jnp.broadcast_to(ref[h : h + 1], (HDIM, 256)) for h in range(HEADS)], axis=0
-    )
-    dm_t = (dm_t * spread_heads(inverse[0])).astype(BF16)
-    products = dm_t.astype(F32) * mixed_ref[0].astype(F32)
-    q_t, k_t, v_ext = q_ref[0], k_ref[0], v_ref[0]
-
-    def d_probs_of(h):
-        heads = jnp.concatenate([only_head(dm_t, h), only_head(dm_t, h + 1)], axis=1)
-        return dot(v_ext[:, tile_of(h)], heads)
-
-    def softmax_back(d_probs, h):
-        e = probs[0, h]
-        own = slice(h * HDIM, (h + 1) * HDIM)
-        sums = jnp.sum(products[own], axis=0, keepdims=True)
-        halves = []
-        for half in range(2):
-            lanes = slice(128 * half, 128 * half + 128)
-            e32 = e[:, lanes].astype(F32)[56 * half : 56 * half + KEYS]
-            ds = e32 * (half_of(d_probs, half) - sums[:, lanes])
-            g_bias[h, half] += ds
-            halves.append(ds)
-        return spread(halves)
-
-    def gather_back(h, ds):
-        own = slice(h * HDIM, (h + 1) * HDIM)
-        d_query_t[own, :] = (dot(k_t[own, :], ds) * HDIM ** (-0.5)).astype(BF16)
-        d_key_value_t[own, :] = dot_t(q_t[own, :], ds).astype(BF16)
-        d_key_value_t[D + h * HDIM : D + (h + 1) * HDIM, :] = dot_t(
-            dm_t[own, :], probs[0, h]
-        ).astype(BF16)
-
-    ahead = d_probs_of(0)
-    waiting = []
-    for h in range(0, HEADS, 2):
-        now = ahead
-        if h + 2 < HEADS:
-            ahead = d_probs_of(h + 2)
-        for c in range(2):
-            waiting.append((h + c, softmax_back(now[:, c * 256 : (c + 1) * 256], h + c)))
-        while len(waiting) > 1:
-            gather_back(*waiting.pop(0))
-    for last in waiting:
-        gather_back(*last)
-    put_image_rows(d_qkv, i, slice(0, D), dot_t(query_back[0], d_query_t[...]))
-    put_image_rows(d_qkv, i, slice(D, 3 * D), dot_t(keys_back[0], d_key_value_t[...]))
+    def image(b):
+        at = i
+        dm_t = dot(query_tab[b], image_rows(d_mixed, at, slice(0, D))).T
+        scales = [jnp.broadcast_to(inverse[b, h : h + 1, :], (HDIM, 256)) for h in range(HEADS)]
+        dm_t = (dm_t * jnp.concatenate(scales, axis=0)).astype(BF16)
+        products = dm_t.astype(F32) * mixed_ref[b].astype(F32)
+        q_t, k_t, v_ext = q_ref[b], k_ref[b], v_ref[b]
+
+        def d_probs_of(h):
+            heads = jnp.concatenate([only_head(dm_t, h), only_head(dm_t, h + 1)], axis=1)
+            return dot(v_ext[:, tile_of(h)], heads)
+
+        def softmax_back(d_probs, h):
+            e = probs[b, h]
+            own = slice(h * HDIM, (h + 1) * HDIM)
+            sums = jnp.sum(products[own], axis=0, keepdims=True)
+            halves = []
+            for half in range(2):
+                lanes = slice(128 * half, 128 * half + 128)
+                e32 = e[:, lanes].astype(F32)[56 * half : 56 * half + KEYS]
+                ds = e32 * (half_of(d_probs, half) - sums[:, lanes])
+                g_bias[h, half] += ds
+                halves.append(ds)
+            return spread(halves)
+
+        def gather_back(h, ds):
+            own = slice(h * HDIM, (h + 1) * HDIM)
+            values = slice(D + h * HDIM, D + (h + 1) * HDIM)
+            d_query_t[b, own, :] = (dot(k_t[own, :], ds) * HDIM ** (-0.5)).astype(BF16)
+            d_key_value_t[b, own, :] = dot_t(q_t[own, :], ds).astype(BF16)
+            d_key_value_t[b, values, :] = dot_t(dm_t[own, :], probs[b, h]).astype(BF16)
+
+        ahead = d_probs_of(0)
+        yield
+        waiting = []
+        for h in range(0, HEADS, 2):
+            now = ahead
+            if h + 2 < HEADS:
+                ahead = d_probs_of(h + 2)
+            for c in range(2):
+                waiting.append((h + c, softmax_back(now[:, c * 256 : (c + 1) * 256], h + c)))
+            while len(waiting) > 1:
+                gather_back(*waiting.pop(0))
+            yield
+        for last in waiting:
+            gather_back(*last)
+        yield
+        put_image_rows(d_qkv, at, slice(0, D), dot_t(query_back[b], d_query_t[b]))
+        put_image_rows(d_qkv, at, slice(D, 3 * D), dot_t(keys_back[b], d_key_value_t[b]))
+
+    for _ in image(0):
+        pass
 
     @pl.when(i == 3)
     def _():
         for c in loads:
             c.wait()
 
-    @pl.when(lax.rem(i, 4) == 3)
-    def _():
-        c = i // 4
-        at = pl.ds(pl.multiple_of(c * CHUNK, 16), LAST)
-        xhat, scale = norm_parts(x_buf[:, at, :].reshape(4 * LAST, D).astype(F32))
+    def finish_rows(first, size):
+        at = slice(first, first + size)
+        xhat, scale = norm_parts(x_buf[:, at, :].reshape(4 * size, D).astype(F32))
         gain = vecs[0:1, :]
         normed = (xhat * gain + vecs[1:2, :]).astype(BF16)
-        row = lax.rem(lax.broadcasted_iota(jnp.int32, (4 * LAST, 1), 0), LAST)
-        counts = row < jnp.where(i == steps - 1, LAST, CHUNK)
-        grads = d_qkv[:, at, :].reshape(4 * LAST, 3 * D)
-        grads = jnp.where(counts, grads, 0)
+        grads = d_qkv[:, at, :].reshape(4 * size, 3 * D)
         d_normed = dot_t(grads, wqkv[...])
-        result = d_res_buf[:, at, :].reshape(4 * LAST, D) + norm_back(d_normed, xhat, scale, gain)
-        result = result.astype(BF16).reshape(4, LAST, D)
-        d_in[:, at, :] = result
+        result = d_res_buf[:, at, :].reshape(4 * size, D) + norm_back(d_normed, xhat, scale, gain)
+        d_in[:, at, :] = result.astype(BF16).reshape(4, size, D)
         g_qkv[...] += dot(normed.T, grads)
         g_vec[0:1, :] += jnp.sum(grads.astype(F32), axis=0, keepdims=True)
         g_vec[1:2, :D] += jnp.sum(d_normed * xhat, axis=0, keepdims=True)
         g_vec[2:3, :D] += jnp.sum(d_normed, axis=0, keepdims=True)
 
-    for c in range(4):
-
-        @pl.when(i == 4 * c + 3)
-        def _(c=c):
+    for c, (step, first, size) in enumerate(chunks):
+
+        @pl.when(i == step)
+        def _(c=c, first=first, size=size):
+            finish_rows(first, size)
             for copy in chunk(c):
                 copy.start()
 
     @pl.when(i == steps - 1)
     def _():
-        device = dp * lax.axis_size("grp") + grp
-        grad_ref[...] = shift_lanes(total[0], part.lane(device), False)
-        half = len(chain_scratch) // 2
-        sums = (chain_scratch[0], chain_scratch[half])
         pack(
-            part_a, list(zip(chain_places, sums)), one_fine, one_coarse,
+            part_a, list(zip(chain_places, sums_a)), one_fine, one_coarse,
             g_bias, g_qkv, g_vec, g_proj, g_vec2, flat, table, shifted, line,
         )
-        cubes = []
-        for c, chain_order in enumerate((order, other_order(order))):
-            own, *buffers, sent, received = chain_scratch[c * half : (c + 1) * half]
-            cubes.append(CubeSum(chain_order, own, *buffers, (sent, received)))
         for k in reversed(range(stages)):
-            for chain in cubes:
-                chain.start(k)
-            for chain in cubes:
-                chain.finish(k)
-        grad_a = jnp.concatenate([chain.total[0] for chain in cubes], axis=0)
-        grad_a_ref[...] = shift_lanes(grad_a, part_a.lane(device), False)
+            for cube in cubes_a:
+                cube.start(k)
+            for cube in cubes_a:
+                cube.finish(k)
+        put_result(part_a, cubes_a, grad_a_ref)
         for c in exchange:
             c.wait()
         for c in range(4):
@@ -1176,12 +1204,15 @@
     hbm = pl.BlockSpec(memory_space=pl.ANY)
     image = lambda *shape: pl.BlockSpec((1, *shape), lambda i: (i, 0, 0))
     by_window = lambda array: array.reshape(4, rows, -1)
-    chain_scratch = []
-    for count in part_a.split(SUM_SHARE):
-        chain_scratch.append(pltpu.VMEM((part.devices, count, 128), BF16))
+    chain_scratch = [
+        pltpu.VMEM((part.devices, count, 128), BF16) for count in part_a.split(SUM_SHARE)
+    ]
+    chain_scratch += chain_scratch
+    chain_scratch += [pltpu.SemaphoreType.DMA((stages,))] * 4
+    for count in part.split(SUM_SHARE):
         chain_scratch += CubeSum.scratch(part.devices, count, stages)
     grad_a, grad_b, output, dx = pl.pallas_call(
-        functools.partial(attend_back_kernel, part_a, part, order, chain_places),
+        functools.partial(attend_back_kernel, part_a, part, order, chain_places, images),
         grid=(images,),
         out_shape=[
             jax.ShapeDtypeStruct((part_a.rows, 128), F32),
@@ -1199,7 +1230,7 @@
             image(16, 256),
         ]
         + [image(256, 256)] * 3
-        + [hbm, hbm, vm, vm, vm, hbm, vm, vm, vm, vm],
+        + [hbm, hbm, vm, vm, vm, vm, hbm, vm, vm, vm, vm],
         out_specs=[
             pl.BlockSpec((part_a.rows, 128), lambda i: (0, 0)),
             pl.BlockSpec((part.rows, 128), lambda i: (0, 0)),
@@ -1214,15 +1245,14 @@
             pltpu.VMEM((16, 512), F32),
             pltpu.VMEM((4, 14 * 16, 128), F32),
             pltpu.VMEM((8, 512), F32),
-            pltpu.VMEM((D, 256), BF16),
-            pltpu.VMEM((2 * D, 256), BF16),
+            pltpu.VMEM((1, D, 256), BF16),
+            pltpu.VMEM((1, 2 * D, 256), BF16),
             pltpu.VMEM((4, rows, 3 * D), BF16),
             pltpu.VMEM((4, rows, D), BF16),
             pltpu.VMEM((4, rows, D), BF16),
             pltpu.VMEM((4, rows, D), F32),
             pltpu.SemaphoreType.DMA((2,)),
         ]
-        + CubeSum.scratch(part.devices, part.rows, stages)
         + [
             pltpu.SemaphoreType.DMA,
             pltpu.SemaphoreType.DMA((3,)),
@@ -1246,7 +1276,7 @@
         by_window(d_res),
         wqkv,
         vecs,
-        blocks,
+        *blocks,
         out,
         g_proj,
         g_vec2,
@@ -1340,8 +1370,8 @@
         order, x, cotangent[0], blocks_b, wqkv, vecs_a, bias, images
     )
     mixed = mixed.reshape(-1, D)
-    out, d_res, d_mixed, sums_b, g_proj, g_vec2 = mlp(
-        part_b, chain_places[0], cot, mixed, x, wproj, vecs_a, blocks_b
+    out, d_res, d_mixed, *sums_b, g_proj, g_vec2 = mlp(
+        part_b, chain_places, cot, mixed, x, wproj, vecs_a, blocks_b
     )
     grad_a, grad_b, output, dx = attend_back(
         part_a, part_b, order, chain_places, saved, d_mixed, probs, inverse, x, d_res, wqkv,

time: 222 us -> 213 us (0.959)
  Pallas kernels: 209 us -> 200 us
    pallas_call x1, Pallas kernels: 87.8 us -> 82.2 us  [attend_back(): pl.pallas_call(functools.partial(attend_back_kernel, part_a, part, order,...]
    pallas_call x1, Pallas kernels: 38.6 us -> 35.3 us  [attend(): pl.pallas_call(functools.partial(attend_kernel, rows, order), grid=(image...]
where the time goes in v7:
time: 213 us
  Pallas kernels  200 us (94%)
  other arithmetic  7.7 us (4%)
  local copies, waits for them, and re-layouts  4.58 us (2%)
    pallas_call x1, Pallas kernels, attend_back(): pl.pallas_call(functools.partial(attend_back_kernel, part_a, part, order,...  82.2 us
    pallas_call x1, Pallas kernels, mlp(): pl.pallas_call(functools.partial(mlp_kernel, part, chain_places), grid=(7...  44.8 us
    pallas_call x1, Pallas kernels, gather_params(): pl.pallas_call(functools.partial(gather_kernel, part_a, part_b, order, ch...  37.8 us
    pallas_call x1, Pallas kernels, attend(): pl.pallas_call(functools.partial(attend_kernel, rows, order), grid=(image...  35.3 us
    convert_element_type x1, other arithmetic, body(): input_grad = dx.reshape(-1, D).astype(F32)  4.36 us

profile of v7, /device:TPU:0, one launch (start us, length us, event | category | flops | bytes accessed | tf_op | source)
XLA Modules:
  0.0 213.1 jit_solution(8845186839584662067)
XLA Ops:
  0.6 1.5 pad_bitcast_fusion.1.a_ref
  2.2 1.6 pad_bitcast_fusion.b_ref
  3.7 37.8 %gather_params.1 = (bf16[384,1152]{1,0:T(8,128)(2,1)}, bf16[384,384]{1,0:T(8,128)(2,1)}, f32[8,384]{1,0:T(8,128)}, f32[12,2,192,128]{3,2,1,0:T(8,128)}, bf16[313...) custom-call(f32[160,128]{1,0:T(8,128)} %pad_bitcast_fusion.1.a_ref, f32[304,128]{1,0:T(8,128)} %pad_bitcast_fusion.b_ref, ...), custom_call_target="tpu_custom_call" | custom-call | tf_op jit(solution)/shard_map/gather_params/pallas_call | solution.py:500
  41.6 35.3 %attend.1 = (bf16[4,784,384]{2,1,0:T(8,128)(2,1)}, bf16[16,12,256,256]{3,2,1,0:T(8,128)(2,1)}, bf16[16,384,256]{2,1,0:T(8,128)(2,1)}, bf16[16,384,256]{2,1,0:T(8...) custom-call(bf16[4,784,384]{2,1,0:T(8,128)(2,1)} %bitcast.17, ...), custom_call_target="tpu_custom_call", output_to_operand_aliasing={{8}: (2, {})} | custom-call | tf_op jit(solution)/shard_map/attend/pallas_call | solution.py:754
  76.9 44.8 %mlp.1 = (bf16[3136,384]{1,0:T(8,128)(2,1)}, f32[3136,384]{1,0:T(8,128)}, bf16[3136,384]{1,0:T(8,128)(2,1)}, bf16[32,160,128]{2,1,0:T(8,128)(2,1)}, bf16[32,144,...) custom-call(bf16[3136,384]{1,0:T(8,128)(2,1)} %get-tuple-element.43.cot_ref, bf16[3136,384]{1,0:T(8,128)(2,1)} %bitcast.24, ...), custom_call_target="tpu_custom_call" | custom-call | tf_op jit(solution)/shard_map/mlp/pallas_call | solution.py:924
  121.7 0.0 copy-start.2
  121.7 0.0 copy-start.5
  121.7 0.0 copy-start.6
  121.7 0.0 copy-start.1
  121.7 0.0 copy-start.3
  121.7 0.0 copy-start.4
  121.7 82.2 %attend_back.1 = (f32[160,128]{1,0:T(8,128)}, f32[304,128]{1,0:T(8,128)}, bf16[3136,384]{1,0:T(8,128)(2,1)}, bf16[4,784,384]{2,1,0:T(8,128)(2,1)}) custom-call(bf16[16,384,256]{2,1,0:T(8,128)(2,1)} %get-tuple-element.39.q_ref, bf16[16,384,256]{2,1,0:T(8,128)(2,1)} %get-tuple-element.40.k_ref, bf16[16,256,384]{2,1,0:T(8,128)(2,1)} %get-tuple-element.41.v_ref, ...), custom_call_target="tpu_custom_call" | custom-call | tf_op jit(solution)/shard_map/attend_back/pallas_call | solution.py:1214
  203.9 0.0 copy-done.2
  203.9 0.0 copy-done.5
  203.9 0.0 copy-done.6
  203.9 1.6 multiply_subtract_fusion.1
  205.5 0.0 copy-done.1
  205.5 0.0 copy-done.3
  205.5 0.0 copy-done.4
  205.5 1.7 multiply_subtract_fusion
  207.3 0.0 copy-start
  207.3 4.4 %bitcast_convert_fusion = f32[1,3136,384]{2,1,0:T(8,128)} fusion(bf16[1,3136,384]{2,1,0:T(8,128)(2,1)} %bitcast.20), kind=kLoop, calls=%fused_computation | loop fusion | flops 1204224 | bytes 7225344 | tf_op jit(solution)/shard_map/convert_element_type | solution.py:1382
  211.7 0.0 copy-done
  211.7 1.4 copy.26
Async XLA Ops:
  121.7 82.3 %copy-start.2 = (f32[18696]{0:T(1024)S(1)}, f32[18696]{0:T(1024)}, u32[]{:S(2)}) copy-start(f32[18696]{0:T(1024)} %param.17) | copy-start | bytes 224356
  121.7 82.3 %copy-start.5 = (f32[18696]{0:T(1024)S(1)}, f32[18696]{0:T(1024)}, u32[]{:S(2)}) copy-start(f32[18696]{0:T(1024)} %param.19) | copy-start | bytes 224356
  121.7 82.2 %copy-start.6 = (f32[18696]{0:T(1024)S(1)}, f32[18696]{0:T(1024)}, u32[]{:S(2)}) copy-start(f32[18696]{0:T(1024)} %param.18) | copy-start | bytes 224356
  121.7 83.9 %copy-start.1 = (f32[36952]{0:T(1024)S(1)}, f32[36952]{0:T(1024)}, u32[]{:S(2)}) copy-start(f32[36952]{0:T(1024)} %param.20) | copy-start | bytes 443428
  121.7 83.8 %copy-start.3 = (f32[36952]{0:T(1024)S(1)}, f32[36952]{0:T(1024)}, u32[]{:S(2)}) copy-start(f32[36952]{0:T(1024)} %param.22) | copy-start | bytes 443428
  121.7 83.8 %copy-start.4 = (f32[36952]{0:T(1024)S(1)}, f32[36952]{0:T(1024)}, u32[]{:S(2)}) copy-start(f32[36952]{0:T(1024)} %param.21) | copy-start | bytes 443428
  207.3 4.4 %copy-start = (bf16[3136,384]{1,0:T(8,128)(2,1)S(1)}, bf16[3136,384]{1,0:T(8,128)(2,1)}, u32[]{:S(2)}) copy-start(bf16[3136,384]{1,0:T(8,128)(2,1)} %get-tuple-element.56) | copy-start | bytes 7225348

commit v8 on v7

--- a/solution.py
+++ b/solution.py
@@ -1168,8 +1168,9 @@
         @pl.when(i == step)
         def _(c=c, first=first, size=size):
             finish_rows(first, size)
-            for copy in chunk(c):
-                copy.start()
+            if c < 3:
+                for copy in chunk(c):
+                    copy.start()
 
     @pl.when(i == steps - 1)
     def _():
@@ -1180,6 +1181,9 @@
         for k in reversed(range(stages)):
             for cube in cubes_a:
                 cube.start(k)
+            if k == stages - 1:
+                for copy in chunk(3):
+                    copy.start()
             for cube in cubes_a:
                 cube.finish(k)
         put_result(part_a, cubes_a, grad_a_ref)

time: 213 us -> 213 us (level)
  no operation moved by 1% of the time
where the time goes in v8:
time: 213 us; the launch traced here: 212 us
  Pallas kernels  199 us (93%)
  other arithmetic  7.7 us (4%)
  local copies, waits for them, and re-layouts  4.58 us (2%)
    pallas_call x1, Pallas kernels, attend_back(): pl.pallas_call(functools.partial(attend_back_kernel, part_a, part, order,...  81.5 us
    pallas_call x1, Pallas kernels, mlp(): pl.pallas_call(functools.partial(mlp_kernel, part, chain_places), grid=(7...  44.8 us
    pallas_call x1, Pallas kernels, gather_params(): pl.pallas_call(functools.partial(gather_kernel, part_a, part_b, order, ch...  37.8 us
    pallas_call x1, Pallas kernels, attend(): pl.pallas_call(functools.partial(attend_kernel, rows, order), grid=(image...  35.3 us
    convert_element_type x1, other arithmetic, body(): input_grad = dx.reshape(-1, D).astype(F32)  4.36 us

profile of v8, /device:TPU:0, one launch (start us, length us, event | category | flops | bytes accessed | tf_op | source)
XLA Modules:
  0.0 212.4 jit_solution(15487658446322421179)
XLA Ops:
  0.6 1.5 pad_bitcast_fusion.1.a_ref
  2.2 1.6 pad_bitcast_fusion.b_ref
  3.7 37.8 %gather_params.1 = (bf16[384,1152]{1,0:T(8,128)(2,1)}, bf16[384,384]{1,0:T(8,128)(2,1)}, f32[8,384]{1,0:T(8,128)}, f32[12,2,192,128]{3,2,1,0:T(8,128)}, bf16[313...) custom-call(f32[160,128]{1,0:T(8,128)} %pad_bitcast_fusion.1.a_ref, f32[304,128]{1,0:T(8,128)} %pad_bitcast_fusion.b_ref, ...), custom_call_target="tpu_custom_call" | custom-call | tf_op jit(solution)/shard_map/gather_params/pallas_call | solution.py:500
  41.6 35.3 %attend.1 = (bf16[4,784,384]{2,1,0:T(8,128)(2,1)}, bf16[16,12,256,256]{3,2,1,0:T(8,128)(2,1)}, bf16[16,384,256]{2,1,0:T(8,128)(2,1)}, bf16[16,384,256]{2,1,0:T(8...) custom-call(bf16[4,784,384]{2,1,0:T(8,128)(2,1)} %bitcast.17, ...), custom_call_target="tpu_custom_call", output_to_operand_aliasing={{8}: (2, {})} | custom-call | tf_op jit(solution)/shard_map/attend/pallas_call | solution.py:754
  76.9 44.8 %mlp.1 = (bf16[3136,384]{1,0:T(8,128)(2,1)}, f32[3136,384]{1,0:T(8,128)}, bf16[3136,384]{1,0:T(8,128)(2,1)}, bf16[32,160,128]{2,1,0:T(8,128)(2,1)}, bf16[32,144,...) custom-call(bf16[3136,384]{1,0:T(8,128)(2,1)} %get-tuple-element.43.cot_ref, bf16[3136,384]{1,0:T(8,128)(2,1)} %bitcast.24, ...), custom_call_target="tpu_custom_call" | custom-call | tf_op jit(solution)/shard_map/mlp/pallas_call | solution.py:924
  121.7 0.0 copy-start.2
  121.7 0.0 copy-start.5
  121.7 0.0 copy-start.6
  121.7 0.0 copy-start.1
  121.7 0.0 copy-start.3
  121.7 0.0 copy-start.4
  121.7 81.5 %attend_back.1 = (f32[160,128]{1,0:T(8,128)}, f32[304,128]{1,0:T(8,128)}, bf16[3136,384]{1,0:T(8,128)(2,1)}, bf16[4,784,384]{2,1,0:T(8,128)(2,1)}) custom-call(bf16[16,384,256]{2,1,0:T(8,128)(2,1)} %get-tuple-element.39.q_ref, bf16[16,384,256]{2,1,0:T(8,128)(2,1)} %get-tuple-element.40.k_ref, bf16[16,256,384]{2,1,0:T(8,128)(2,1)} %get-tuple-element.41.v_ref, ...), custom_call_target="tpu_custom_call" | custom-call | tf_op jit(solution)/shard_map/attend_back/pallas_call | solution.py:1218
  203.3 0.0 copy-done.2
  203.3 0.0 copy-done.5
  203.3 0.0 copy-done.6
  203.3 1.6 multiply_subtract_fusion.1
  204.9 0.0 copy-done.1
  204.9 0.0 copy-done.3
  204.9 0.0 copy-done.4
  204.9 1.7 multiply_subtract_fusion
  206.7 0.0 copy-start
  206.7 4.4 %bitcast_convert_fusion = f32[1,3136,384]{2,1,0:T(8,128)} fusion(bf16[1,3136,384]{2,1,0:T(8,128)(2,1)} %bitcast.20), kind=kLoop, calls=%fused_computation | loop fusion | flops 1204224 | bytes 7225344 | tf_op jit(solution)/shard_map/convert_element_type | solution.py:1386
  211.0 0.0 copy-done
  211.0 1.4 copy.26
Async XLA Ops:
  121.7 81.6 %copy-start.2 = (f32[18696]{0:T(1024)S(1)}, f32[18696]{0:T(1024)}, u32[]{:S(2)}) copy-start(f32[18696]{0:T(1024)} %param.17) | copy-start | bytes 224356
  121.7 81.6 %copy-start.5 = (f32[18696]{0:T(1024)S(1)}, f32[18696]{0:T(1024)}, u32[]{:S(2)}) copy-start(f32[18696]{0:T(1024)} %param.19) | copy-start | bytes 224356
  121.7 81.6 %copy-start.6 = (f32[18696]{0:T(1024)S(1)}, f32[18696]{0:T(1024)}, u32[]{:S(2)}) copy-start(f32[18696]{0:T(1024)} %param.18) | copy-start | bytes 224356
  121.7 83.2 %copy-start.1 = (f32[36952]{0:T(1024)S(1)}, f32[36952]{0:T(1024)}, u32[]{:S(2)}) copy-start(f32[36952]{0:T(1024)} %param.20) | copy-start | bytes 443428
  121.7 83.2 %copy-start.3 = (f32[36952]{0:T(1024)S(1)}, f32[36952]{0:T(1024)}, u32[]{:S(2)}) copy-start(f32[36952]{0:T(1024)} %param.22) | copy-start | bytes 443428
  121.7 83.2 %copy-start.4 = (f32[36952]{0:T(1024)S(1)}, f32[36952]{0:T(1024)}, u32[]{:S(2)}) copy-start(f32[36952]{0:T(1024)} %param.21) | copy-start | bytes 443428
  206.7 4.4 %copy-start = (bf16[3136,384]{1,0:T(8,128)(2,1)S(1)}, bf16[3136,384]{1,0:T(8,128)(2,1)}, u32[]{:S(2)}) copy-start(bf16[3136,384]{1,0:T(8,128)(2,1)} %get-tuple-element.56) | copy-start | bytes 7225348
